TPU v7x, 32 devices: a whole 2x2x4 slice. The times are simulated.
32 devices in a mesh: dp: 4 (over z), fsdp: 8 (over y, x, core).
Axes of the slice: x: 2, y: 2, z: 4, core: 2. Of those that a mesh axis runs over, the one named last changes fastest.
Arguments:
- features: bfloat16 [256, 64, 2048], P(('dp', 'fsdp')), may hold values from -6 to 6
- crop_ids: int32 [256, 64], P(('dp', 'fsdp')), may hold values from -1 to 15, as said below
- labels: int32 [256, 64], P(('dp', 'fsdp')), may hold values from 0 to 18
- w_reduce: bfloat16 [2048, 512], P(None, 'fsdp'), may hold values from -0.125 to 0.125
- gain_reduce: float32 [512], replicated, may hold values from 0.5 to 1.5
- bias_reduce: float32 [512], replicated, may hold values from -1 to 1
- w_dilated: bfloat16 [3, 3, 512, 512], P(None, None, None, 'fsdp'), may hold values from -0.09375 to 0.09375
- gain_dilated: float32 [512], replicated, may hold values from 0.5 to 1.5
- bias_dilated: float32 [512], replicated, may hold values from -1 to 1
- w_expand: bfloat16 [512, 2048], P(None, 'fsdp'), may hold values from -0.25 to 0.25
- gain_expand: float32 [2048], replicated, may hold values from 0.5 to 1.5
- bias_expand: float32 [2048], replicated, may hold values from -1 to 1
- w_point: bfloat16 [2048, 256], P(None, 'fsdp'), may hold values from -0.125 to 0.125
- gain_point: float32 [256], replicated, may hold values from 0.5 to 1.5
- bias_point: float32 [256], replicated, may hold values from -1 to 1
- w_rate: bfloat16 [3, 3, 2048, 256], P(None, None, None, 'fsdp'), may hold values from -0.046875 to 0.046875
- gain_rate: float32 [256], replicated, may hold values from 0.5 to 1.5
- bias_rate: float32 [256], replicated, may hold values from -1 to 1
- w_rate_double: bfloat16 [3, 3, 2048, 256], P(None, None, None, 'fsdp'), may hold values from -0.046875 to 0.046875
- gain_rate_double: float32 [256], replicated, may hold values from 0.5 to 1.5
- bias_rate_double: float32 [256], replicated, may hold values from -1 to 1
- w_rate_triple: bfloat16 [3, 3, 2048, 256], P(None, None, None, 'fsdp'), may hold values from -0.046875 to 0.046875
- gain_rate_triple: float32 [256], replicated, may hold values from 0.5 to 1.5
- bias_rate_triple: float32 [256], replicated, may hold values from -1 to 1
- w_pool: bfloat16 [2048, 256], P(None, 'fsdp'), may hold values from -0.125 to 0.125
- w_merge: bfloat16 [1280, 256], P(None, 'fsdp'), may hold values from -0.15625 to 0.15625
- gain_merge: float32 [256], replicated, may hold values from 0.5 to 1.5
- bias_merge: float32 [256], replicated, may hold values from -1 to 1
- w_classes: bfloat16 [256, 19], P('fsdp'), may hold values from -0.75 to 0.75
Outputs:
- class_logits: bfloat16 [256, 64, 19], P(('dp', 'fsdp'))
- grad_features: float32 [256, 64, 2048], P(('dp', 'fsdp'))
- grad_reduce: float32 [2048, 512], P(None, 'fsdp')
- grad_gain_reduce: float32 [512], replicated
- grad_bias_reduce: float32 [512], replicated
- grad_dilated: float32 [3, 3, 512, 512], P(None, None, None, 'fsdp')
- grad_gain_dilated: float32 [512], replicated
- grad_bias_dilated: float32 [512], replicated
- grad_expand: float32 [512, 2048], P(None, 'fsdp')
- grad_gain_expand: float32 [2048], replicated
- grad_bias_expand: float32 [2048], replicated
- grad_point: float32 [2048, 256], P(None, 'fsdp')
- grad_gain_point: float32 [256], replicated
- grad_bias_point: float32 [256], replicated
- grad_rate: float32 [3, 3, 2048, 256], P(None, None, None, 'fsdp')
- grad_gain_rate: float32 [256], replicated
- grad_bias_rate: float32 [256], replicated
- grad_rate_double: float32 [3, 3, 2048, 256], P(None, None, None, 'fsdp')
- grad_gain_rate_double: float32 [256], replicated
- grad_bias_rate_double: float32 [256], replicated
- grad_rate_triple: float32 [3, 3, 2048, 256], P(None, None, None, 'fsdp')
- grad_gain_rate_triple: float32 [256], replicated
- grad_bias_rate_triple: float32 [256], replicated
- grad_pool: float32 [2048, 256], P(None, 'fsdp')
- grad_merge: float32 [1280, 256], P(None, 'fsdp')
- grad_gain_merge: float32 [256], replicated
- grad_bias_merge: float32 [256], replicated
- grad_classes: float32 [256, 19], P('fsdp')
Inputs may be any that keep to these rules, and one draw needn't show every extreme that they name: `crop_ids`: each aligned tile of 64 rows holds 4 rectangular crops numbered tile * 4 + 0 to 3; two of them span all the tile's rows; -1 marks padding pixels; every crop has pixels.
All inputs are finite; a program needn't handle non-finite values.
Results may differ from a plain program's by a relative error of at most 0.04.
Values may be sent and summed in bfloat16 or wider, within the bound.
A program may use at most 448 MiB of HBM per device.

v0:
```python
import jax
import jax.numpy as jnp
from jax import lax
from jax.sharding import PartitionSpec as P

CLASSES = 19
CROPS_TILE = 4
DILATION_SPAN = 4
RATE = 12


eps = 1e-05


def passed_along(value, axis, by):
    count = lax.axis_size(axis)
    pairs = [(i, i + by) for i in range(count) if 0 <= i + by < count]
    return lax.ppermute(value, axis, pairs)


def padded(cells, sides, width):
    for axis, dim in sides:
        count = lax.axis_size(axis)
        ends = count - 1
        head = lax.slice_in_dim(cells, 0, width, axis=dim)
        tail = lax.slice_in_dim(cells, cells.shape[dim] - width, cells.shape[dim], axis=dim)
        cells = jnp.concatenate(
            [
                lax.ppermute(tail, axis, [(i, (i + 1) % count) for i in range(ends)]),
                cells,
                lax.ppermute(head, axis, [((i + 1) % count, i) for i in range(ends)]),
            ],
            axis=dim,
        )
    return cells


def flat_dot(first_op, second_op):
    return jnp.dot(first_op, second_op, preferred_element_type=jnp.float32)


def inner_dot(first_op, second_op):
    return lax.dot_general(
        first_op, second_op, (((0,), (0,)), ((), ())), preferred_element_type=jnp.float32
    )


def outer_dot(first_op, second_op):
    return lax.dot_general(
        first_op, second_op, (((1,), (1,)), ((), ())), preferred_element_type=jnp.float32
    )


def slope(values):
    gate_value = jax.nn.sigmoid(values)
    return gate_value * (1.0 + values * (1.0 - gate_value))


def widen_rows(values, extent, mover):
    row_count = values.shape[0]
    neighbours = -(-extent // row_count)
    above = [mover(values, distance) for distance in range(neighbours, 0, -1)]
    below = [mover(values, -distance) for distance in range(1, neighbours + 1)]
    stacked = jnp.concatenate(above + [values] + below, axis=0)
    start_row = neighbours * row_count - extent
    return stacked[start_row : start_row + row_count + 2 * extent]


def rim_slice(widened, spacing, margin, height):
    return widened[margin - spacing : margin + height + spacing]


def offset_table(broad_key_rows, crop_random_keys, spacing, margin):
    height, breadth = crop_random_keys.shape
    first_row = margin - spacing
    extended = jnp.pad(
        broad_key_rows[first_row : first_row + height + 2 * spacing], ((0, 0), (spacing, spacing))
    )
    tables = []
    for row_tap in range(3):
        for col_tap in range(3):
            nearby = extended[
                row_tap * spacing : row_tap * spacing + height,
                col_tap * spacing : col_tap * spacing + breadth,
            ]
            tables.append(
                ((nearby == crop_random_keys) & (crop_random_keys > 0))
                .astype(jnp.float32)
                .reshape(height * breadth, 1)
            )
    return tables


def spread_offsets(widened, kernel, tables, spacing, height, breadth):
    channels = widened.shape[2]
    extended = jnp.pad(widened, ((0, 0), (spacing, spacing), (0, 0)))
    summed = jnp.zeros((height * breadth, kernel.shape[3]), jnp.float32)
    for row_tap in range(3):
        for col_tap in range(3):
            nearby = extended[
                row_tap * spacing : row_tap * spacing + height,
                col_tap * spacing : col_tap * spacing + breadth,
            ]
            summed = summed + tables[3 * row_tap + col_tap] * flat_dot(
                nearby.reshape(height * breadth, channels), kernel[row_tap, col_tap]
            )
    return summed


def collect_taps(widened, kernel, tables, spacing, height, breadth):
    channels = widened.shape[2]
    extended = jnp.pad(widened, ((0, 0), (spacing, spacing), (0, 0)))
    summed = jnp.zeros((height * breadth, kernel.shape[2]), jnp.float32)
    for row_tap in range(3):
        for col_tap in range(3):
            back_row = 2 - row_tap
            back_col = 2 - col_tap
            nearby = extended[
                back_row * spacing : back_row * spacing + height,
                back_col * spacing : back_col * spacing + breadth,
            ]
            summed = summed + tables[3 * back_row + back_col] * outer_dot(
                nearby.reshape(height * breadth, channels), kernel[row_tap, col_tap]
            )
    return summed


def kernel_offsets(widened, grads_low, tables, spacing, height, breadth):
    channels = widened.shape[2]
    extended = jnp.pad(widened, ((0, 0), (spacing, spacing), (0, 0)))
    pieces = []
    for row_tap in range(3):
        for col_tap in range(3):
            nearby = extended[
                row_tap * spacing : row_tap * spacing + height,
                col_tap * spacing : col_tap * spacing + breadth,
            ]
            masked = (tables[3 * row_tap + col_tap] * grads_low).astype(jnp.bfloat16)
            pieces.append(inner_dot(nearby.reshape(height * breadth, channels), masked))
    return pieces


def statistics(partial_value):
    return lax.psum(partial_value, ("dp", "fsdp"))


def norm_apply(values, totals, squares, pixel_count, factor, offset):
    average = totals / pixel_count
    inverse = lax.rsqrt(squares / pixel_count - average * average + eps)
    normed = (values - average) * inverse
    return (normed * factor + offset, normed, inverse)


def norm_forward(values, inside, pixel_count, factor, offset):
    totals, squares = statistics(
        (jnp.sum(values * inside, axis=0), jnp.sum(values * values * inside, axis=0))
    )
    return norm_apply(values, totals, squares, pixel_count, factor, offset)


def norm_backward(upstream, normed, inverse, factor, inside, pixel_count):
    totals, crossed = lax.psum(
        (jnp.sum(upstream * inside, axis=0), jnp.sum(upstream * normed * inside, axis=0)),
        ("dp", "fsdp"),
    )
    passed = (
        inside
        * factor
        * inverse
        * (upstream - totals / pixel_count - normed * crossed / pixel_count)
    )
    return (passed, crossed, totals)


def body(
    features,
    crop_ids,
    labels,
    w_reduce,
    gain_reduce,
    bias_reduce,
    w_dilated,
    gain_dilated,
    bias_dilated,
    w_expand,
    gain_expand,
    bias_expand,
    w_point,
    gain_point,
    bias_point,
    w_rate,
    gain_rate,
    bias_rate,
    w_rate_double,
    gain_rate_double,
    bias_rate_double,
    w_rate_triple,
    gain_rate_triple,
    bias_rate_triple,
    w_pool,
    w_merge,
    gain_merge,
    bias_merge,
    w_classes,
):
    local_rows, local_columns, channels = features.shape
    pixel_values = local_rows * local_columns
    inputs_flat = features.reshape(pixel_values, channels)
    crop_random_keys = crop_ids + 1
    outer_extent = 3 * RATE
    spacings = (RATE, 2 * RATE, 3 * RATE)
    broad_key_rows = widen_rows(
        crop_random_keys,
        outer_extent,
        lambda piece, distance: passed_along(piece, "fsdp", distance),
    )
    inside = (crop_random_keys > 0).astype(jnp.float32).reshape(pixel_values, 1)
    inner_neck = offset_table(broad_key_rows, crop_random_keys, DILATION_SPAN, outer_extent)
    near_rates = [
        offset_table(broad_key_rows, crop_random_keys, spacing, outer_extent)
        for spacing in spacings
    ]
    (
        full_reduce,
        complete_dilated,
        full_expand,
        full_point,
        full_rate,
        full_double,
        full_triple,
        full_pool,
        full_merge,
        full_classes,
    ) = (
        lax.all_gather(w_reduce, "fsdp", axis=1, tiled=True),
        lax.all_gather(w_dilated, "fsdp", axis=3, tiled=True),
        lax.all_gather(w_expand, "fsdp", axis=1, tiled=True),
        lax.all_gather(w_point, "fsdp", axis=1, tiled=True),
        lax.all_gather(w_rate, "fsdp", axis=3, tiled=True),
        lax.all_gather(w_rate_double, "fsdp", axis=3, tiled=True),
        lax.all_gather(w_rate_triple, "fsdp", axis=3, tiled=True),
        lax.all_gather(w_pool, "fsdp", axis=1, tiled=True),
        lax.all_gather(w_merge, "fsdp", axis=1, tiled=True),
        lax.all_gather(w_classes, "fsdp", axis=0, tiled=True),
    )
    rate_kernels = (full_rate, full_double, full_triple)
    rate_gains = (gain_rate, gain_rate_double, gain_rate_triple)
    rate_biases = (bias_rate, bias_rate_double, bias_rate_triple)
    act_one = flat_dot(inputs_flat, full_reduce)
    totals, squares, pixel_count = statistics(
        (
            jnp.sum(act_one * inside, axis=0),
            jnp.sum(act_one * act_one * inside, axis=0),
            jnp.sum(inside),
        )
    )
    pre_one, normed_one, inverse_one = norm_apply(
        act_one, totals, squares, pixel_count, gain_reduce, bias_reduce
    )
    first_hidden = jax.nn.silu(pre_one).astype(jnp.bfloat16)
    first_broad = padded(
        first_hidden.reshape(local_rows, local_columns, -1), (("fsdp", 0),), DILATION_SPAN
    )
    second_activation = spread_offsets(
        first_broad, complete_dilated, inner_neck, DILATION_SPAN, local_rows, local_columns
    )
    pre_two, normed_two, inverse_two = norm_forward(
        second_activation, inside, pixel_count, gain_dilated, bias_dilated
    )
    hidden_two = jax.nn.silu(pre_two).astype(jnp.bfloat16)
    act_three = flat_dot(hidden_two, full_expand)
    pre_three, normed_three, inverse_three = norm_forward(
        act_three, inside, pixel_count, gain_expand, bias_expand
    )
    pre_three = pre_three + inputs_flat
    block_out = jax.nn.silu(pre_three).astype(jnp.bfloat16)
    wide_block = widen_rows(
        block_out.reshape(local_rows, local_columns, channels),
        outer_extent,
        lambda piece, distance: passed_along(piece, "fsdp", distance),
    )
    point_act = flat_dot(block_out, full_point)
    pre_point, normed_point, inverse_point = norm_forward(
        point_act, inside, pixel_count, gain_point, bias_point
    )
    branch_point = jax.nn.silu(pre_point).astype(jnp.bfloat16)
    rate_states = []
    rate_branches = []
    for kernel, factor, offset, spacing, tables in zip(
        rate_kernels, rate_gains, rate_biases, spacings, near_rates
    ):
        rate_act = spread_offsets(
            rim_slice(wide_block, spacing, outer_extent, local_rows),
            kernel,
            tables,
            spacing,
            local_rows,
            local_columns,
        )
        pre_rate, normed_rate, inverse_rate = norm_forward(
            rate_act, inside, pixel_count, factor, offset
        )
        rate_states.append((pre_rate, normed_rate, inverse_rate))
        rate_branches.append(jax.nn.silu(pre_rate).astype(jnp.bfloat16))
    crop_flat = crop_ids.reshape(pixel_values)
    crop_total = CROPS_TILE
    first_crop = lax.axis_index("dp") * crop_total
    owner_group = lax.axis_size("fsdp")
    owner_place = lax.axis_index("fsdp")
    local_crop = crop_flat - first_crop
    member = local_crop[:, None] == jnp.arange(crop_total)[None, :]
    member_low = member.astype(jnp.bfloat16)
    crop_sums = inner_dot(member_low, block_out)
    crop_sizes = jnp.sum(member.astype(jnp.float32), axis=0)
    crop_sums, crop_sizes = lax.psum((crop_sums, crop_sizes), "fsdp")
    pooled = (crop_sums / crop_sizes[:, None]).astype(jnp.bfloat16)
    pool_act = flat_dot(pooled, full_pool)
    pool_low = jax.nn.silu(pool_act).astype(jnp.bfloat16)
    branch_pool = flat_dot(member_low, pool_low).astype(jnp.bfloat16)
    joined = jnp.concatenate([branch_point] + rate_branches + [branch_pool], axis=1)
    merge_act = flat_dot(joined, full_merge)
    pre_merge, normed_merge, inverse_merge = norm_forward(
        merge_act, inside, pixel_count, gain_merge, bias_merge
    )
    merged = jax.nn.silu(pre_merge).astype(jnp.bfloat16)
    logits_full = flat_dot(merged, full_classes)
    class_logits = logits_full.astype(jnp.bfloat16).reshape(local_rows, local_columns, -1)
    (
        full_reduce,
        complete_dilated,
        full_expand,
        full_point,
        full_rate,
        full_double,
        full_triple,
        full_pool,
        full_merge,
        full_classes,
    ) = (
        lax.all_gather(w_reduce, "fsdp", axis=1, tiled=True),
        lax.all_gather(w_dilated, "fsdp", axis=3, tiled=True),
        lax.all_gather(w_expand, "fsdp", axis=1, tiled=True),
        lax.all_gather(w_point, "fsdp", axis=1, tiled=True),
        lax.all_gather(w_rate, "fsdp", axis=3, tiled=True),
        lax.all_gather(w_rate_double, "fsdp", axis=3, tiled=True),
        lax.all_gather(w_rate_triple, "fsdp", axis=3, tiled=True),
        lax.all_gather(w_pool, "fsdp", axis=1, tiled=True),
        lax.all_gather(w_merge, "fsdp", axis=1, tiled=True),
        lax.all_gather(w_classes, "fsdp", axis=0, tiled=True),
    )
    rate_kernels = (full_rate, full_double, full_triple)
    highest = jnp.max(logits_full, axis=1, keepdims=True)
    shifted = jnp.exp(logits_full - highest)
    probability = shifted / jnp.sum(shifted, axis=1, keepdims=True)
    targets = (labels.reshape(pixel_values, 1) == jnp.arange(CLASSES)[None, :]).astype(jnp.float32)
    grad_logits = (inside * (probability - targets) / pixel_count).astype(jnp.bfloat16)
    grad_classes = inner_dot(merged, grad_logits)
    grad_merged = outer_dot(grad_logits, full_classes)
    passed, grad_gain_merge, grad_bias_merge = norm_backward(
        grad_merged * slope(pre_merge), normed_merge, inverse_merge, gain_merge, inside, pixel_count
    )
    grad_merge_act = passed.astype(jnp.bfloat16)
    grad_merge = inner_dot(joined, grad_merge_act)
    grad_joined = outer_dot(grad_merge_act, full_merge)
    branch_width = full_merge.shape[1]
    passed, grad_gain_point, grad_bias_point = norm_backward(
        grad_joined[:, :branch_width] * slope(pre_point),
        normed_point,
        inverse_point,
        gain_point,
        inside,
        pixel_count,
    )
    grad_point_act = passed.astype(jnp.bfloat16)
    grad_point = inner_dot(block_out, grad_point_act)
    grad_block = outer_dot(grad_point_act, full_point)
    rate_grads = []
    rate_weight_grads = []
    rate_gain_grads = []
    rate_bias_grads = []
    for branch in range(3):
        column = (1 + branch) * branch_width
        pre_rate, normed_rate, inverse_rate = rate_states[branch]
        passed, gain_grad, bias_grad = norm_backward(
            grad_joined[:, column : column + branch_width] * slope(pre_rate),
            normed_rate,
            inverse_rate,
            rate_gains[branch],
            inside,
            pixel_count,
        )
        grad_rate_act = passed.astype(jnp.bfloat16)
        pieces = kernel_offsets(
            rim_slice(wide_block, spacings[branch], outer_extent, local_rows),
            grad_rate_act,
            near_rates[branch],
            spacings[branch],
            local_rows,
            local_columns,
        )
        rate_weight_grads.append(jnp.stack(pieces).reshape(3, 3, channels, branch_width))
        rate_grads.append(grad_rate_act)
        rate_gain_grads.append(gain_grad)
        rate_bias_grads.append(bias_grad)
    rate_grads_low = jnp.concatenate(rate_grads, axis=1).reshape(local_rows, local_columns, -1)
    wide_grad_rate = widen_rows(
        rate_grads_low, outer_extent, lambda piece, distance: passed_along(piece, "fsdp", distance)
    )
    for branch in range(3):
        grad_slab = wide_grad_rate[:, :, branch * branch_width : (branch + 1) * branch_width]
        grad_block = grad_block + collect_taps(
            rim_slice(grad_slab, spacings[branch], outer_extent, local_rows),
            rate_kernels[branch],
            near_rates[branch],
            spacings[branch],
            local_rows,
            local_columns,
        )
    crop_grad = lax.dot_general(
        member.astype(jnp.float32),
        grad_joined[:, 4 * branch_width :],
        (((0,), (0,)), ((), ())),
        precision=lax.Precision.HIGHEST,
        preferred_element_type=jnp.float32,
    )
    crop_grad = lax.psum(crop_grad, "fsdp")
    grad_pool_act = (crop_grad * slope(pool_act)).astype(jnp.bfloat16)
    owned_crops = (jnp.arange(crop_total) % owner_group == owner_place).astype(jnp.float32)[:, None]
    grad_pool = inner_dot(pooled, (grad_pool_act * owned_crops).astype(jnp.bfloat16))
    grad_pooled = outer_dot(grad_pool_act, full_pool) / crop_sizes[:, None]
    grad_block = grad_block + inside * jnp.take(
        grad_pooled, jnp.clip(local_crop, 0, crop_total - 1), axis=0
    )
    grad_pre_three = grad_block * slope(pre_three)
    passed, grad_gain_expand, grad_bias_expand = norm_backward(
        grad_pre_three, normed_three, inverse_three, gain_expand, inside, pixel_count
    )
    grad_three = passed.astype(jnp.bfloat16)
    grad_expand = inner_dot(hidden_two, grad_three)
    grad_hidden_two = outer_dot(grad_three, full_expand)
    passed, grad_gain_dilated, grad_bias_dilated = norm_backward(
        grad_hidden_two * slope(pre_two), normed_two, inverse_two, gain_dilated, inside, pixel_count
    )
    second_gradient = passed.astype(jnp.bfloat16)
    dilated_fragments = kernel_offsets(
        first_broad, second_gradient, inner_neck, DILATION_SPAN, local_rows, local_columns
    )
    grad_dilated = jnp.stack(dilated_fragments).reshape(
        3, 3, second_gradient.shape[1], second_gradient.shape[1]
    )
    broad_neck_gradient = padded(
        second_gradient.reshape(local_rows, local_columns, -1), (("fsdp", 0),), DILATION_SPAN
    )
    grad_hidden_one = collect_taps(
        broad_neck_gradient, complete_dilated, inner_neck, DILATION_SPAN, local_rows, local_columns
    )
    passed, grad_gain_reduce, grad_bias_reduce = norm_backward(
        grad_hidden_one * slope(pre_one), normed_one, inverse_one, gain_reduce, inside, pixel_count
    )
    grad_one = passed.astype(jnp.bfloat16)
    grad_reduce = inner_dot(inputs_flat, grad_one)
    grad_features = (grad_pre_three + outer_dot(grad_one, full_reduce)).reshape(
        local_rows, local_columns, channels
    )
    shards = (
        lax.psum_scatter(grad_reduce, "fsdp", scatter_dimension=1, tiled=True),
        lax.psum_scatter(grad_dilated, "fsdp", scatter_dimension=3, tiled=True),
        lax.psum_scatter(grad_expand, "fsdp", scatter_dimension=1, tiled=True),
        lax.psum_scatter(grad_point, "fsdp", scatter_dimension=1, tiled=True),
        lax.psum_scatter(rate_weight_grads[0], "fsdp", scatter_dimension=3, tiled=True),
        lax.psum_scatter(rate_weight_grads[1], "fsdp", scatter_dimension=3, tiled=True),
        lax.psum_scatter(rate_weight_grads[2], "fsdp", scatter_dimension=3, tiled=True),
        lax.psum_scatter(grad_pool, "fsdp", scatter_dimension=1, tiled=True),
        lax.psum_scatter(grad_merge, "fsdp", scatter_dimension=1, tiled=True),
        lax.psum_scatter(grad_classes, "fsdp", scatter_dimension=0, tiled=True),
    )
    shards = (
        lax.psum(shards[0].astype(jnp.bfloat16), "dp").astype(jnp.float32),
        lax.psum(shards[1].astype(jnp.bfloat16), "dp").astype(jnp.float32),
        lax.psum(shards[2].astype(jnp.bfloat16), "dp").astype(jnp.float32),
        lax.psum(shards[3].astype(jnp.bfloat16), "dp").astype(jnp.float32),
        lax.psum(shards[4].astype(jnp.bfloat16), "dp").astype(jnp.float32),
        lax.psum(shards[5].astype(jnp.bfloat16), "dp").astype(jnp.float32),
        lax.psum(shards[6].astype(jnp.bfloat16), "dp").astype(jnp.float32),
        lax.psum(shards[7].astype(jnp.bfloat16), "dp").astype(jnp.float32),
        lax.psum(shards[8].astype(jnp.bfloat16), "dp").astype(jnp.float32),
        lax.psum(shards[9].astype(jnp.bfloat16), "dp").astype(jnp.float32),
    )
    return (
        class_logits,
        grad_features,
        shards[0],
        grad_gain_reduce,
        grad_bias_reduce,
        shards[1],
        grad_gain_dilated,
        grad_bias_dilated,
        shards[2],
        grad_gain_expand,
        grad_bias_expand,
        shards[3],
        grad_gain_point,
        grad_bias_point,
        shards[4],
        rate_gain_grads[0],
        rate_bias_grads[0],
        shards[5],
        rate_gain_grads[1],
        rate_bias_grads[1],
        shards[6],
        rate_gain_grads[2],
        rate_bias_grads[2],
        shards[7],
        shards[8],
        grad_gain_merge,
        grad_bias_merge,
        shards[9],
    )


def solution(mesh):
    return jax.shard_map(
        body,
        mesh=mesh,
        in_specs=(
            P(("dp", "fsdp"), None, None),
            P(("dp", "fsdp"), None),
            P(("dp", "fsdp"), None),
            P(None, "fsdp"),
            P(),
            P(),
            P(None, None, None, "fsdp"),
            P(),
            P(),
            P(None, "fsdp"),
            P(),
            P(),
            P(None, "fsdp"),
            P(),
            P(),
            P(None, None, None, "fsdp"),
            P(),
            P(),
            P(None, None, None, "fsdp"),
            P(),
            P(),
            P(None, None, None, "fsdp"),
            P(),
            P(),
            P(None, "fsdp"),
            P(None, "fsdp"),
            P(),
            P(),
            P("fsdp", None),
        ),
        out_specs=(
            P(("dp", "fsdp"), None, None),
            P(("dp", "fsdp"), None, None),
            P(None, "fsdp"),
            P(),
            P(),
            P(None, None, None, "fsdp"),
            P(),
            P(),
            P(None, "fsdp"),
            P(),
            P(),
            P(None, "fsdp"),
            P(),
            P(),
            P(None, None, None, "fsdp"),
            P(),
            P(),
            P(None, None, None, "fsdp"),
            P(),
            P(),
            P(None, None, None, "fsdp"),
            P(),
            P(),
            P(None, "fsdp"),
            P(None, "fsdp"),
            P(),
            P(),
            P("fsdp", None),
        ),
        check_vma=False,
    )
```

profile of v0, /device:TPU:0, one launch (start us, length us, event | category | flops | bytes accessed | tf_op | source)
XLA Modules:
  0.0 2116.6 jit_solution(13876331331139279268)
XLA Ops:
  20.9 18.7 all_gather.48
  65.7 40.1 %all-reduce.21 = (f32[512]{0:T(512)S(1)}, f32[]{:T(128)}, f32[512]{0:T(512)S(1)}) all-reduce(f32[512]{0:T(512)S(1)} %get-tuple-element.39, f32[]{:T(128)} %fusion.295, f32[512]{0:T(512)S(1)} %get-tuple-element.38), channel_id=1, replica_groups=mesh['dp'=4,'fsdp'=8] {'dp','fsdp'}, use_global_device_ids=true, to_apply=%region_5.6 | all-reduce | flops 1025 | bytes 8200 | tf_op jit(solution)/shard_map/psum | solution.py:144
  124.9 44.5 %all-reduce.20 = (f32[512]{0:T(512)S(1)}, f32[512]{0:T(512)S(1)}) all-reduce(f32[512]{0:T(512)S(1)} %get-tuple-element.37, f32[512]{0:T(512)S(1)} %get-tuple-element.36), channel_id=1, replica_groups=mesh['dp'=4,'fsdp'=8] {'dp','fsdp'}, use_global_device_ids=true, to_apply=%region_9.10 | all-reduce | flops 1024 | bytes 8192 | tf_op jit(solution)/shard_map/psum | solution.py:144
  175.3 39.9 %all-reduce.19 = (f32[2048]{0:T(1024)S(1)}, f32[2048]{0:T(1024)S(1)}) all-reduce(f32[2048]{0:T(1024)S(1)} %get-tuple-element.31, f32[2048]{0:T(1024)S(1)} %get-tuple-element.30), channel_id=1, replica_groups=mesh['dp'=4,'fsdp'=8] {'dp','fsdp'}, use_global_device_ids=true, to_apply=%region_13.14 | all-reduce | flops 4096 | bytes 32768 | tf_op jit(solution)/shard_map/psum | solution.py:144
  241.3 128.1 %all-reduce.22 = (f32[4,2048]{1,0:T(4,128)S(1)}, f32[4]{0:T(128)S(1)}) all-reduce(f32[4,2048]{1,0:T(4,128)S(1)} %fusion.221, f32[4]{0:T(128)S(1)} %convert_reduce_fusion), channel_id=1, replica_groups=mesh['dp'=4,'fsdp'=8] {'fsdp'}, use_global_device_ids=true, to_apply=%region_30.31 | all-reduce | flops 8196 | bytes 65568 | tf_op jit(solution)/shard_map/psum | solution.py:315
  373.0 10.8 collective-permute-done.18
  385.1 67.3 %collective-permute-done.19 = bf16[8,64,2048]{2,1,0:T(8,128)(2,1)} collective-permute-done((bf16[8,64,2048]{2,1,0:T(8,128)(2,1)S(1)}, bf16[8,64,2048]{2,1,0:T(8,128)(2,1)}, u32[]{:S(2)}, u32[]{:S(2)}) %collective-permute-start.19) | collective-permute-done | bytes 2097184 | tf_op jit(solution)/shard_map/ppermute | solution.py:18
  485.8 33.3 %collective-permute-done.9 = bf16[8,64,2048]{2,1,0:T(8,128)(2,1)} collective-permute-done((bf16[8,64,2048]{2,1,0:T(8,128)(2,1)S(1)}, bf16[8,64,2048]{2,1,0:T(8,128)(2,1)}, u32[]{:S(2)}, u32[]{:S(2)}) %collective-permute-start.9) | collective-permute-done | bytes 2097184 | tf_op jit(solution)/shard_map/ppermute | solution.py:18
  527.2 61.2 %collective-permute-done.20 = bf16[8,64,2048]{2,1,0:T(8,128)(2,1)} collective-permute-done((bf16[8,64,2048]{2,1,0:T(8,128)(2,1)S(1)}, bf16[8,64,2048]{2,1,0:T(8,128)(2,1)}, u32[]{:S(2)}, u32[]{:S(2)}) %collective-permute-start.20) | collective-permute-done | bytes 2097184 | tf_op jit(solution)/shard_map/ppermute | solution.py:18
  597.6 17.6 slice.840
  643.6 14.2 pad_slice_fusion.13
  714.1 61.4 %all-reduce.18 = (f32[256]{0:T(256)S(1)}, f32[256]{0:T(256)S(1)}, f32[256]{0:T(256)S(1)}, f32[256]{0:T(256)S(1)}, f32[256]{0:T(256)S(1)}, /*index=5*/f32[256]{0:T(256)S(1)}, f32[256]{0:T(256)S(1)}, f32[256]{0:T(256)S(1)}) all-reduce(f32[256]{0:T(256)S(1)} %get-tuple-element.66, ...), channel_id=1, replica_groups=mesh['dp'=4,'fsdp'=8] {'dp','fsdp'}, use_global_device_ids=true, to_apply=%region_15.16 | all-reduce | flops 2048 | bytes 16384 | tf_op jit(solution)/shard_map/psum | solution.py:144
  783.4 41.4 %all-reduce.17 = (f32[256]{0:T(256)S(1)}, f32[256]{0:T(256)S(1)}) all-reduce(f32[256]{0:T(256)S(1)} %get-tuple-element.51, f32[256]{0:T(256)S(1)} %get-tuple-element.50), channel_id=1, replica_groups=mesh['dp'=4,'fsdp'=8] {'dp','fsdp'}, use_global_device_ids=true, to_apply=%region_34.35 | all-reduce | flops 512 | bytes 4096 | tf_op jit(solution)/shard_map/psum | solution.py:144
  831.0 38.6 %all-reduce.16 = (f32[256]{0:T(256)S(1)}, f32[256]{0:T(256)S(1)}) all-reduce(f32[256]{0:T(256)S(1)} %get-tuple-element.49, f32[256]{0:T(256)S(1)} %get-tuple-element.48), channel_id=1, replica_groups=mesh['dp'=4,'fsdp'=8] {'dp','fsdp'}, use_global_device_ids=true, to_apply=%region_42.43 | all-reduce | flops 512 | bytes 4096 | tf_op jit(solution)/shard_map/psum | solution.py:162
  879.6 12.7 psum.351
  898.8 39.2 %all-reduce.15 = (f32[256]{0:T(256)S(1)}, f32[256]{0:T(256)S(1)}, f32[256]{0:T(256)S(1)}, f32[256]{0:T(256)S(1)}, f32[256]{0:T(256)}, /*index=5*/f32[256]{0:T(256)S(1)}, f32[256]{0:T(256)}, f32[256]{0:T(256)S(1)}) all-reduce(f32[256]{0:T(256)S(1)} %get-tuple-element.64, ...), channel_id=1, replica_groups=mesh['dp'=4,'fsdp'=8] {'dp','fsdp'}, use_global_device_ids=true, to_apply=%region_58.59 | all-reduce | flops 2048 | bytes 16384 | tf_op jit(solution)/shard_map/psum | solution.py:162
  983.0 20.3 collective-permute-done.28
  1005.8 20.0 collective-permute-done.29
  1051.0 11.4 collective-permute-done.30
  1139.9 42.2 %multiply_reduce_fusion.1 = (f32[2048]{0:T(1024)S(1)}, f32[2048]{0:T(1024)S(1)}, f32[512,2048]{1,0:T(8,128)}) fusion(f32[512]{0:T(512)S(1)} %mul.1668, f32[2048]{0:T(1024)S(1)} %copy-done.93, f32[512,2048]{1,0:T(8,128)} %get-tuple-element.311, f32[2048]{0:T(1024)S(1)} %copy-done.91, bf16[512,2048]{1,0:T(8,128)(2,1)} %bitcast.545, f32[2048]{0:T(1024)S(1)} %copy-done.105, ...), kind=kOutput, calls=%fused_computation.33 | convolution fusion | flops 616558592 | bytes 129337856 | tf_op jit(solution)/shard_map/dot_general | solution.py:49
  1182.1 45.7 %all-reduce.14 = (f32[2048]{0:T(1024)S(1)}, f32[2048]{0:T(1024)S(1)}) all-reduce(f32[2048]{0:T(1024)S(1)} %get-tuple-element.29, f32[2048]{0:T(1024)S(1)} %get-tuple-element.28), channel_id=1, replica_groups=mesh['dp'=4,'fsdp'=8] {'dp','fsdp'}, use_global_device_ids=true, to_apply=%region_63.64 | all-reduce | flops 4096 | bytes 32768 | tf_op jit(solution)/shard_map/psum | solution.py:162
  1243.7 39.4 %all-reduce.13 = (f32[512]{0:T(512)S(1)}, f32[512]{0:T(512)S(1)}) all-reduce(f32[512]{0:T(512)S(1)} %get-tuple-element.35, f32[512]{0:T(512)S(1)} %get-tuple-element.34), channel_id=1, replica_groups=mesh['dp'=4,'fsdp'=8] {'dp','fsdp'}, use_global_device_ids=true, to_apply=%region_67.68 | all-reduce | flops 1024 | bytes 8192 | tf_op jit(solution)/shard_map/psum | solution.py:162
  1301.4 43.5 %all-reduce.12 = (f32[512]{0:T(512)S(1)}, f32[512]{0:T(512)S(1)}) all-reduce(f32[512]{0:T(512)S(1)} %get-tuple-element.33, f32[512]{0:T(512)S(1)} %get-tuple-element.32), channel_id=1, replica_groups=mesh['dp'=4,'fsdp'=8] {'dp','fsdp'}, use_global_device_ids=true, to_apply=%region_71.72 | all-reduce | flops 1024 | bytes 8192 | tf_op jit(solution)/shard_map/psum | solution.py:162
  1395.5 19.4 copy.79
  1441.4 19.4 copy.78
  1483.5 20.0 copy.77
  1517.2 95.2 %reduce-scatter.25.cloned.1.call-done = f32[3,3,2048,32]{2,3,1,0:T(8,128)} async-done(((f32[3,3,2048,256]{2,3,1,0:T(8,128)}), f32[3,3,2048,32]{2,3,1,0:T(8,128)}) %reduce-scatter.25.cloned.1.call-update) | async-done | bytes 2359312 | tf_op jit(solution)/shard_map/reduce_scatter | solution.py:472
  1615.3 126.7 %reduce-scatter.23.cloned.1.call-done = f32[3,3,2048,32]{2,3,1,0:T(8,128)} async-done(((f32[3,3,2048,256]{2,3,1,0:T(8,128)}), f32[3,3,2048,32]{2,3,1,0:T(8,128)}) %reduce-scatter.23.cloned.1.call-update) | async-done | bytes 2359312 | tf_op jit(solution)/shard_map/reduce_scatter | solution.py:471
  1744.9 126.7 %reduce-scatter.21.cloned.1.call-done = f32[3,3,2048,32]{2,3,1,0:T(8,128)} async-done(((f32[3,3,2048,256]{2,3,1,0:T(8,128)}), f32[3,3,2048,32]{2,3,1,0:T(8,128)}) %reduce-scatter.21.cloned.1.call-update) | async-done | bytes 2359312 | tf_op jit(solution)/shard_map/reduce_scatter | solution.py:470
  1875.2 33.2 %reduce-scatter.31.cloned.1.call-done = f32[32,19]{1,0:T(8,128)} async-done(((f32[256,19]{1,0:T(8,128)}), f32[32,19]{1,0:T(8,128)}) %reduce-scatter.31.cloned.1.call-update) | async-done | bytes 2448
  1909.2 11.8 psum.367
  1928.5 169.7 %all-reduce.26.cloned.1.call-done = (bf16[2048,64]{0,1:T(8,128)(2,1)}, bf16[3,3,512,64]{2,3,1,0:T(8,128)(2,1)}, bf16[512,256]{1,0:T(8,128)(2,1)}, bf16[2048,32]{...) async-done(((bf16[2048,64]{0,1:T(8,128)(2,1)}, ...) | async-done | bytes 4997136 | tf_op jit(solution)/shard_map/psum | solution.py:478
  (808 shorter events, 585.2 us)
Async XLA Ops:
  8.0 109.1 %all-gather.12.cloned.1.call-start = ((), (), s32[]{:S(2)}) async-start(), calls=%async_computation.11 | async-start | bytes 5308416 | tf_op jit(solution)/shard_map/all_gather | solution.py:236
  8.7 161.3 %all-gather.14.cloned.1.call-start = ((), (), s32[]{:S(2)}) async-start(), calls=%async_computation.12 | async-start | bytes 2359296 | tf_op jit(solution)/shard_map/all_gather | solution.py:237
  9.5 359.9 %all-gather.24.cloned.1.call-start = ((), (), s32[]{:S(2)}) async-start(), calls=%async_computation.17 | async-start | bytes 1179648 | tf_op jit(solution)/shard_map/all_gather | solution.py:242
  10.1 360.9 %all-gather.16.cloned.1.call-start = ((), (), s32[]{:S(2)}) async-start(), calls=%async_computation.13 | async-start | bytes 1179648 | tf_op jit(solution)/shard_map/all_gather | solution.py:238
  10.6 647.3 %all-gather.22.cloned.1.call-start = ((), (), s32[]{:S(2)}) async-start(), calls=%async_computation.16 | async-start | bytes 10616832 | tf_op jit(solution)/shard_map/all_gather | solution.py:241
  11.2 650.1 %all-gather.20.cloned.1.call-start = ((), (), s32[]{:S(2)}) async-start(), calls=%async_computation.15 | async-start | bytes 10616832 | tf_op jit(solution)/shard_map/all_gather | solution.py:240
  12.0 670.2 %all-gather.18.cloned.1.call-start = ((), (), s32[]{:S(2)}) async-start(), calls=%async_computation.14 | async-start | bytes 10616832 | tf_op jit(solution)/shard_map/all_gather | solution.py:239
  20.3 1486.0 %reduce-scatter.29.cloned.1.call-start = ((), (), s32[]{:S(2)}) async-start(), calls=%async_computation.26 | async-start | bytes 1474560 | tf_op jit(solution)/shard_map/reduce_scatter | solution.py:474
  220.5 163.3 %collective-permute-start.18 = (bf16[8,64,2048]{2,1,0:T(8,128)(2,1)S(1)}, bf16[8,64,2048]{2,1,0:T(8,128)(2,1)}, u32[]{:S(2)}, u32[]{:S(2)}) collective-permute-start(bf16[8,64,2048]{2,1,0:T(8,128)(2,1)S(1)} %bitcast.520), channel_id=1, source_target_pairs={{0,5},{1,6},{2,7},{8,13},{9,14},{10,15},{16,21},{17,22},{18,23},{2... | collective-permute-start | bytes 6291464 | tf_op jit(solution)/shard_map/ppermute | solution.py:18
  224.9 227.5 %collective-permute-start.19 = (bf16[8,64,2048]{2,1,0:T(8,128)(2,1)S(1)}, bf16[8,64,2048]{2,1,0:T(8,128)(2,1)}, u32[]{:S(2)}, u32[]{:S(2)}) collective-permute-start(bf16[8,64,2048]{2,1,0:T(8,128)(2,1)S(1)} %bitcast.521), channel_id=1, source_target_pairs={{0,4},{1,5},{2,6},{3,7},{8,12},{9,13},{10,14},{11,15},{16,20},{17,... | collective-permute-start | bytes 6291464 | tf_op jit(solution)/shard_map/ppermute | solution.py:18
  228.2 233.7 %collective-permute-start.12 = (bf16[8,64,2048]{2,1,0:T(8,128)(2,1)S(1)}, bf16[8,64,2048]{2,1,0:T(8,128)(2,1)}, u32[]{:S(2)}, u32[]{:S(2)}) collective-permute-start(bf16[8,64,2048]{2,1,0:T(8,128)(2,1)S(1)} %bitcast.522), channel_id=1, source_target_pairs={{0,3},{1,4},{2,5},{3,6},{4,7},{8,11},{9,12},{10,13},{11,14},{12,15... | collective-permute-start | bytes 6291464 | tf_op jit(solution)/shard_map/ppermute | solution.py:18
  231.1 235.5 %collective-permute-start.6 = (bf16[8,64,2048]{2,1,0:T(8,128)(2,1)S(1)}, bf16[8,64,2048]{2,1,0:T(8,128)(2,1)}, u32[]{:S(2)}, u32[]{:S(2)}) collective-permute-start(bf16[8,64,2048]{2,1,0:T(8,128)(2,1)S(1)} %bitcast.523), channel_id=1, source_target_pairs={{0,2},{1,3},{2,4},{3,5},{4,6},{5,7},{8,10},{9,11},{10,12},{11,13},... | collective-permute-start | bytes 6291464 | tf_op jit(solution)/shard_map/ppermute | solution.py:18
  237.4 233.6 %collective-permute-start.7 = (bf16[8,64,2048]{2,1,0:T(8,128)(2,1)S(1)}, bf16[8,64,2048]{2,1,0:T(8,128)(2,1)}, u32[]{:S(2)}, u32[]{:S(2)}) collective-permute-start(bf16[8,64,2048]{2,1,0:T(8,128)(2,1)S(1)} %bitcast.524), channel_id=1, source_target_pairs={{0,1},{1,2},{2,3},{3,4},{4,5},{5,6},{6,7},{8,9},{9,10},{10,11},{11... | collective-permute-start | bytes 6291464 | tf_op jit(solution)/shard_map/ppermute | solution.py:18
  383.8 100.3 %collective-permute-start.8 = (bf16[8,64,2048]{2,1,0:T(8,128)(2,1)S(1)}, bf16[8,64,2048]{2,1,0:T(8,128)(2,1)S(1)}, u32[]{:S(2)}, u32[]{:S(2)}) collective-permute-start(bf16[8,64,2048]{2,1,0:T(8,128)(2,1)S(1)} %bitcast.525), channel_id=1, source_target_pairs={{1,0},{2,1},{3,2},{4,3},{5,4},{6,5},{7,6},{9,8},{10,9},{11,10},{12... | collective-permute-start | bytes 6291464 | tf_op jit(solution)/shard_map/ppermute | solution.py:18
  452.5 66.6 %collective-permute-start.9 = (bf16[8,64,2048]{2,1,0:T(8,128)(2,1)S(1)}, bf16[8,64,2048]{2,1,0:T(8,128)(2,1)}, u32[]{:S(2)}, u32[]{:S(2)}) collective-permute-start(bf16[8,64,2048]{2,1,0:T(8,128)(2,1)S(1)} %bitcast.526), channel_id=1, source_target_pairs={{2,0},{3,1},{4,2},{5,3},{6,4},{7,5},{10,8},{11,9},{12,10},{13,11},... | collective-permute-start | bytes 6291464 | tf_op jit(solution)/shard_map/ppermute | solution.py:18
  462.0 61.9 %collective-permute-start.13 = (bf16[8,64,2048]{2,1,0:T(8,128)(2,1)S(1)}, bf16[8,64,2048]{2,1,0:T(8,128)(2,1)}, u32[]{:S(2)}, u32[]{:S(2)}) collective-permute-start(bf16[8,64,2048]{2,1,0:T(8,128)(2,1)S(1)} %bitcast.527), channel_id=1, source_target_pairs={{3,0},{4,1},{5,2},{6,3},{7,4},{11,8},{12,9},{13,10},{14,11},{15,12... | collective-permute-start | bytes 6291464 | tf_op jit(solution)/shard_map/ppermute | solution.py:18
  466.5 121.9 %collective-permute-start.20 = (bf16[8,64,2048]{2,1,0:T(8,128)(2,1)S(1)}, bf16[8,64,2048]{2,1,0:T(8,128)(2,1)}, u32[]{:S(2)}, u32[]{:S(2)}) collective-permute-start(bf16[8,64,2048]{2,1,0:T(8,128)(2,1)S(1)} %bitcast.528), channel_id=1, source_target_pairs={{4,0},{5,1},{6,2},{7,3},{12,8},{13,9},{14,10},{15,11},{20,16},{21,... | collective-permute-start | bytes 6291464 | tf_op jit(solution)/shard_map/ppermute | solution.py:18
  471.1 118.4 %collective-permute-start.21 = (bf16[8,64,2048]{2,1,0:T(8,128)(2,1)S(1)}, bf16[8,64,2048]{2,1,0:T(8,128)(2,1)}, u32[]{:S(2)}, u32[]{:S(2)}) collective-permute-start(bf16[8,64,2048]{2,1,0:T(8,128)(2,1)S(1)} %bitcast.529), channel_id=1, source_target_pairs={{5,0},{6,1},{7,2},{13,8},{14,9},{15,10},{21,16},{22,17},{23,18},{2... | collective-permute-start | bytes 6291464 | tf_op jit(solution)/shard_map/ppermute | solution.py:18
  874.1 633.7 %reduce-scatter.27.cloned.1.call-start = ((), (), s32[]{:S(2)}) async-start(), calls=%async_computation.25 | async-start | bytes 2359296 | tf_op jit(solution)/shard_map/reduce_scatter | solution.py:473
  894.2 615.2 %reduce-scatter.19.cloned.1.call-start = ((), (), s32[]{:S(2)}) async-start(), calls=%async_computation.21 | async-start | bytes 2359296 | tf_op jit(solution)/shard_map/reduce_scatter | solution.py:469
  945.3 85.6 %collective-permute-start.22 = (bf16[8,64,768]{2,1,0:T(8,128)(2,1)S(1)}, bf16[8,64,768]{2,1,0:T(8,128)(2,1)}, u32[]{:S(2)}, u32[]{:S(2)}) collective-permute-start(bf16[8,64,768]{2,1,0:T(8,128)(2,1)S(1)} %bitcast.548), channel_id=1, source_target_pairs={{0,2},{1,3},{2,4},{3,5},{4,6},{5,7},{8,10},{9,11},{10,12},{11,13},... | collective-permute-start | bytes 2359304 | tf_op jit(solution)/shard_map/ppermute | solution.py:18
  950.3 83.2 %collective-permute-start.23 = (bf16[8,64,768]{2,1,0:T(8,128)(2,1)S(1)}, bf16[8,64,768]{2,1,0:T(8,128)(2,1)}, u32[]{:S(2)}, u32[]{:S(2)}) collective-permute-start(bf16[8,64,768]{2,1,0:T(8,128)(2,1)S(1)} %bitcast.549), channel_id=1, source_target_pairs={{0,1},{1,2},{2,3},{3,4},{4,5},{5,6},{6,7},{8,9},{9,10},{10,11},{11... | collective-permute-start | bytes 2359304 | tf_op jit(solution)/shard_map/ppermute | solution.py:18
  955.4 70.3 %collective-permute-start.29 = (bf16[8,64,768]{2,1,0:T(8,128)(2,1)S(1)}, bf16[8,64,768]{2,1,0:T(8,128)(2,1)}, u32[]{:S(2)}, u32[]{:S(2)}) collective-permute-start(bf16[8,64,768]{2,1,0:T(8,128)(2,1)S(1)} %bitcast.551), channel_id=1, source_target_pairs={{0,4},{1,5},{2,6},{3,7},{8,12},{9,13},{10,14},{11,15},{16,20},{17,... | collective-permute-start | bytes 2359304 | tf_op jit(solution)/shard_map/ppermute | solution.py:18
  957.9 70.4 %collective-permute-start.26 = (bf16[8,64,768]{2,1,0:T(8,128)(2,1)S(1)}, bf16[8,64,768]{2,1,0:T(8,128)(2,1)}, u32[]{:S(2)}, u32[]{:S(2)}) collective-permute-start(bf16[8,64,768]{2,1,0:T(8,128)(2,1)S(1)} %bitcast.552), channel_id=1, source_target_pairs={{0,3},{1,4},{2,5},{3,6},{4,7},{8,11},{9,12},{10,13},{11,14},{12,15... | collective-permute-start | bytes 2359304 | tf_op jit(solution)/shard_map/ppermute | solution.py:18
  967.7 543.4 %reduce-scatter.17.cloned.1.call-start = ((), (), s32[]{:S(2)}) async-start(), calls=%async_computation.20 | async-start | bytes 4718592 | tf_op jit(solution)/shard_map/reduce_scatter | solution.py:468
  1238.7 274.4 %reduce-scatter.13.cloned.1.call-start = ((), (), s32[]{:S(2)}) async-start(), calls=%async_computation.18 | async-start | bytes 4718592 | tf_op jit(solution)/shard_map/reduce_scatter | solution.py:466
  1351.7 163.3 %reduce-scatter.15.cloned.1.call-start = ((), (), s32[]{:S(2)}) async-start(), calls=%async_computation.19 | async-start | bytes 10616832 | tf_op jit(solution)/shard_map/reduce_scatter | solution.py:467
  1373.1 239.4 %reduce-scatter.25.cloned.1.call-start = ((), (), s32[]{:S(2)}) async-start(), calls=%async_computation.24 | async-start | bytes 21233664 | tf_op jit(solution)/shard_map/reduce_scatter | solution.py:472
  1414.9 327.1 %reduce-scatter.23.cloned.1.call-start = ((), (), s32[]{:S(2)}) async-start(), calls=%async_computation.23 | async-start | bytes 21233664 | tf_op jit(solution)/shard_map/reduce_scatter | solution.py:471
  1460.8 410.8 %reduce-scatter.21.cloned.1.call-start = ((), (), s32[]{:S(2)}) async-start(), calls=%async_computation.22 | async-start | bytes 21233664 | tf_op jit(solution)/shard_map/reduce_scatter | solution.py:470
  1503.6 404.8 %reduce-scatter.31.cloned.1.call-start = ((), (), s32[]{:S(2)}) async-start(), calls=%async_computation.27 | async-start | bytes 147456
  1506.2 592.0 %all-reduce.26.cloned.1.call-start = ((), (), s32[]{:S(2)}) async-start(), calls=%async_computation.28 | async-start | bytes 9994240 | tf_op jit(solution)/shard_map/psum | solution.py:478
  (222 other events, 4200.8 us)
Sparse Core Ops, SparseCore 0:
  10.0 32.4 all-gather.9
  44.4 39.7 all-gather.11
  86.0 28.2 all-gather.13
  116.1 23.8 all-gather.23
  141.7 23.4 all-gather.15
  167.0 60.3 all-gather.21
  229.2 174.0 all-gather.19
  405.2 89.8 all-gather.17
  874.2 38.4 reduce-scatter.28
  915.8 71.9 reduce-scatter.26
  991.4 51.2 reduce-scatter.18
  1238.8 51.1 reduce-scatter.16
  1351.8 51.0 reduce-scatter.12
  1406.3 76.4 reduce-scatter.14
  1486.3 126.1 reduce-scatter.24
  1615.9 126.0 reduce-scatter.22
  1745.5 126.0 reduce-scatter.20
  1875.0 33.3 reduce-scatter.30
  1914.1 184.0 all-reduce.25
where the time goes:
time: 2130 us; the launch traced here: 2120 us
  waiting for transfers between devices  812 us (38%)
  blocking collectives  614 us (29%)
  matrix products  316 us (15%)
  local copies, waits for them, and re-layouts  189 us (9%)
  other arithmetic  94.3 us (4%)
  starting transfers between devices  74.1 us (3%)
    ppermute x30, waiting for transfers between devices, passed_along(): return lax.ppermute(value, axis, pairs)  249 us
    psum x5, blocking collectives, statistics(): return lax.psum(partial_value, ('dp', 'fsdp'))  227 us
    psum x5, blocking collectives, norm_backward(): lax.psum((jnp.sum(upstream * inside, axis=0), jnp.sum(upstream * normed *...  206 us
    psum x1, waiting for transfers between devices, body(): lax.psum(shards[0].astype(jnp.bfloat16), 'dp').astype(jnp.float32)  170 us
    dot_general x42, matrix products, outer_dot(): lax.dot_general(first_op, second_op, (((1,), (1,)), ((), ())), preferred_...  144 us
    psum x1, blocking collectives, body(): crop_sums, crop_sizes = lax.psum((crop_sums, crop_sizes), 'fsdp')  128 us
    reduce_scatter x1, waiting for transfers between devices, body(): lax.psum_scatter(rate_weight_grads[1], 'fsdp', scatter_dimension=3, tiled...  127 us
    reduce_scatter x1, waiting for transfers between devices, body(): lax.psum_scatter(rate_weight_grads[0], 'fsdp', scatter_dimension=3, tiled...  127 us
  transfers between devices with their start and end apart: 53, of which 18 were waited for; matrix products, arithmetic and copies ran while one was open for 25% of the time, Pallas kernels for 0%

commit v1 on v0

--- a/solution.py
+++ b/solution.py
@@ -1,15 +1,573 @@
+import functools
 import jax
 import jax.numpy as jnp
 from jax import lax
+from jax.experimental import pallas as pl
+from jax.experimental.pallas import tpu as pltpu
 from jax.sharding import PartitionSpec as P
+
 
 CLASSES = 19
 CROPS_TILE = 4
 DILATION_SPAN = 4
 RATE = 12
 
-
 eps = 1e-05
+
+MESH = pl.DeviceIdType.MESH
+ANY = pl.BlockSpec(memory_space=pl.ANY)
+VM = pl.BlockSpec(memory_space=pltpu.VMEM)
+DMA = pltpu.SemaphoreType.DMA
+PAD = 144
+VLIM = 60 * 2**20
+
+
+def greet(fs, ds):
+    f = lax.axis_index("fsdp")
+    d = lax.axis_index("dp")
+    bar = pltpu.get_barrier_semaphore()
+    for k in fs:
+        pl.semaphore_signal(bar, inc=1, device_id=(d, f ^ k), device_id_type=MESH)
+    for k in ds:
+        pl.semaphore_signal(bar, inc=1, device_id=(d ^ k, f), device_id_type=MESH)
+    pl.semaphore_wait(bar, len(fs) + len(ds))
+    return f, d
+
+
+def remote(src, dst, ss, rs, d, f):
+    c = pltpu.make_async_remote_copy(
+        src_ref=src, dst_ref=dst, send_sem=ss, recv_sem=rs, device_id=(d, f), device_id_type=MESH
+    )
+    c.start()
+    return c
+
+
+def sum_kernel(x_ref, o_ref, b1, b2, s1, r1, s2, r2):
+    f, d = greet(range(1, 8), range(1, 4))
+    b1[f] = x_ref[...]
+    cps = [remote(x_ref, b1.at[f], s1.at[k], r1.at[k], d, f ^ k) for k in range(1, 8)]
+    for c in cps:
+        c.wait()
+    tot = b1[0]
+    for k in range(1, 8):
+        tot = tot + b1[k]
+    b2[d] = tot
+    cps = [remote(b2.at[d], b2.at[d], s2.at[k], r2.at[k], d ^ k, f) for k in range(1, 4)]
+    for c in cps:
+        c.wait()
+    tot = b2[0]
+    for k in range(1, 4):
+        tot = tot + b2[k]
+    o_ref[...] = tot
+
+
+def total_sum(rows, cid):
+    x = jnp.stack(rows)
+    R, C = x.shape
+    return pl.pallas_call(
+        sum_kernel,
+        out_shape=jax.ShapeDtypeStruct((R, C), jnp.float32),
+        in_specs=[VM],
+        out_specs=VM,
+        scratch_shapes=[
+            pltpu.VMEM((8, R, C), jnp.float32),
+            pltpu.VMEM((4, R, C), jnp.float32),
+            DMA((8,)),
+            DMA((8,)),
+            DMA((4,)),
+            DMA((4,)),
+        ],
+        compiler_params=pltpu.CompilerParams(collective_id=cid, has_side_effects=True),
+        name=f"total_sum_{cid}",
+    )(x)
+
+
+def spread_kernel(x_ref, o_ref, ss, rs, ls):
+    f, d = greet(range(1, 8), ())
+    w = o_ref.shape[2]
+    h = x_ref.shape[1]
+    dst = o_ref.at[:, pl.ds(pl.multiple_of(PAD + h * f, 16), h), :]
+
+    def part(g):
+        return x_ref.at[:, :, pl.ds(pl.multiple_of(g * w, 128), w)]
+
+    cps = [remote(part(f ^ k), dst, ss.at[k], rs.at[k], d, f ^ k) for k in (6, 7, 2, 3, 4, 5, 1)]
+    own = pltpu.make_async_copy(part(f), dst, ls)
+    own.start()
+    for c in cps:
+        c.wait()
+    own.wait()
+
+
+def spread_channels(x, cid):
+    q, h, C = x.shape
+    return pl.pallas_call(
+        spread_kernel,
+        out_shape=jax.ShapeDtypeStruct((q, 8 * h + 2 * PAD, C // 8), x.dtype),
+        in_specs=[VM],
+        out_specs=ANY,
+        scratch_shapes=[DMA((8,)), DMA((8,)), DMA(())],
+        compiler_params=pltpu.CompilerParams(collective_id=cid, has_side_effects=True, vmem_limit_bytes=VLIM),
+        name=f"spread_{cid}",
+    )(x)
+
+
+def collect_kernel(x_ref, o_ref, ss, rs, ls):
+    f, d = greet(range(1, 8), ())
+    w = x_ref.shape[2]
+    h = o_ref.shape[1]
+    dst = o_ref.at[:, :, pl.ds(pl.multiple_of(f * w, 128), w)]
+
+    def part(g):
+        return x_ref.at[:, pl.ds(pl.multiple_of(h * g, 16), h), :]
+
+    cps = [remote(part(f ^ k), dst, ss.at[k], rs.at[k], d, f ^ k) for k in (6, 7, 2, 3, 4, 5, 1)]
+    own = pltpu.make_async_copy(part(f), dst, ls)
+    own.start()
+    for c in cps:
+        c.wait()
+    own.wait()
+
+
+def collect_channels(x, cid):
+    q, t, w = x.shape
+    return pl.pallas_call(
+        collect_kernel,
+        out_shape=jax.ShapeDtypeStruct((q, t // 8, 8 * w), x.dtype),
+        in_specs=[VM],
+        out_specs=ANY,
+        scratch_shapes=[DMA((8,)), DMA((8,)), DMA(())],
+        compiler_params=pltpu.CompilerParams(collective_id=cid, has_side_effects=True, vmem_limit_bytes=VLIM),
+        name=f"collect_{cid}",
+    )(x)
+
+
+def gather_kernel(x_ref, o_ref, ss, rs, ps, pr, ls):
+    f, d = greet((1, 2, 4, 6), ())
+    h = x_ref.shape[1]
+
+    def slot(g):
+        return o_ref.at[:, pl.ds(pl.multiple_of(PAD + h * g, 16), h), :]
+
+    cps = [remote(x_ref, slot(f), ss.at[k], rs.at[k], d, f ^ (2 * k)) for k in (3, 1, 2)]
+    own = pltpu.make_async_copy(x_ref, slot(f), ls)
+    own.start()
+    pair = [remote(x_ref, slot(f), ps.at[0], pr.at[0], d, f ^ 1)]
+    for k, c in zip((3, 1, 2), cps):
+        c.wait_recv()
+        got = slot(f ^ (2 * k))
+        pair.append(remote(got, got, ps.at[k], pr.at[k], d, f ^ 1))
+    for c in cps:
+        c.wait_send()
+    for c in pair:
+        c.wait()
+    own.wait()
+
+
+def gather_rows(x, cid):
+    q, h, C = x.shape
+    return pl.pallas_call(
+        gather_kernel,
+        out_shape=jax.ShapeDtypeStruct((q, 8 * h + 2 * PAD, C), x.dtype),
+        in_specs=[VM],
+        out_specs=ANY,
+        scratch_shapes=[DMA((4,)), DMA((4,)), DMA((4,)), DMA((4,)), DMA(())],
+        compiler_params=pltpu.CompilerParams(collective_id=cid, has_side_effects=True, vmem_limit_bytes=VLIM),
+        name=f"gather_{cid}",
+    )(x)
+
+
+def scatter_kernel(x_ref, o_ref, near, mine, far, ps, pr, ss, rs):
+    f, d = greet((1, 2, 4, 6), ())
+    c0 = f & 1
+    pair = [
+        remote(x_ref.at[2 * k + 1 - c0], near.at[k], ps.at[k], pr.at[k], d, f ^ 1) for k in range(4)
+    ]
+    me = lax.shift_right_logical(f, 1)
+    cps = []
+    for c in pair:
+        c.wait()
+    for k in (3, 1, 2, 0):
+        g = me ^ k
+        val = x_ref[2 * g + c0].astype(jnp.float32) + near[g].astype(jnp.float32)
+        if k:
+            mine[k] = val.astype(mine.dtype)
+            cps.append(remote(mine.at[k], far.at[k], ss.at[k], rs.at[k], d, f ^ (2 * k)))
+        else:
+            o_ref[...] = val
+    for c in cps:
+        c.wait()
+    o_ref[...] += far[1].astype(jnp.float32) + far[2].astype(jnp.float32) + far[3].astype(jnp.float32)
+
+
+def scatter_sum(x, cid):
+    n, R, C = x.shape
+    return pl.pallas_call(
+        scatter_kernel,
+        out_shape=jax.ShapeDtypeStruct((R, C), jnp.float32),
+        in_specs=[VM],
+        out_specs=VM,
+        scratch_shapes=[
+            pltpu.VMEM((4, R, C), x.dtype),
+            pltpu.VMEM((4, R, C), x.dtype),
+            pltpu.VMEM((4, R, C), x.dtype),
+            DMA((4,)),
+            DMA((4,)),
+            DMA((4,)),
+            DMA((4,)),
+        ],
+        compiler_params=pltpu.CompilerParams(collective_id=cid, has_side_effects=True, vmem_limit_bytes=VLIM),
+        name=f"scatter_{cid}",
+    )(x)
+
+
+def nt_dot(a, b):
+    return lax.dot_general(a, b, (((1,), (1,)), ((), ())), preferred_element_type=jnp.float32)
+
+
+def nn_dot(a, b):
+    return lax.dot_general(a, b, (((1,), (0,)), ((), ())), preferred_element_type=jnp.float32)
+
+
+def tn_dot(a, b):
+    return lax.dot_general(a, b, (((0,), (0,)), ((), ())), preferred_element_type=jnp.float32)
+
+
+def span(shift, count):
+    return max(0, -shift), min(count, count - shift)
+
+
+def conv_forward_kernel(steps, y_ref, key_ref, k_ref, o_ref, acc):
+    Q = y_ref.shape[0]
+    h = o_ref.shape[2]
+    w = y_ref.shape[2]
+    out = k_ref.shape[1]
+    dest = pl.program_id(0)
+    base = PAD + h * dest
+    T = 8 * h
+    for b, s in enumerate(steps):
+        acc[...] = jnp.zeros_like(acc)
+        for i in (-1, 0, 1):
+            first = h * dest + 16 * s * i
+
+            @pl.when((first + h > 0) & (first < T))
+            def _():
+                at = pl.multiple_of(base + 16 * s * i, 16)
+                for j in (-1, 0, 1):
+                    lo, hi = span(s * j, Q)
+                    here = key_ref[lo:hi, pl.ds(pl.multiple_of(base, 16), h), :]
+                    there = key_ref[lo + s * j : hi + s * j, pl.ds(at, h), :]
+                    ok = (here == there) & (here > 0)
+                    ok = jnp.concatenate([ok] * (w // 128), axis=2)
+                    x = jnp.where(ok, y_ref[lo + s * j : hi + s * j, pl.ds(at, h), :], 0)
+                    x = x.reshape((hi - lo) * h, w)
+                    acc[lo * h : hi * h] += nt_dot(x, k_ref[9 * b + 3 * (i + 1) + j + 1])
+
+        o_ref[0, :, :, b * out : (b + 1) * out] = acc[...].reshape(Q, h, out).astype(o_ref.dtype)
+
+
+def conv_forward(y, key, k, steps):
+    Q, TT, w = y.shape
+    h = (TT - 2 * PAD) // 8
+    out = k.shape[1]
+    return pl.pallas_call(
+        functools.partial(conv_forward_kernel, steps),
+        out_shape=jax.ShapeDtypeStruct((8, Q, h, 3 * out), jnp.bfloat16),
+        grid=(8,),
+        in_specs=[VM, VM, VM],
+        out_specs=pl.BlockSpec((1, Q, h, 3 * out), lambda i: (i, 0, 0, 0)),
+        scratch_shapes=[pltpu.VMEM((Q * h, out), jnp.float32)],
+        compiler_params=pltpu.CompilerParams(vmem_limit_bytes=VLIM),
+        name="conv_forward",
+    )(y, key, k)
+
+
+def conv_data_kernel(steps, g_ref, key_ref, k_ref, o_ref, acc):
+    Q = g_ref.shape[0]
+    h = o_ref.shape[1]
+    w = o_ref.shape[2]
+    out = k_ref.shape[1]
+    dest = pl.program_id(0)
+    base = PAD + h * dest
+    T = 8 * h
+    acc[...] = jnp.zeros_like(acc)
+    for b, s in enumerate(steps):
+        for i in (-1, 0, 1):
+            first = h * dest - 16 * s * i
+
+            @pl.when((first + h > 0) & (first < T))
+            def _():
+                at = pl.multiple_of(base - 16 * s * i, 16)
+                for j in (-1, 0, 1):
+                    lo, hi = span(-s * j, Q)
+                    here = key_ref[lo:hi, pl.ds(pl.multiple_of(base, 16), h), :]
+                    there = key_ref[lo - s * j : hi - s * j, pl.ds(at, h), :]
+                    ok = (here == there) & (here > 0)
+                    ok = jnp.concatenate([ok] * (out // 128), axis=2)
+                    x = jnp.where(
+                        ok, g_ref[lo - s * j : hi - s * j, pl.ds(at, h), b * out : (b + 1) * out], 0
+                    )
+                    x = x.reshape((hi - lo) * h, out)
+                    acc[lo * h : hi * h] += nn_dot(x, k_ref[9 * b + 3 * (i + 1) + j + 1])
+
+    o_ref[...] = acc[...].reshape(Q, h, w).astype(o_ref.dtype)
+
+
+def conv_data(g, key, k, steps):
+    Q, TT, _ = g.shape
+    h = (TT - 2 * PAD) // 8
+    w = k.shape[2]
+    return pl.pallas_call(
+        functools.partial(conv_data_kernel, steps),
+        out_shape=jax.ShapeDtypeStruct((Q, 8 * h, w), jnp.bfloat16),
+        grid=(8,),
+        in_specs=[VM, VM, VM],
+        out_specs=pl.BlockSpec((Q, h, w), lambda i: (0, i, 0)),
+        scratch_shapes=[pltpu.VMEM((Q * h, w), jnp.float32)],
+        compiler_params=pltpu.CompilerParams(vmem_limit_bytes=VLIM),
+        name="conv_data",
+    )(g, key, k)
+
+
+def conv_weight_kernel(steps, y_ref, key_ref, g_ref, o_ref, x_ref):
+    Q = y_ref.shape[0]
+    w = y_ref.shape[2]
+    out = o_ref.shape[1]
+    TT = y_ref.shape[1]
+    T = TT - 2 * PAD
+    b = pl.program_id(0)
+    for n, s in enumerate(steps):
+
+        @pl.when(b == n)
+        def _():
+            for i in (-1, 0, 1):
+                r0, r1 = span(16 * s * i, T)
+                r0, r1 = r0 // 128 * 128, -(-r1 // 128) * 128
+                for j in (-1, 0, 1):
+                    lo, hi = span(s * j, Q)
+                    L = r1 - r0
+
+                    def one(q, _):
+                        here = key_ref[q, PAD + r0 : PAD + r1, :]
+                        a = PAD + r0 + 16 * s * i
+                        there = key_ref[q + s * j, a : a + L, :]
+                        ok = (here == there) & (here > 0)
+                        ok = jnp.concatenate([ok] * (w // 128), axis=1)
+                        x = jnp.where(ok, y_ref[q + s * j, a : a + L, :], 0)
+                        x_ref[pl.ds(pl.multiple_of((q - lo) * L, 128), L), :] = x
+                        return 0
+
+                    lax.fori_loop(lo, hi, one, 0)
+                    d = g_ref[lo:hi, PAD + r0 : PAD + r1, n * out : (n + 1) * out]
+                    d = d.reshape((hi - lo) * L, out)
+                    o_ref[3 * (i + 1) + j + 1] = tn_dot(d, x_ref[: (hi - lo) * L, :]).astype(o_ref.dtype)
+
+
+def conv_weight(y, key, g, steps, out):
+    Q, TT, w = y.shape
+    T = TT - 2 * PAD
+    return pl.pallas_call(
+        functools.partial(conv_weight_kernel, steps),
+        out_shape=jax.ShapeDtypeStruct((27, out, w), jnp.bfloat16),
+        grid=(3,),
+        in_specs=[VM, VM, VM],
+        out_specs=pl.BlockSpec((9, out, w), lambda i: (i, 0, 0)),
+        scratch_shapes=[pltpu.VMEM((Q * T, w), jnp.bfloat16)],
+        compiler_params=pltpu.CompilerParams(vmem_limit_bytes=VLIM),
+        name="conv_weight",
+    )(y, key, g)
+
+
+def norm_coeffs(totals, squares, count):
+    average = totals / count
+    return average, lax.rsqrt(squares / count - average * average + eps)
+
+
+def fast_body(
+    features, crop_ids, labels, w_reduce, gain_reduce, bias_reduce, w_dilated, gain_dilated, bias_dilated,
+    w_expand, gain_expand, bias_expand, w_point, gain_point, bias_point, w_rate, gain_rate, bias_rate,
+    w_rate_double, gain_rate_double, bias_rate_double, w_rate_triple, gain_rate_triple, bias_rate_triple,
+    w_pool, w_merge, gain_merge, bias_merge, w_classes,
+):
+    rows, cols, C = features.shape
+    Q = cols // 4
+    h = rows * 4
+    N = rows * cols
+    nf = lax.axis_size("fsdp")
+    W = gain_point.shape[0]
+    steps = (RATE // 4, 2 * RATE // 4, 3 * RATE // 4)
+    place = lax.axis_index("fsdp")
+
+    def perm(a):
+        a = a.reshape((rows, Q, 4) + a.shape[2:])
+        return jnp.swapaxes(a, 0, 1).reshape((N,) + a.shape[3:])
+
+    def unperm(a):
+        a = a.reshape((Q, rows, 4) + a.shape[1:])
+        return jnp.swapaxes(a, 0, 1).reshape((rows, cols) + a.shape[3:])
+
+    kt = jnp.concatenate([jnp.swapaxes(w.reshape(9, C, -1), 1, 2) for w in (w_rate, w_rate_double, w_rate_triple)])
+    full_reduce = lax.all_gather(w_reduce, "fsdp", axis=1, tiled=True)
+    full_dilated = lax.all_gather(w_dilated, "fsdp", axis=3, tiled=True)
+    full_expand = lax.all_gather(w_expand, "fsdp", axis=1, tiled=True)
+    kernel = lax.all_to_all(kt, "fsdp", split_axis=2, concat_axis=1, tiled=True)
+    full_point = lax.all_gather(w_point, "fsdp", axis=1, tiled=True)
+    full_merge = lax.all_gather(w_merge, "fsdp", axis=1, tiled=True)
+    full_pool = lax.all_gather(w_pool, "fsdp", axis=1, tiled=True)
+    full_classes = lax.all_gather(w_classes, "fsdp", axis=0, tiled=True)
+
+    x0 = perm(features)
+    local_crop = perm(crop_ids) - lax.axis_index("dp") * CROPS_TILE
+    in_crop = perm(crop_ids) >= 0
+    inside = in_crop.astype(jnp.float32)[:, None]
+    key_loc = jnp.where(in_crop, local_crop + 1, 0).astype(jnp.bfloat16)
+    key_all = lax.all_gather(key_loc.reshape(Q, h), "fsdp", axis=1, tiled=True)
+    key_pad = jnp.pad(key_all, ((0, 0), (PAD, PAD)))
+    key = jnp.broadcast_to(key_pad[:, :, None], key_pad.shape + (128,))
+
+    a_one = flat_dot(x0, full_reduce)
+    neck = a_one.shape[1]
+    st = total_sum(
+        [jnp.sum(a_one * inside, axis=0), jnp.sum(a_one * a_one * inside, axis=0), jnp.full((neck,), jnp.sum(inside))], 1
+    )
+    count = st[2, 0]
+    m_one, s_one = norm_coeffs(st[0], st[1], count)
+    n_one = (a_one - m_one) * s_one
+    p_one = n_one * gain_reduce + bias_reduce
+    h_one = jax.nn.silu(p_one).astype(jnp.bfloat16)
+
+    def halo(a):
+        a = a.reshape(Q, h, -1)
+        e = 4 * DILATION_SPAN
+        up = passed_along(a[:, h - e :], "fsdp", 1)
+        down = passed_along(a[:, :e], "fsdp", -1)
+        return jnp.concatenate([up, a, down], axis=1)
+
+    e = 4 * DILATION_SPAN
+    key_near = lax.dynamic_slice_in_dim(key_pad, PAD - e + h * place, h + 2 * e, axis=1)
+    key_here = key_near[:, e : e + h]
+
+    def taps(a):
+        a = jnp.pad(a, ((1, 1), (0, 0), (0, 0)))
+        kn = jnp.pad(key_near, ((1, 1), (0, 0)))
+        pieces = []
+        for i in range(3):
+            for j in range(3):
+                ok = (kn[j : j + Q, e * i : e * i + h] == key_here) & (key_here > 0)
+                pieces.append(jnp.where(ok[:, :, None], a[j : j + Q, e * i : e * i + h], 0).reshape(N, -1))
+        return pieces
+
+    x_taps = taps(halo(h_one))
+    a_two = sum(flat_dot(x_taps[t], full_dilated[t // 3, t % 3]) for t in range(9))
+    st = total_sum([jnp.sum(a_two * inside, axis=0), jnp.sum(a_two * a_two * inside, axis=0)], 2)
+    m_two, s_two = norm_coeffs(st[0], st[1], count)
+    n_two = (a_two - m_two) * s_two
+    p_two = n_two * gain_dilated + bias_dilated
+    h_two = jax.nn.silu(p_two).astype(jnp.bfloat16)
+    a_three = flat_dot(h_two, full_expand)
+    st = total_sum([jnp.sum(a_three * inside, axis=0), jnp.sum(a_three * a_three * inside, axis=0)], 3)
+    m_three, s_three = norm_coeffs(st[0], st[1], count)
+    n_three = (a_three - m_three) * s_three
+    p_three = n_three * gain_expand + bias_expand + x0
+    y = jax.nn.silu(p_three).astype(jnp.bfloat16)
+
+    y_own = spread_channels(y.reshape(Q, h, C), 4)
+    part = conv_forward(y_own, key, kernel, steps)
+    a_rates = scatter_sum(part.reshape(nf, N, 3 * W), 5)
+    a_point = flat_dot(y, full_point)
+    a_br = jnp.concatenate([a_point, a_rates], axis=1)
+    member = local_crop[:, None] == jnp.arange(CROPS_TILE)[None, :]
+    member = (member & in_crop[:, None]).astype(jnp.bfloat16)
+    crop_sums = inner_dot(member, y)
+    crop_sizes = jnp.sum(member.astype(jnp.float32), axis=0)
+    crop_sums, crop_sizes = lax.psum((crop_sums, crop_sizes), "fsdp")
+    st = total_sum([jnp.sum(a_br * inside, axis=0), jnp.sum(a_br * a_br * inside, axis=0)], 6)
+    m_br, s_br = norm_coeffs(st[0], st[1], count)
+    g_br = jnp.concatenate([gain_point, gain_rate, gain_rate_double, gain_rate_triple])
+    b_br = jnp.concatenate([bias_point, bias_rate, bias_rate_double, bias_rate_triple])
+    n_br = (a_br - m_br) * s_br
+    p_br = n_br * g_br + b_br
+    u_br = jax.nn.silu(p_br).astype(jnp.bfloat16)
+    pooled = (crop_sums / crop_sizes[:, None]).astype(jnp.bfloat16)
+    pool_act = flat_dot(pooled, full_pool)
+    pool_low = jax.nn.silu(pool_act).astype(jnp.bfloat16)
+    u_pool = flat_dot(member, pool_low).astype(jnp.bfloat16)
+    joined = jnp.concatenate([u_br, u_pool], axis=1)
+    a_merge = flat_dot(joined, full_merge)
+    st = total_sum([jnp.sum(a_merge * inside, axis=0), jnp.sum(a_merge * a_merge * inside, axis=0)], 7)
+    m_merge, s_merge = norm_coeffs(st[0], st[1], count)
+    n_merge = (a_merge - m_merge) * s_merge
+    p_merge = n_merge * gain_merge + bias_merge
+    merged = jax.nn.silu(p_merge).astype(jnp.bfloat16)
+    logits = flat_dot(merged, full_classes)
+    class_logits = unperm(logits.astype(jnp.bfloat16))
+
+    probability = jax.nn.softmax(logits, axis=1)
+    targets = (perm(labels)[:, None] == jnp.arange(CLASSES)[None, :]).astype(jnp.float32)
+    d_logits = (inside * (probability - targets) / count).astype(jnp.bfloat16)
+    grad_classes = inner_dot(merged, d_logits)
+
+    def back(up, n, s, gain, cid):
+        st = total_sum([jnp.sum(up * inside, axis=0), jnp.sum(up * n * inside, axis=0)], cid)
+        d = inside * gain * s * (up - st[0] / count - n * st[1] / count)
+        return d.astype(jnp.bfloat16), st[1], st[0]
+
+    d_merge, gg_merge, gb_merge = back(outer_dot(d_logits, full_classes) * slope(p_merge), n_merge, s_merge, gain_merge, 8)
+    grad_merge = inner_dot(joined, d_merge)
+    d_joined = outer_dot(d_merge, full_merge)
+    d_br, gg_br, gb_br = back(d_joined[:, : 4 * W] * slope(p_br), n_br, s_br, g_br, 9)
+    crop_grad = lax.dot_general(
+        member.astype(jnp.float32), d_joined[:, 4 * W :], (((0,), (0,)), ((), ())),
+        precision=lax.Precision.HIGHEST, preferred_element_type=jnp.float32,
+    )
+    crop_grad = lax.psum(crop_grad, "fsdp")
+    d_pool = (crop_grad * slope(pool_act)).astype(jnp.bfloat16)
+    owned = (jnp.arange(CROPS_TILE) % nf == place).astype(jnp.float32)[:, None]
+    grad_pool = inner_dot(pooled, (d_pool * owned).astype(jnp.bfloat16))
+    grad_pooled = outer_dot(d_pool, full_pool) / crop_sizes[:, None]
+    g_all = gather_rows(d_br[:, W:].reshape(Q, h, 3 * W), 10)
+    d_y_own = conv_data(g_all, key, kernel, steps)
+    d_y = collect_channels(d_y_own, 11).reshape(N, C).astype(jnp.float32)
+    grad_k = conv_weight(y_own, key, g_all, steps, W)
+    grad_k = lax.all_to_all(grad_k, "fsdp", split_axis=1, concat_axis=2, tiled=True)
+    grad_k = lax.psum(grad_k, "dp").astype(jnp.float32)
+    grad_point = inner_dot(y, d_br[:, :W])
+    d_y = d_y + outer_dot(d_br[:, :W], full_point)
+    d_y = d_y + lax.dot_general(
+        member.astype(jnp.float32), grad_pooled, (((1,), (0,)), ((), ())),
+        precision=lax.Precision.HIGHEST, preferred_element_type=jnp.float32,
+    )
+    d_p3 = d_y * slope(p_three)
+    d_three, gg_expand, gb_expand = back(d_p3, n_three, s_three, gain_expand, 12)
+    grad_expand = inner_dot(h_two, d_three)
+    d_h2 = outer_dot(d_three, full_expand)
+    d_two, gg_dilated, gb_dilated = back(d_h2 * slope(p_two), n_two, s_two, gain_dilated, 13)
+    grad_dilated = jnp.stack([inner_dot(x_taps[t], d_two) for t in range(9)])
+    d_taps = taps(halo(d_two))
+    d_h1 = sum(outer_dot(d_taps[8 - t], full_dilated[t // 3, t % 3]) for t in range(9))
+    d_one, gg_reduce, gb_reduce = back(d_h1 * slope(p_one), n_one, s_one, gain_reduce, 14)
+    grad_reduce = inner_dot(x0, d_one)
+    grad_features = unperm(d_p3 + outer_dot(d_one, full_reduce))
+
+    def shard(g, dim):
+        g = lax.psum_scatter(g, "fsdp", scatter_dimension=dim, tiled=True)
+        return lax.psum(g.astype(jnp.bfloat16), "dp").astype(jnp.float32)
+
+    grad_k = jnp.swapaxes(grad_k.reshape(3, 3, 3, -1, C), 3, 4)
+    return (
+        class_logits,
+        grad_features,
+        shard(grad_reduce, 1), gg_reduce, gb_reduce,
+        shard(grad_dilated, 2).reshape(3, 3, neck, -1), gg_dilated, gb_dilated,
+        shard(grad_expand, 1), gg_expand, gb_expand,
+        shard(grad_point, 1), gg_br[:W], gb_br[:W],
+        grad_k[0], gg_br[W : 2 * W], gb_br[W : 2 * W],
+        grad_k[1], gg_br[2 * W : 3 * W], gb_br[2 * W : 3 * W],
+        grad_k[2], gg_br[3 * W :], gb_br[3 * W :],
+        shard(grad_pool, 1),
+        shard(grad_merge, 1), gg_merge, gb_merge,
+        shard(grad_classes, 0),
+    )
 
 
 def passed_along(value, axis, by):
@@ -519,8 +1077,10 @@
 
 
 def solution(mesh):
+    tiled = mesh.shape["fsdp"] == 8 and mesh.shape["dp"] == 4
+
     return jax.shard_map(
-        body,
+        fast_body if tiled else body,
         mesh=mesh,
         in_specs=(
             P(("dp", "fsdp"), None, None),

time: 2130 us -> 1160 us (0.54)
  waiting for transfers between devices: 812 us -> 297 us
  blocking collectives: 614 us -> 122 us
  Pallas kernels: 0 us -> 354 us
  matrix products: 316 us -> 89.4 us
  starting transfers between devices: 74.1 us -> 16.6 us
    psum x13 -> x3, blocking collectives: 586 us -> 48.5 us  [the longest x1 23.3 us: fast_body(): crop_sums, crop_sizes = lax.psum((crop_sums, crop_sizes), 'fsdp')]
    pallas_call x0 -> x17, Pallas kernels: none -> 354 us  [the longest x10 111 us: total_sum(): pl.pallas_call(sum_kernel, out_shape=jax.ShapeDtypeStruct((R, C), jnp.flo...]
    reduce_scatter x9 -> x6, waiting for transfers between devices: 349 us -> 23.6 us  [shard(): g = lax.psum_scatter(g, 'fsdp', scatter_dimension=dim, tiled=True)]
    ppermute x30 -> x4, waiting for transfers between devices: 249 us -> 3.38 us  [passed_along(): return lax.ppermute(value, axis, pairs)]
    dot_general x42 -> x15, matrix products: 144 us -> 25.2 us  [outer_dot(): lax.dot_general(first_op, second_op, (((1,), (1,)), ((), ())), preferred_...]
    all_to_all x0 -> x2, waiting for transfers between devices: none -> 82.6 us  [the longest x1 82.6 us: fast_body(): lax.all_to_all(grad_k, 'fsdp', split_axis=1, concat_axis=2, tiled=True)]
    dot_general x42 -> x15, matrix products: 93.2 us -> 30.8 us  [inner_dot(): lax.dot_general(first_op, second_op, (((0,), (0,)), ((), ())), preferred_...]
    ppermute x30 -> x4, starting transfers between devices: 66.7 us -> 5.89 us  [passed_along(): return lax.ppermute(value, axis, pairs)]
  transfers between devices with their start and end apart: 53 -> 19, of which waited for: 18 -> 5; matrix products, arithmetic and copies ran while one was open for 25% -> 26% of each run, Pallas kernels for 0% -> 28%
where the time goes in v1:
time: 1160 us; the launch traced here: 1150 us
  Pallas kernels  354 us (31%)
  waiting for transfers between devices  297 us (26%)
  local copies, waits for them, and re-layouts  175 us (15%)
  blocking collectives  122 us (11%)
  matrix products  89.4 us (8%)
  other arithmetic  82.9 us (7%)
  starting transfers between devices  16.6 us (1%)
  between operations  15.7 us (1%)
    psum x1, waiting for transfers between devices, shard(): return lax.psum(g.astype(jnp.bfloat16), 'dp').astype(jnp.float32)  153 us
    pallas_call x10, Pallas kernels, total_sum(): pl.pallas_call(sum_kernel, out_shape=jax.ShapeDtypeStruct((R, C), jnp.flo...  111 us
    all_to_all x1, waiting for transfers between devices, fast_body(): lax.all_to_all(grad_k, 'fsdp', split_axis=1, concat_axis=2, tiled=True)  82.6 us
    all_gather x1, blocking collectives, fast_body(): key_all = lax.all_gather(key_loc.reshape(Q, h), 'fsdp', axis=1, tiled=True)  48.5 us
    pallas_call x1, Pallas kernels, scatter_sum(): pl.pallas_call(scatter_kernel, out_shape=jax.ShapeDtypeStruct((R, C), jnp...  47.3 us
    unnamed x218, local copies, waits for them, and re-layouts  44.5 us
    pallas_call x1, Pallas kernels, conv_weight(): pl.pallas_call(functools.partial(conv_weight_kernel, steps), out_shape=ja...  43.5 us
    pallas_call x1, Pallas kernels, gather_rows(): pl.pallas_call(gather_kernel, out_shape=jax.ShapeDtypeStruct((q, 8 * h +...  43.2 us
  transfers between devices with their start and end apart: 19, of which 5 were waited for; matrix products, arithmetic and copies ran while one was open for 26% of the time, Pallas kernels for 28%

profile of v1, /device:TPU:0, one launch (start us, length us, event | category | flops | bytes accessed | tf_op | source)
XLA Modules:
  0.0 1152.5 jit_solution(9195984209907166705)
XLA Ops:
  12.2 23.4 %copy.164 = bf16[27,32,2048]{1,0,2:T(8,128)(2,1)} copy(bf16[27,32,2048]{2,1,0:T(8,128)(2,1)S(1)} %pad_maximum_fusion) | data formatting | bytes 7077888 | tf_op jit(solution)/shard_map/concatenate | solution.py:409
  35.6 14.5 %reshape.298 = bf16[8,2,110592]{2,1,0:T(2,128)(2,1)} reshape(bf16[2048,27,32]{2,1,0:T(8,128)(2,1)} %bitcast.273) | data formatting | bytes 7077888
  64.0 48.5 %all-gather = bf16[8,32,16]{1,2,0:T(8,128)(2,1)S(1)} all-gather(bf16[1,32,16]{1,2,0:T(8,128)(2,1)} %bitcast.358), channel_id=1, replica_groups=mesh['dp'=4,'fsdp'=8] {'fsdp'}, dimensions={0}, use_global_device_ids=true | all-gather | bytes 9216 | tf_op jit(solution)/shard_map/all_gather | solution.py:424
  133.6 12.3 %total_sum_1.1 = f32[3,512]{1,0:T(4,128)} custom-call(f32[3,512]{1,0:T(4,128)} %maximum_maximum_fusion.x_ref), custom_call_target="tpu_custom_call" | custom-call | tf_op jit(solution)/shard_map/total_sum_1/pallas_call | solution.py:67
  166.7 12.2 %all-gather.1 = bf16[8,32,19]{1,2,0:T(8,128)(2,1)S(1)} all-gather(bf16[1,32,19]{1,2,0:T(8,128)(2,1)} %bitcast.389), channel_id=1, replica_groups=mesh['dp'=4,'fsdp'=8] {'fsdp'}, dimensions={0}, use_global_device_ids=true | all-gather | bytes 10944 | tf_op jit(solution)/shard_map/all_gather | solution.py:417
  182.4 12.9 %all_gather.30 = bf16[1280,256]{0,1:T(8,128)(2,1)} all-gather(bf16[1280,32]{0,1:T(8,128)(2,1)} %param.54), channel_id=1, replica_groups=mesh['dp'=4,'fsdp'=8] {'fsdp'}, dimensions={1}, use_global_device_ids=true | all-gather | bytes 737280 | tf_op jit(solution)/shard_map/all_gather | solution.py:415
  195.2 14.1 %reshape.299 = bf16[2048,27,32]{2,1,0:T(8,128)(2,1)} reshape(bf16[8,2,110592]{2,1,0:T(2,128)(2,1)S(1)} %all-to-all-done) | data formatting | bytes 7077888
  209.4 19.6 %copy.166 = bf16[27,8,32,256]{3,2,1,0:T(8,128)(2,1)} copy(bf16[27,8,32,256]{2,0,3,1:T(8,128)(2,1)} %bitcast.274) | data formatting | bytes 7077888 | tf_op jit(solution)/shard_map/all_to_all | solution.py:413
  243.0 10.1 total_sum_2.1
  260.9 11.0 total_sum_3.1
  278.4 28.0 %spread_4.1.y_ref = bf16[16,544,256]{2,1,0:T(8,128)(2,1)} custom-call(bf16[16,32,2048]{2,1,0:T(8,128)(2,1)} %bitcast.275), custom_call_target="tpu_custom_call" | custom-call | tf_op jit(solution)/shard_map/spread_4/pallas_call | solution.py:104
  308.7 26.9 %conv_forward.1 = bf16[8,16,32,768]{3,2,1,0:T(8,128)(2,1)} custom-call(bf16[16,544,256]{2,1,0:T(8,128)(2,1)} %spread_4.1.y_ref, bf16[16,544,128]{2,1,0:T(8,128)(2,1)} %broadcast_in_dim.183.key_ref, bf16[27,256,256]{2,1,0:T(8,128)(2,1)} %bitcast.276), custom_call_target="tpu_custom_call" | custom-call | tf_op jit(solution)/shard_map/conv_forward/pallas_call | solution.py:273
  335.6 47.3 %scatter_5.1 = f32[512,768]{1,0:T(8,128)} custom-call(bf16[8,512,768]{2,1,0:T(8,128)(2,1)} %bitcast.278), custom_call_target="tpu_custom_call" | custom-call | tf_op jit(solution)/shard_map/scatter_5/pallas_call | solution.py:205
  383.4 23.3 %all-reduce.4 = (f32[4,2048]{1,0:T(4,128)S(1)}, f32[4]{0:T(128)S(1)}) all-reduce(f32[4,2048]{1,0:T(4,128)S(1)} %fusion.45, f32[4]{0:T(128)S(1)} %copy-done.93), channel_id=1, replica_groups=mesh['dp'=4,'fsdp'=8] {'fsdp'}, use_global_device_ids=true, to_apply=%region_9.10 | all-reduce | flops 8196 | bytes 65568 | tf_op jit(solution)/shard_map/psum | solution.py:483
  411.9 10.3 total_sum_6.1
  427.8 10.1 total_sum_7.1
  444.9 10.0 total_sum_8.1
  467.0 10.4 total_sum_9.1
  487.4 43.2 %gather_10.1.g_ref = bf16[16,544,768]{2,1,0:T(8,128)(2,1)} custom-call(bf16[16,32,768]{2,1,0:T(8,128)(2,1)} %bitcast.301), custom_call_target="tpu_custom_call" | custom-call | tf_op jit(solution)/shard_map/gather_10/pallas_call | solution.py:169
  530.7 26.9 %conv_data.1.x_ref = bf16[16,256,256]{2,1,0:T(8,128)(2,1)} custom-call(bf16[16,544,768]{2,1,0:T(8,128)(2,1)} %gather_10.1.g_ref, bf16[16,544,128]{2,1,0:T(8,128)(2,1)} %broadcast_in_dim.183.key_ref, bf16[27,256,256]{2,1,0:T(8,128)(2,1)} %bitcast.277), custom_call_target="tpu_custom_call" | custom-call | tf_op jit(solution)/shard_map/conv_data/pallas_call | solution.py:320
  557.6 27.1 %collect_11.1 = bf16[16,32,2048]{2,1,0:T(8,128)(2,1)} custom-call(bf16[16,256,256]{2,1,0:T(8,128)(2,1)} %conv_data.1.x_ref), custom_call_target="tpu_custom_call" | custom-call | tf_op jit(solution)/shard_map/collect_11/pallas_call | solution.py:134
  586.1 13.2 %psum.79 = f32[4,256]{1,0:T(4,128)S(1)} all-reduce(f32[4,256]{1,0:T(4,128)S(1)} %fusion.18), channel_id=1, replica_groups=mesh['dp'=4,'fsdp'=8] {'fsdp'}, use_global_device_ids=true, to_apply=%region_20.21 | all-reduce | flops 1024 | bytes 8192 | tf_op jit(solution)/shard_map/psum | solution.py:523
  612.3 10.8 total_sum_12.1
  641.1 10.4 total_sum_13.1
  671.3 15.7 %total_sum_14.1 = f32[2,512]{1,0:T(2,128)} custom-call(f32[2,512]{1,0:T(2,128)} %pad_maximum_fusion.17.x_ref), custom_call_target="tpu_custom_call" | custom-call | tf_op jit(solution)/shard_map/total_sum_14/pallas_call | solution.py:67
  709.3 17.1 %copy.177 = f32[9,512,512]{1,0,2:T(8,128)} copy(f32[9,512,512]{2,1,0:T(8,128)} %fusion.3) | data formatting | bytes 18874368 | tf_op jit(solution)/shard_map/stack | solution.py:545
  726.4 43.5 %conv_weight.1 = bf16[27,256,256]{2,1,0:T(8,128)(2,1)} custom-call(bf16[16,544,256]{2,1,0:T(8,128)(2,1)} %spread_4.1.y_ref, bf16[16,544,128]{2,1,0:T(8,128)(2,1)} %broadcast_in_dim.183.key_ref, bf16[16,544,768]{2,1,0:T(8,128)(2,1)} %gather_10.1.g_ref), custom_call_target="tpu_custom_call" | custom-call | tf_op jit(solution)/shard_map/conv_weight/pallas_call | solution.py:369
  785.0 82.6 %all-to-all-done.1 = bf16[27,256,256]{2,0,1:T(8,128)(2,1)} async-done(((bf16[27,256,256]{2,0,1:T(8,128)(2,1)}), bf16[27,256,256]{2,0,1:T(8,128)(2,1)}, u32[]{:S(2)}, u32[]{:S(2)}) %all-to-all-start.1) | async-done | bytes 3538976 | tf_op jit(solution)/shard_map/all_to_all | solution.py:532
  882.3 23.6 %reduce-scatter.12.cloned.1.call-done = f32[9,512,64]{1,0,2:T(8,128)} async-done(((f32[9,512,512]{1,0,2:T(8,128)}), f32[9,512,64]{1,0,2:T(8,128)}) %reduce-scatter.12.cloned.1.call-update) | async-done | bytes 1179664 | tf_op jit(solution)/shard_map/reduce_scatter | solution.py:553
  911.3 31.5 %reduce-scatter.22.cloned.1.call-done = f32[32,19]{1,0:T(8,128)} async-done(((f32[256,19]{1,0:T(8,128)}), f32[32,19]{1,0:T(8,128)}) %reduce-scatter.22.cloned.1.call-update) | async-done | bytes 2448
  943.5 11.9 %psum.87 = bf16[32,19]{0,1:T(8,128)(2,1)S(1)} all-reduce(bf16[32,19]{0,1:T(8,128)(2,1)S(1)} %copy.187), channel_id=1, replica_groups=mesh['dp'=4,'fsdp'=8] {'dp'}, use_global_device_ids=true, to_apply=%region_41.42 | all-reduce | flops 608 | bytes 2432 | tf_op jit(solution)/shard_map/psum | solution.py:554
  978.2 152.7 %all-reduce.8.cloned.1.call-done = (bf16[2048,64]{0,1:T(8,128)(2,1)}, bf16[3,3,512,64]{2,3,1,0:T(8,128)(2,1)}, bf16[512,256]{1,0:T(8,128)(2,1)}, bf16[2048,32]{0...) async-done(((bf16[2048,64]{0,1:T(8,128)(2,1)}, bf16[3,3,512,64]{2,3,1,0:T(8,128)(2,1)}, ...) | async-done | bytes 4997136 | tf_op jit(solution)/shard_map/psum | solution.py:554
  (406 shorter events, 281.6 us)
Async XLA Ops:
  7.2 121.2 %all-gather.8.cloned.1.call-start = ((), (), s32[]{:S(2)}) async-start(), calls=%async_computation.9 | async-start | bytes 2359296 | tf_op jit(solution)/shard_map/all_gather | solution.py:410
  7.9 225.6 %all-gather.10.cloned.1.call-start = ((), (), s32[]{:S(2)}) async-start(), calls=%async_computation.10 | async-start | bytes 5308416 | tf_op jit(solution)/shard_map/all_gather | solution.py:411
  8.7 245.9 %all-gather.12.cloned.1.call-start = ((), (), s32[]{:S(2)}) async-start(), calls=%async_computation.11 | async-start | bytes 2359296 | tf_op jit(solution)/shard_map/all_gather | solution.py:412
  9.4 397.3 %all-gather.16.cloned.1.call-start = ((), (), s32[]{:S(2)}) async-start(), calls=%async_computation.13 | async-start | bytes 1179648 | tf_op jit(solution)/shard_map/all_gather | solution.py:416
  50.1 145.2 %all-to-all-start = ((bf16[8,2,110592]{2,1,0:T(2,128)(2,1)}), bf16[8,2,110592]{2,1,0:T(2,128)(2,1)S(1)}, u32[]{:S(2)}, u32[]{:S(2)}) async-start(bf16[8,2,110592]{2,1,0:T(2,128)(2,1)} %reshape.298), calls=%async_computation | async-start | bytes 7077888 | tf_op jit(solution)/shard_map/all_to_all | solution.py:413
  55.5 353.2 %all-gather.14.cloned.1.call-start = ((), (), s32[]{:S(2)}) async-start(), calls=%async_computation.12 | async-start | bytes 1179648 | tf_op jit(solution)/shard_map/all_gather | solution.py:414
  56.1 727.4 %reduce-scatter.20.cloned.1.call-start = ((), (), s32[]{:S(2)}) async-start(), calls=%async_computation.19 | async-start | bytes 1474560 | tf_op jit(solution)/shard_map/reduce_scatter | solution.py:553
  58.4 63.9 %copy-start.74 = (pred[512]{0:T(512)(128)(4,1)}, pred[512]{0:T(512)(128)(4,1)S(1)}, u32[]{:S(2)}) copy-start(pred[512]{0:T(512)(128)(4,1)S(1)} %ge.36) | copy-start | bytes 1540
  151.7 77.3 %collective-permute-start = (bf16[16,16,512]{2,1,0:T(8,128)(2,1)}, bf16[16,16,512]{2,1,0:T(8,128)(2,1)}, u32[]{:S(2)}, u32[]{:S(2)}) collective-permute-start(bf16[16,16,512]{2,1,0:T(8,128)(2,1)} %get-tuple-element.233), channel_id=1, source_target_pairs={{0,1},{1,2},{2,3},{3,4},{4,5},{5,6},{6,7},{8,9},{9,10},{10,11},{11... | collective-permute-start | bytes 786440 | tf_op jit(solution)/shard_map/ppermute | solution.py:576
  153.7 75.3 %collective-permute-start.1 = (bf16[16,16,512]{2,1,0:T(8,128)(2,1)}, bf16[16,16,512]{2,1,0:T(8,128)(2,1)}, u32[]{:S(2)}, u32[]{:S(2)}) collective-permute-start(bf16[16,16,512]{2,1,0:T(8,128)(2,1)} %get-tuple-element.234), channel_id=1, source_target_pairs={{1,0},{2,1},{3,2},{4,3},{5,4},{6,5},{7,6},{9,8},{10,9},{11,10},{12... | collective-permute-start | bytes 786440 | tf_op jit(solution)/shard_map/ppermute | solution.py:576
  162.3 246.1 %copy-start.41 = (s32[512]{0:T(512)}, s32[512]{0:T(512)S(1)}, u32[]{:S(2)}) copy-start(s32[512]{0:T(512)S(1)} %sub.207) | copy-start | bytes 6148
  278.4 28.0 %copy-start.39 = (bf16[16,544]{1,0:T(8,128)(2,1)S(1)}, bf16[16,544]{1,0:T(8,128)(2,1)}, u32[]{:S(2)}) copy-start(bf16[16,544]{1,0:T(8,128)(2,1)} %pad.16) | copy-start | bytes 52228
  335.6 47.3 %copy-start = (bf16[512,2048]{1,0:T(8,128)(2,1)S(1)}, bf16[512,2048]{1,0:T(8,128)(2,1)}, u32[]{:S(2)}) copy-start(bf16[512,2048]{1,0:T(8,128)(2,1)} %multiply_convert_fusion.1) | copy-start | bytes 6291460
  335.6 47.3 %copy-start.75 = (pred[512]{0:T(512)(128)(4,1)S(1)}, pred[512]{0:T(512)(128)(4,1)}, u32[]{:S(2)}) copy-start(pred[512]{0:T(512)(128)(4,1)} %copy-done.74) | copy-start | bytes 1540
  335.6 47.7 %copy-start.93 = (f32[4]{0:T(128)S(1)}, f32[4]{0:T(128)}, u32[]{:S(2)}) copy-start(f32[4]{0:T(128)} %convert_reduce_fusion) | copy-start | bytes 52
  460.8 414.7 %reduce-scatter.16.cloned.1.call-start = ((), (), s32[]{:S(2)}) async-start(), calls=%async_computation.17 | async-start | bytes 2359296 | tf_op jit(solution)/shard_map/reduce_scatter | solution.py:553
  485.3 391.8 %reduce-scatter.18.cloned.1.call-start = ((), (), s32[]{:S(2)}) async-start(), calls=%async_computation.18 | async-start | bytes 2359296 | tf_op jit(solution)/shard_map/reduce_scatter | solution.py:553
  557.6 27.1 %copy-start.42 = (s32[512]{0:T(512)S(1)}, s32[512]{0:T(512)}, u32[]{:S(2)}) copy-start(s32[512]{0:T(512)} %copy-done.41) | copy-start | bytes 6148
  557.6 27.1 %copy-start.76 = (pred[512]{0:T(512)(128)(4,1)S(1)}, pred[512]{0:T(512)(128)(4,1)}, u32[]{:S(2)}) copy-start(pred[512]{0:T(512)(128)(4,1)} %copy-done.74) | copy-start | bytes 1540
  557.6 41.7 %copy-start.86 = (f32[4]{0:T(128)S(1)}, f32[4]{0:T(128)}, u32[]{:S(2)}) copy-start(f32[4]{0:T(128)} %copy-done.85) | copy-start | bytes 52
  601.1 277.6 %reduce-scatter.14.cloned.1.call-start = ((), (), s32[]{:S(2)}) async-start(), calls=%async_computation.16 | async-start | bytes 4718592 | tf_op jit(solution)/shard_map/reduce_scatter | solution.py:553
  635.5 245.0 %reduce-scatter.10.cloned.1.call-start = ((), (), s32[]{:S(2)}) async-start(), calls=%async_computation.14 | async-start | bytes 4718592 | tf_op jit(solution)/shard_map/reduce_scatter | solution.py:553
  655.9 2.6 collective-permute-start.2
  657.2 4.7 collective-permute-start.3
  695.1 210.9 %reduce-scatter.12.cloned.1.call-start = ((), (), s32[]{:S(2)}) async-start(), calls=%async_computation.15 | async-start | bytes 18874368 | tf_op jit(solution)/shard_map/reduce_scatter | solution.py:553
  776.9 90.7 %all-to-all-start.1 = ((bf16[27,256,256]{2,0,1:T(8,128)(2,1)}), bf16[27,256,256]{2,0,1:T(8,128)(2,1)}, u32[]{:S(2)}, u32[]{:S(2)}) async-start(bf16[27,256,256]{2,0,1:T(8,128)(2,1)} %copy.179), calls=%async_computation.5 | async-start | bytes 8388608 | tf_op jit(solution)/shard_map/all_to_all | solution.py:532
  781.7 161.0 %reduce-scatter.22.cloned.1.call-start = ((), (), s32[]{:S(2)}) async-start(), calls=%async_computation.20 | async-start | bytes 147456
  783.4 347.6 %all-reduce.8.cloned.1.call-start = ((), (), s32[]{:S(2)}) async-start(), calls=%async_computation.21 | async-start | bytes 9994240 | tf_op jit(solution)/shard_map/psum | solution.py:554
  909.0 47.1 %copy-start.11 = (f32[512,512]{1,0:T(8,128)S(1)}, f32[512,512]{1,0:T(8,128)}, u32[]{:S(2)}) copy-start(f32[512,512]{1,0:T(8,128)} %get-tuple-element.268) | copy-start | bytes 3145732
  909.0 47.1 %copy-start.32 = (f32[512,512]{1,0:T(8,128)S(1)}, f32[512,512]{1,0:T(8,128)}, u32[]{:S(2)}) copy-start(f32[512,512]{1,0:T(8,128)} %get-tuple-element.277) | copy-start | bytes 3145732
  909.0 47.1 %copy-start.67 = (f32[1,512]{1,0:T(1,128)S(1)}, f32[1,512]{1,0:T(1,128)}, u32[]{:S(2)}) copy-start(f32[1,512]{1,0:T(1,128)} %copy-done.66) | copy-start | bytes 6148
  909.0 47.1 %copy-start.69 = (f32[1,512]{1,0:T(1,128)S(1)}, f32[1,512]{1,0:T(1,128)}, u32[]{:S(2)}) copy-start(f32[1,512]{1,0:T(1,128)} %copy-done.68) | copy-start | bytes 6148
  (92 other events, 642.2 us)
Sparse Core Ops, SparseCore 0:
  9.9 30.5 all-gather.7
  42.5 61.6 all-gather.9
  106.0 36.2 all-gather.11
  144.1 24.3 all-gather.15
  170.2 24.5 all-gather.13
  460.9 52.0 reduce-scatter.19
  516.3 40.9 reduce-scatter.15
  601.2 39.5 reduce-scatter.17
  644.2 51.4 reduce-scatter.13
  699.8 51.3 reduce-scatter.9
  754.8 151.1 reduce-scatter.11
  909.4 33.3 reduce-scatter.21
  947.7 183.2 all-reduce.7

commit v2 on v1

--- a/solution.py
+++ b/solution.py
@@ -378,6 +378,746 @@
     )(y, key, g)
 
 
+class Gather:
+    def __init__(self, src, slot, sems, d, f):
+        self.src, self.slot, self.sems, self.d, self.f = src, slot, sems, d, f
+
+    def start(self):
+        far_s, far_r, near_s, near_r, local = self.sems
+        d, f = self.d, self.f
+        mine = self.slot(f)
+        self.far = {k: remote(self.src, mine, far_s.at[k], far_r.at[k], d, f ^ (2 * k)) for k in (3, 1, 2)}
+        self.near = [remote(self.src, mine, near_s.at[0], near_r.at[0], d, f ^ 1)]
+        self.own = pltpu.make_async_copy(self.src, mine, local)
+        self.own.start()
+
+    def forward(self):
+        far_s, far_r, near_s, near_r, local = self.sems
+        for k in (1, 2, 3):
+            self.far[k].wait_recv()
+            got = self.slot(self.f ^ (2 * k))
+            self.near.append(remote(got, got, near_s.at[k], near_r.at[k], self.d, self.f ^ 1))
+
+    def arrive(self):
+        self.own.wait()
+        for c in self.near:
+            c.wait_recv()
+
+    def finish(self):
+        for c in list(self.far.values()) + self.near:
+            c.wait_send()
+
+
+def gather_sems():
+    return [DMA((4,)), DMA((4,)), DMA((4,)), DMA((4,)), DMA(())]
+
+
+def sum_sems(R, C):
+    return [
+        pltpu.VMEM((8, R, C), jnp.float32),
+        pltpu.VMEM((4, R, C), jnp.float32),
+        DMA((8,)),
+        DMA((8,)),
+        DMA((4,)),
+        DMA((4,)),
+    ]
+
+
+def sum_all(rows, bufs, d, f):
+    b1, b2, s1, r1, s2, r2 = bufs
+    for n, row in enumerate(rows):
+        b1[f, n : n + 1, :] = row
+    cps = [remote(b1.at[f], b1.at[f], s1.at[k], r1.at[k], d, f ^ k) for k in (6, 2, 4, 7, 3, 5, 1)]
+    for c in cps:
+        c.wait()
+    tot = b1[0]
+    for k in range(1, 8):
+        tot = tot + b1[k]
+    b2[d] = tot
+    cps = [remote(b2.at[d], b2.at[d], s2.at[k], r2.at[k], d ^ k, f) for k in (3, 2, 1)]
+    for c in cps:
+        c.wait()
+    tot = b2[0]
+    for k in range(1, 4):
+        tot = tot + b2[k]
+    return tot
+
+
+def column_sums(a, ins):
+    m = a * jnp.concatenate([ins] * (a.shape[1] // 128), axis=1)
+    return jnp.sum(m, axis=0, keepdims=True), jnp.sum(m * a, axis=0, keepdims=True)
+
+
+def bend(p):
+    g = 1.0 / (1.0 + jnp.exp(-p))
+    return p * g, g * (1.0 + p * (1.0 - g))
+
+
+def same_crop(here, there, width):
+    ok = (here == there) & (here > 0)
+    return jnp.concatenate([ok] * (width // 128), axis=ok.ndim - 1)
+
+
+def cat_rows(parts):
+    return jnp.concatenate(parts, axis=1)
+
+
+def bottleneck_kernel(
+    x_ref, kb_ref, ins_ref, gr, br, gd, bd, ge, be,
+    wr_s, wd_s, we_s, wp_s, wm_s, wc_s, k_s0, k_s1, k_s2, kp_s,
+    yo_o, y_o, n3_o, l3_o, n1_o, l1_o, n2_o, l2_o, ext_o, h2_o, key_o, k_o, wr_o, wd_o, we_o, wp_o, wm_o, wc_o, cnt_o,
+    xp, a1, a2, a3, ext, h2, y, n3, l3, n1, l1, n2, l2, key, wr, wd, we,
+    *sems,
+):
+    sems = list(sems)
+
+    def take(n):
+        got = sems[:n]
+        del sems[:n]
+        return got
+
+    f, d = greet(range(1, 8), range(1, 4))
+    N, C = x_ref.shape
+    Q, h = ext.shape[0], ext.shape[1] // 2
+    e = h // 2
+    rows = h // 4
+    neck = a1.shape[1]
+    T = 8 * h
+
+    def rows_of(ref, n):
+        return lambda g: ref.at[pl.ds(pl.multiple_of(n * g, n), n)]
+
+    nr, nd_, ne, np_ = wr_s.shape[0], wd_s.shape[1], we_s.shape[1], wp_s.shape[0]
+    g_key = Gather(kb_ref, lambda g: key.at[:, pl.ds(pl.multiple_of(PAD + h * g, 16), h), :], take(5), d, f)
+    g_wr = Gather(wr_s, rows_of(wr, nr), take(5), d, f)
+    g_wd = Gather(wd_s, lambda g: wd.at[:, pl.ds(pl.multiple_of(nd_ * g, 16), nd_), :], take(5), d, f)
+    g_we = Gather(we_s, lambda g: we.at[:, pl.ds(pl.multiple_of(ne * g, 128), ne)], take(5), d, f)
+    g_wp = Gather(wp_s, rows_of(wp_o, np_), take(5), d, f)
+    g_wm = Gather(wm_s, rows_of(wm_o, np_), take(5), d, f)
+    g_wc = Gather(wc_s, rows_of(wc_o, np_), take(5), d, f)
+    ks, kr, kl, hs, hr, ys, yr, yl, os_ = take(9)
+    sum1, sum2, sum3 = take(6), take(6), take(6)
+
+    g_key.start()
+    g_wr.start()
+    g_wd.start()
+    order = lax.broadcasted_iota(jnp.int32, (N, N), 0)
+    m, r, q = order % 4, (order // 4) % rows, order // h
+    pick = (r * (N // rows) + q * 4 + m) == lax.broadcasted_iota(jnp.int32, (N, N), 1)
+    pick = pick.astype(jnp.float32).astype(jnp.bfloat16)
+    for c in range(0, C, 256):
+        xp[:, c : c + 256] = nn_dot(pick, x_ref[:, c : c + 256]).astype(jnp.bfloat16)
+    key[:, :PAD, :] = jnp.zeros((Q, PAD, 128), jnp.bfloat16)
+    key[:, PAD + T :, :] = jnp.zeros((Q, PAD, 128), jnp.bfloat16)
+    g_key.forward()
+    g_wr.forward()
+    g_we.start()
+    g_wr.arrive()
+    sums, squares = [], []
+    for c in range(0, neck, 256):
+        a = nt_dot(xp[...], wr[c : c + 256, :])
+        a1[:, c : c + 256] = a
+        s, t = column_sums(a, ins_ref[...])
+        sums.append(s)
+        squares.append(t)
+    inside = jnp.sum(ins_ref[...], axis=0, keepdims=True)
+    st = sum_all([cat_rows(sums), cat_rows(squares), cat_rows([inside] * (neck // 128))], sum1, d, f)
+    count = st[2:3, :]
+    cnt_o[...] = jnp.zeros_like(cnt_o)
+    cnt_o[0:1, :neck] = count
+    mean = st[0:1] / count
+    inv = lax.rsqrt(st[1:2] / count - mean * mean + eps)
+    cnt_o[1:2, :neck] = inv
+    for c in range(0, neck, 256):
+        w = slice(c, c + 256)
+        n = (a1[:, w] - mean[:, w]) * inv[:, w]
+        act, lean = bend(n * gr[:, w] + br[:, w])
+        ext[:, e : e + h, w] = act.astype(jnp.bfloat16).reshape(Q, h, 256)
+        n1[:, w] = n.astype(jnp.bfloat16)
+        l1[:, w] = lean.astype(jnp.bfloat16)
+    up = remote(ext.at[:, pl.ds(e, e)], ext.at[:, pl.ds(e + h, e)], hs.at[0], hr.at[0], d, lax.rem(f + 7, 8))
+    down = remote(ext.at[:, pl.ds(h, e)], ext.at[:, pl.ds(0, e)], hs.at[1], hr.at[1], d, lax.rem(f + 1, 8))
+    g_wd.forward()
+    kcp = []
+    for k in (6, 7, 2, 3, 4, 5, 1):
+        for b, src in enumerate((k_s0, k_s1, k_s2, kp_s)):
+            n = src.shape[0]
+            o = src.shape[1]
+            kcp.append(
+                remote(
+                    src.at[:, :, pl.ds(pl.multiple_of((f ^ k) * 256, 128), 256)],
+                    k_o.at[pl.ds(9 * b, n), pl.ds(pl.multiple_of(o * f, 16), o), :],
+                    ks.at[b, k], kr.at[b, k], d, f ^ k,
+                )
+            )
+    for b, src in enumerate((k_s0, k_s1, k_s2, kp_s)):
+        n = src.shape[0]
+        o = src.shape[1]
+        c = pltpu.make_async_copy(
+            src.at[:, :, pl.ds(pl.multiple_of(f * 256, 128), 256)],
+            k_o.at[pl.ds(9 * b, n), pl.ds(pl.multiple_of(o * f, 16), o), :],
+            kl.at[b],
+        )
+        c.start()
+        kcp.append(c)
+    for g in (g_wp, g_wm, g_wc):
+        g.start()
+    g_key.arrive()
+    outs = [(n1, n1_o), (l1, l1_o), (key, key_o), (wr, wr_o)]
+    base = pl.multiple_of(PAD + h * f, 16)
+    up.wait()
+    down.wait()
+    outs.append((ext, ext_o))
+    g_wd.arrive()
+    outs.append((wd, wd_o))
+    a2[...] = jnp.zeros_like(a2)
+    for i in range(3):
+        for j in (1, 0, 2):
+            lo, hi = span(j - 1, Q)
+            ok = same_crop(
+                key[lo:hi, pl.ds(base, h), :],
+                key[lo + j - 1 : hi + j - 1, pl.ds(pl.multiple_of(base + e * (i - 1), 16), h), :],
+                neck,
+            )
+            v = jnp.where(ok, ext[lo + j - 1 : hi + j - 1, e * i : e * i + h, :], 0).reshape((hi - lo) * h, neck)
+            for c in range(0, neck, 256):
+                a2[lo * h : hi * h, c : c + 256] += nt_dot(v, wd[3 * i + j, c : c + 256, :])
+    sums, squares = [], []
+    for c in range(0, neck, 256):
+        s, t = column_sums(a2[:, c : c + 256], ins_ref[...])
+        sums.append(s)
+        squares.append(t)
+    st = sum_all([cat_rows(sums), cat_rows(squares)], sum2, d, f)
+    mean = st[0:1] / count
+    inv = lax.rsqrt(st[1:2] / count - mean * mean + eps)
+    cnt_o[2:3, :neck] = inv
+    for c in range(0, neck, 256):
+        w = slice(c, c + 256)
+        n = (a2[:, w] - mean[:, w]) * inv[:, w]
+        act, lean = bend(n * gd[:, w] + bd[:, w])
+        h2[:, w] = act.astype(jnp.bfloat16)
+        n2[:, w] = n.astype(jnp.bfloat16)
+        l2[:, w] = lean.astype(jnp.bfloat16)
+    outs += [(n2, n2_o), (l2, l2_o), (h2, h2_o)]
+    g_we.forward()
+    g_we.arrive()
+    outs.append((we, we_o))
+    sums, squares = [], []
+    for c in range(0, C, 256):
+        a = nn_dot(h2[...], we[:, c : c + 256])
+        a3[:, c : c + 256] = a
+        s, t = column_sums(a, ins_ref[...])
+        sums.append(s)
+        squares.append(t)
+    st = sum_all([cat_rows(sums), cat_rows(squares)], sum3, d, f)
+    total = count[:, :1]
+    mean3 = st[0:1] / total
+    inv3 = lax.rsqrt(st[1:2] / total - mean3 * mean3 + eps)
+    coef = sum3[0]
+    coef[0, 0:1, :] = mean3
+    coef[0, 1:2, :] = inv3
+    cnt_o[3:4, :] = inv3
+    sent = []
+    dst = yo_o.at[:, pl.ds(base, h), :]
+    for k in (6, 7, 2, 3, 4, 5, 1, 0):
+        g = f ^ k
+        w = pl.ds(pl.multiple_of(g * 256, 256), 256)
+        n = (a3[:, w] - coef[0, 0:1, w]) * coef[0, 1:2, w]
+        act, lean = bend(n * ge[:, w] + be[:, w] + xp[:, w].astype(jnp.float32))
+        y[:, :, w] = act.astype(jnp.bfloat16).reshape(Q, h, 256)
+        n3[:, w] = n.astype(jnp.bfloat16)
+        l3[:, w] = lean.astype(jnp.bfloat16)
+        part = y.at[:, :, w]
+        if k:
+            sent.append(remote(part, dst, ys.at[k], yr.at[k], d, g))
+        else:
+            own = pltpu.make_async_copy(part, dst, yl)
+            own.start()
+            sent.append(own)
+    outs += [(y, y_o), (n3, n3_o), (l3, l3_o)]
+    saved = []
+    for n, (src, to) in enumerate(outs):
+        c = pltpu.make_async_copy(src, to, os_.at[n])
+        c.start()
+        saved.append(c)
+    for g in (g_wp, g_wm, g_wc):
+        g.forward()
+    for g in (g_wp, g_wm, g_wc):
+        g.arrive()
+    for g in (g_key, g_wr, g_wd, g_we, g_wp, g_wm, g_wc):
+        g.finish()
+    for c in kcp + sent + saved:
+        c.wait()
+
+
+def bottleneck(x, kb, ins, vecs, shards, kparts):
+    N, C = x.shape
+    Q, h, _ = kb.shape
+    wr, wd, we, wp, wm, wc = shards
+    neck = we.shape[0]
+    W = 8 * wp.shape[0]
+    b16, f32 = jnp.bfloat16, jnp.float32
+    S = jax.ShapeDtypeStruct
+    TT = 8 * h + 2 * PAD
+    outs = [
+        S((Q, TT, C // 8), b16), S((Q, h, C), b16), S((N, C), b16), S((N, C), b16),
+        S((N, neck), b16), S((N, neck), b16), S((N, neck), b16), S((N, neck), b16),
+        S((Q, 2 * h, neck), b16), S((N, neck), b16), S((Q, TT, 128), b16), S((28, W, C // 8), b16),
+        S((neck, C), b16), S((9, neck, neck), b16), S((neck, C), b16), S((W, C), b16), S((W, wm.shape[1]), b16),
+        S((W, 128), b16), S((8, C), f32),
+    ]
+    V = pltpu.VMEM
+    scratch = [
+        V((N, C), b16), V((N, neck), f32), V((N, neck), f32), V((N, C), f32), V((Q, 2 * h, neck), b16), V((N, neck), b16),
+        V((Q, h, C), b16), V((N, C), b16), V((N, C), b16),
+        V((N, neck), b16), V((N, neck), b16), V((N, neck), b16), V((N, neck), b16), V((Q, TT, 128), b16),
+        V((neck, C), b16), V((9, neck, neck), b16), V((neck, C), b16),
+    ]
+    for _ in range(7):
+        scratch += gather_sems()
+    scratch += [DMA((4, 8)), DMA((4, 8)), DMA((4,)), DMA((2,)), DMA((2,)), DMA((8,)), DMA((8,)), DMA(()), DMA((16,))]
+    scratch += sum_sems(3, neck) + sum_sems(2, neck) + sum_sems(2, C)
+    return pl.pallas_call(
+        bottleneck_kernel,
+        out_shape=outs,
+        in_specs=[VM] * 9 + [ANY] * 10,
+        out_specs=[ANY] * 18 + [VM],
+        scratch_shapes=scratch,
+        compiler_params=pltpu.CompilerParams(collective_id=1, has_side_effects=True, vmem_limit_bytes=VLIM),
+        name="bottleneck",
+    )(x, kb, ins, *vecs, *shards, *kparts)
+
+
+def branches_back_kernel(
+    steps, d_ref, y_ref, key_ref, k_ref, pooled_ref, dr_ref, size_ref, dy_o, gk_o,
+    g, gt, x, gk, dyo, acc, gp, *sems,
+):
+    sems = list(sems)
+    f, d = greet(range(1, 8), ())
+    Q, h, w = y_ref.shape[0], d_ref.shape[1], y_ref.shape[2]
+    W = k_ref.shape[1]
+    T = 8 * h
+    o = W // 8
+    g_d = Gather(d_ref, lambda n: g.at[:, pl.ds(pl.multiple_of(PAD + h * n, 16), h), :], sems[:5], d, f)
+    ws, wr, wl, ds_, dr_, dl = sems[5:]
+    g_d.start()
+    gk[27] = tn_dot(dr_ref[...], pooled_ref[...]).astype(gk.dtype)
+    gp[...] = nn_dot(dr_ref[...], k_ref[27]) / size_ref[:, :1]
+    g_d.forward()
+    g_d.arrive()
+
+    def turn(q, _):
+        for b in range(3):
+            gt[b * W : (b + 1) * W, pl.ds(pl.multiple_of(q * T, 256), T)] = g[q, PAD : PAD + T, b * W : (b + 1) * W].T
+        return 0
+
+    lax.fori_loop(0, Q, turn, 0)
+    cps = []
+    for b, s in enumerate(steps):
+        for i in (-1, 0, 1):
+            for j in (-1, 0, 1):
+                lo, hi = span(s * j, Q)
+                a = PAD + 16 * s * i
+
+                def one(q, _):
+                    ok = same_crop(key_ref[q, PAD : PAD + T, :], key_ref[q + s * j, a : a + T, :], w)
+                    x[pl.ds(pl.multiple_of((q - lo) * T, 256), T), :] = jnp.where(ok, y_ref[q + s * j, a : a + T, :], 0)
+                    return 0
+
+                lax.fori_loop(lo, hi, one, 0)
+                gk[9 * b + 3 * (i + 1) + j + 1] = nn_dot(
+                    gt[b * W : (b + 1) * W, lo * T : hi * T], x[: (hi - lo) * T, :]
+                ).astype(gk.dtype)
+        n = 9 if b < 2 else 10
+        for k in (6, 7, 2, 3, 4, 5, 1, 0):
+            src = gk.at[pl.ds(9 * b, n), pl.ds(pl.multiple_of(o * (f ^ k), 16), o), :]
+            dst = gk_o.at[pl.ds(9 * b, n), :, pl.ds(pl.multiple_of(w * f, 128), w)]
+            if k:
+                cps.append(remote(src, dst, ws.at[b, k], wr.at[b, k], d, f ^ k))
+            else:
+                c = pltpu.make_async_copy(src, dst, wl.at[b])
+                c.start()
+                cps.append(c)
+
+    dst = dy_o.at[:, :, pl.ds(pl.multiple_of(w * f, 128), w)]
+
+    def rows_of(k):
+        return pl.ds(pl.multiple_of(h * (f ^ k), 16), h)
+
+    def dest_step(m, _):
+        k = 7 - m
+        dest = f ^ k
+        base = pl.multiple_of(PAD + h * dest, 16)
+        here = key_ref[:, pl.ds(base, h), :].astype(jnp.float32).reshape(Q * h, 128)
+        here = jnp.concatenate([here] * (w // 128), axis=1)
+        total = jnp.zeros((Q * h, w), jnp.float32)
+        for c in range(CROPS_TILE):
+            total = jnp.where(here == c + 1.0, gp[c : c + 1, :], total)
+        acc[...] = total
+        for b, s in enumerate(steps):
+            for i in (-1, 0, 1):
+                first = h * dest - 16 * s * i
+
+                @pl.when((first + h > 0) & (first < T))
+                def _():
+                    at = pl.multiple_of(base - 16 * s * i, 16)
+                    for j in (-1, 0, 1):
+                        lo, hi = span(-s * j, Q)
+                        ok = same_crop(
+                            key_ref[lo:hi, pl.ds(base, h), :], key_ref[lo - s * j : hi - s * j, pl.ds(at, h), :], W
+                        )
+                        v = jnp.where(ok, g[lo - s * j : hi - s * j, pl.ds(at, h), b * W : (b + 1) * W], 0)
+                        acc[lo * h : hi * h] += nn_dot(v.reshape((hi - lo) * h, W), k_ref[9 * b + 3 * (i + 1) + j + 1])
+
+        rows = rows_of(k)
+        dyo[:, rows, :] = acc[...].reshape(Q, h, w).astype(dyo.dtype)
+        src = dyo.at[:, rows, :]
+
+        @pl.when(k > 0)
+        def _():
+            remote(src, dst, ds_.at[k], dr_.at[k], d, dest)
+
+        @pl.when(k == 0)
+        def _():
+            pltpu.make_async_copy(src, dst, dl).start()
+
+        return 0
+
+    lax.fori_loop(0, 8, dest_step, 0)
+    for k in range(1, 8):
+        c = pltpu.make_async_remote_copy(
+            src_ref=dyo.at[:, rows_of(k), :], dst_ref=dst, send_sem=ds_.at[k], recv_sem=dr_.at[k],
+            device_id=(d, f ^ k), device_id_type=MESH,
+        )
+        c.wait()
+    pltpu.make_async_copy(dyo.at[:, rows_of(0), :], dst, dl).wait()
+    g_d.finish()
+    for c in cps:
+        c.wait()
+
+
+def branches_back(d, y, key, k, pooled, dr, sizes, steps):
+    Q, h, W3 = d.shape
+    TT, w = y.shape[1:]
+    W = W3 // 3
+    T = 8 * h
+    b16, f32 = jnp.bfloat16, jnp.float32
+    V = pltpu.VMEM
+    return pl.pallas_call(
+        functools.partial(branches_back_kernel, steps),
+        out_shape=[jax.ShapeDtypeStruct((Q, h, 8 * w), b16), jax.ShapeDtypeStruct((28, W // 8, 8 * w), b16)],
+        in_specs=[VM] * 7,
+        out_specs=[ANY] * 2,
+        scratch_shapes=[
+            V((Q, TT, W3), b16), V((W3, Q * T), b16), V((Q * T, w), b16), V((28, W, w), b16), V((Q, T, w), b16),
+            V((Q * h, w), f32), V((8, w), f32),
+        ]
+        + gather_sems()
+        + [DMA((3, 8)), DMA((3, 8)), DMA((3,)), DMA((8,)), DMA((8,)), DMA(())],
+        compiler_params=pltpu.CompilerParams(collective_id=10, has_side_effects=True, vmem_limit_bytes=VLIM),
+        name="branches_back",
+    )(d, y, key, k, pooled, dr, sizes)
+
+
+class Sum:
+    def __init__(self, bufs, d, f):
+        self.b1, self.b2, self.s1, self.r1, self.s2, self.r2 = bufs
+        self.d, self.f = d, f
+
+    def start(self, rows):
+        b1, d, f = self.b1, self.d, self.f
+        for n, row in enumerate(rows):
+            b1[f, n : n + 1, :] = row
+        self.cps = [remote(b1.at[f], b1.at[f], self.s1.at[k], self.r1.at[k], d, f ^ k) for k in (6, 2, 4, 7, 3, 5, 1)]
+
+    def turn(self):
+        b1, b2, d, f = self.b1, self.b2, self.d, self.f
+        for c in self.cps:
+            c.wait()
+        tot = b1[0]
+        for k in range(1, 8):
+            tot = tot + b1[k]
+        b2[d] = tot
+        self.cps = [remote(b2.at[d], b2.at[d], self.s2.at[k], self.r2.at[k], d ^ k, f) for k in (3, 2, 1)]
+
+    def result(self):
+        for c in self.cps:
+            c.wait()
+        tot = self.b2[0]
+        for k in range(1, 4):
+            tot = tot + self.b2[k]
+        return tot
+
+
+class Reduce:
+    def __init__(self, full, part, near, far, tot, zr, out, quarter, sems, d, f):
+        self.full, self.part, self.near, self.fars, self.tot, self.zr, self.out = full, part, near, far, tot, zr, out
+        self.quarter, self.d, self.f = quarter, d, f
+        self.sems = sems
+        self.c0 = f % 2
+        self.me = f // 2
+        self.sent = []
+
+    def pair(self):
+        ps, pr = self.sems[:2]
+        self.cps = [
+            remote(self.full.at[self.part(2 * g + 1 - self.c0)], self.near.at[g], ps.at[g], pr.at[g], self.d, self.f ^ 1)
+            for g in range(4)
+        ]
+
+    def far(self):
+        ss, rs = self.sems[2:4]
+        for c in self.cps:
+            c.wait()
+        self.cps = []
+        for k in (3, 1, 2, 0):
+            g = self.me ^ k
+            val = self.full[self.part(2 * g + self.c0)].astype(jnp.float32) + self.near[g].astype(jnp.float32)
+            self.near[g] = val.astype(self.near.dtype)
+            if k:
+                self.cps.append(
+                    remote(self.near.at[g], self.fars.at[k], ss.at[k], rs.at[k], self.d, self.f ^ (2 * k))
+                )
+
+    def tiles(self):
+        ss, rs = self.sems[4:6]
+        for c in self.cps:
+            c.wait()
+        val = self.near[self.me].astype(jnp.float32)
+        for k in (1, 2, 3):
+            val = val + self.fars[k].astype(jnp.float32)
+        self.tot[...] = val.astype(self.tot.dtype)
+        self.cps = [
+            remote(self.tot.at[self.quarter(self.d ^ k)], self.zr.at[self.d], ss.at[k], rs.at[k], self.d ^ k, self.f)
+            for k in (3, 2, 1)
+        ]
+        self.zr[self.d] = self.tot[self.quarter(self.d)]
+
+    def back(self):
+        ss, rs = self.sems[6:8]
+        for c in self.cps:
+            c.wait()
+        val = self.zr[0].astype(jnp.float32)
+        for k in (1, 2, 3):
+            val = val + self.zr[k].astype(jnp.float32)
+        mine = self.quarter(self.d)
+        self.out[mine] = val.astype(self.out.dtype)
+        self.cps = [
+            remote(self.out.at[mine], self.out.at[mine], ss.at[k], rs.at[k], self.d ^ k, self.f) for k in (3, 2, 1)
+        ]
+
+    def done(self):
+        for c in self.cps:
+            c.wait()
+
+
+def reduce_scratch(block, quarter):
+    V, b16 = pltpu.VMEM, jnp.bfloat16
+    return [V((4,) + block, b16), V((4,) + block, b16), V(block, b16), V((4,) + quarter, b16)] + [DMA((4,))] * 8
+
+
+def wide(row, n):
+    return jnp.concatenate([row] * n, axis=1)
+
+
+def bottleneck_back_kernel(
+    x_ref, ins_ref, st_ref, gr, gd, ge, dy, dpt, y_ref, pm_in, wp, n3, l3, we, n2, l2, h2, wd, ext, n1, l1, wr, key_any,
+    gf_o, pm_o, ex_o, di_o, re_o, s3_o, s2_o, s1_o,
+    pm, ex, di, re_, dp3, d3, acc, ext2, d1n, key, gf, pick, ksem, hs, hr, gs,
+    *sems,
+):
+    sems = list(sems)
+
+    def take(n):
+        got = sems[:n]
+        del sems[:n]
+        return got
+
+    f, d = greet(range(1, 8), range(1, 4))
+    N, C = x_ref.shape
+    Q, h = ext2.shape[0], ext2.shape[1] // 2
+    e = h // 2
+    rows = h // 4
+    neck = acc.shape[1]
+    nb = neck // 8
+    nw = pm.shape[0] // 8
+    PW = pm.shape[1] // 4
+    W = dpt.shape[1]
+
+    def ds(i, n):
+        return pl.ds(pl.multiple_of(n * i, n), n)
+
+    def reducer(full, part, out, quarter):
+        near, far, tot, zr = take(4)
+        return Reduce(full, part, near, far, tot, zr, out, quarter, take(8), d, f)
+
+    r_pm = reducer(pm, lambda g: (ds(g, nw),), pm_o, lambda g: (slice(None), ds(g, PW)))
+    r_ex = reducer(ex, lambda g: (slice(None), ds(g, C // 8)), ex_o, lambda g: (ds(g, neck // 4),))
+    r_di = reducer(
+        di, lambda g: (slice(None), ds(g, nb)), di_o, lambda g: (slice(None), ds(g, nb // 4))
+    )
+    r_re = reducer(re_, lambda g: (ds(g, nb),), re_o, lambda g: (ds(g, nb // 4),))
+    sum3, sum2, sum1 = (Sum(take(6), d, f) for _ in range(3))
+
+    kcp = pltpu.make_async_copy(key_any.at[:, pl.ds(pl.multiple_of(PAD - e + h * f, 16), 2 * h), :], key, ksem)
+    kcp.start()
+    count = st_ref[0:1, 0:1]
+    for c in range(0, C, 256):
+        pm[:, c : c + 256] = tn_dot(dpt[...], y_ref[:, c : c + 256]).astype(jnp.bfloat16)
+    pm[:, C:] = pm_in[...]
+    r_pm.pair()
+    ones, crossed = [], []
+    ins = wide(ins_ref[...], 2)
+    for c in range(0, C, 256):
+        w = slice(c, c + 256)
+        v = dy[:, w].astype(jnp.float32) + nn_dot(dpt[...], wp[:, w])
+        v = v * l3[:, w].astype(jnp.float32)
+        dp3[:, w] = v.astype(jnp.bfloat16)
+        v = v * ins
+        ones.append(jnp.sum(v, axis=0, keepdims=True))
+        crossed.append(jnp.sum(v * n3[:, w].astype(jnp.float32), axis=0, keepdims=True))
+    sum3.start([cat_rows(ones), cat_rows(crossed)])
+    order = lax.broadcasted_iota(jnp.int32, (N, N), 1)
+    m, r, q = order % 4, (order // 4) % rows, order // h
+    hit = (r * (N // rows) + q * 4 + m) == lax.broadcasted_iota(jnp.int32, (N, N), 0)
+    pick[...] = hit.astype(jnp.float32).astype(jnp.bfloat16)
+    sum3.turn()
+    r_pm.far()
+    tot = sum3.result()
+    s3_o[...] = tot
+    for c in range(0, C, 256):
+        w = slice(c, c + 256)
+        v = dp3[:, w].astype(jnp.float32) - tot[0:1, w] / count - n3[:, w].astype(jnp.float32) * (tot[1:2, w] / count)
+        d3[:, w] = (ins * v * (ge[:, w] * st_ref[3:4, w])).astype(jnp.bfloat16)
+    ones, crossed = [], []
+    for c in range(0, neck, 256):
+        w = slice(c, c + 256)
+        v = nt_dot(d3[...], we[w, :]) * l2[:, w].astype(jnp.float32)
+        acc[:, w] = v
+        v = v * ins
+        ones.append(jnp.sum(v, axis=0, keepdims=True))
+        crossed.append(jnp.sum(v * n2[:, w].astype(jnp.float32), axis=0, keepdims=True))
+    sum2.start([cat_rows(ones), cat_rows(crossed)])
+    for c in range(0, C, 256):
+        ex[:, c : c + 256] = tn_dot(h2[...], d3[:, c : c + 256]).astype(jnp.bfloat16)
+    sum2.turn()
+    r_ex.pair()
+    tot = sum2.result()
+    s2_o[...] = tot
+    for c in range(0, neck, 256):
+        w = slice(c, c + 256)
+        v = acc[:, w] - tot[0:1, w] / count - n2[:, w].astype(jnp.float32) * (tot[1:2, w] / count)
+        v = ins * v * (gd[:, w] * st_ref[2:3, w])
+        ext2[:, e : e + h, w] = v.astype(jnp.bfloat16).reshape(Q, h, 256)
+    up = remote(ext2.at[:, pl.ds(e, e)], ext2.at[:, pl.ds(e + h, e)], hs.at[0], hr.at[0], d, lax.rem(f + 7, 8))
+    down = remote(ext2.at[:, pl.ds(h, e)], ext2.at[:, pl.ds(0, e)], hs.at[1], hr.at[1], d, lax.rem(f + 1, 8))
+    kcp.wait()
+    r_pm.tiles()
+    r_ex.far()
+    for i in range(3):
+        for j in range(3):
+            lo, hi = span(j - 1, Q)
+            ok = same_crop(
+                key[lo:hi, e : e + h, :], key[lo + j - 1 : hi + j - 1, e * i : e * i + h, :], neck
+            )
+            v = jnp.where(ok, ext[lo + j - 1 : hi + j - 1, e * i : e * i + h, :], 0).reshape((hi - lo) * h, neck)
+            g = ext2[lo:hi, e : e + h, :].reshape((hi - lo) * h, neck)
+            di[3 * i + j] = tn_dot(g, v).astype(jnp.bfloat16)
+    r_di.pair()
+    up.wait()
+    down.wait()
+    acc[...] = jnp.zeros_like(acc)
+    for i in range(3):
+        for j in (1, 0, 2):
+            lo, hi = span(1 - j, Q)
+            ok = same_crop(
+                key[lo:hi, e : e + h, :], key[lo + 1 - j : hi + 1 - j, e * (2 - i) : e * (2 - i) + h, :], neck
+            )
+            v = jnp.where(ok, ext2[lo + 1 - j : hi + 1 - j, e * (2 - i) : e * (2 - i) + h, :], 0)
+            v = v.reshape((hi - lo) * h, neck)
+            for c in range(0, neck, 256):
+                acc[lo * h : hi * h, c : c + 256] += nn_dot(v, wd[3 * i + j, :, c : c + 256])
+    ones, crossed = [], []
+    for c in range(0, neck, 256):
+        w = slice(c, c + 256)
+        v = acc[:, w] * l1[:, w].astype(jnp.float32)
+        acc[:, w] = v
+        v = v * ins
+        ones.append(jnp.sum(v, axis=0, keepdims=True))
+        crossed.append(jnp.sum(v * n1[:, w].astype(jnp.float32), axis=0, keepdims=True))
+    sum1.start([cat_rows(ones), cat_rows(crossed)])
+    r_di.far()
+    sum1.turn()
+    r_pm.back()
+    r_ex.tiles()
+    tot = sum1.result()
+    s1_o[...] = tot
+    for c in range(0, neck, 256):
+        w = slice(c, c + 256)
+        v = acc[:, w] - tot[0:1, w] / count - n1[:, w].astype(jnp.float32) * (tot[1:2, w] / count)
+        v = (ins * v * (gr[:, w] * st_ref[1:2, w])).astype(jnp.bfloat16)
+        d1n[:, w] = nn_dot(pick[...], v).astype(jnp.bfloat16)
+    for c in range(0, C, 256):
+        re_[:, c : c + 256] = tn_dot(d1n[...], x_ref[:, c : c + 256]).astype(jnp.bfloat16)
+    r_re.pair()
+    out = []
+    for n, c in enumerate(range(0, C, 256)):
+        w = slice(c, c + 256)
+        if n >= 2:
+            out[n - 2].wait()
+        gf[n % 2] = nn_dot(pick[...], dp3[:, w]) + nn_dot(d1n[...], wr[:, w])
+        cp = pltpu.make_async_copy(gf.at[n % 2], gf_o.at[:, pl.ds(c, 256)], gs.at[n % 2])
+        cp.start()
+        out.append(cp)
+        if n == 1:
+            r_re.far()
+        if n == 3:
+            r_ex.back()
+        if n == 5:
+            r_di.tiles()
+    r_re.tiles()
+    r_di.back()
+    r_re.back()
+    out[-2].wait()
+    out[-1].wait()
+    for r in (r_pm, r_ex, r_di, r_re):
+        r.done()
+
+
+def bottleneck_back(*args):
+    x, st, dpt, pm_in, h2 = args[0], args[2], args[7], args[9], args[16]
+    N, C = x.shape
+    Q, h2_, neck = args[18].shape
+    h = h2_ // 2
+    W = dpt.shape[1]
+    PM = C + pm_in.shape[1]
+    b16, f32 = jnp.bfloat16, jnp.float32
+    S, V = jax.ShapeDtypeStruct, pltpu.VMEM
+    blocks = [
+        ((W // 8, PM), (W // 8, PM // 4)),
+        ((neck, C // 8), (neck // 4, C // 8)),
+        ((9, neck // 8, neck), (9, neck // 32, neck)),
+        ((neck // 8, C), (neck // 32, C)),
+    ]
+    scratch = [
+        V((W, PM), b16), V((neck, C), b16), V((9, neck, neck), b16), V((neck, C), b16), V((N, C), b16), V((N, C), b16),
+        V((N, neck), f32), V((Q, 2 * h, neck), b16), V((N, neck), b16), V((Q, 2 * h, 128), b16), V((2, N, 256), f32),
+        V((N, N), b16), DMA(()), DMA((2,)), DMA((2,)), DMA((2,)),
+    ]
+    for block, quarter in blocks:
+        scratch += reduce_scratch(block, quarter)
+    scratch += sum_sems(2, C) + sum_sems(2, neck) + sum_sems(2, neck)
+    return pl.pallas_call(
+        bottleneck_back_kernel,
+        out_shape=[S((N, C), f32)] + [S(b, b16) for b, _ in blocks] + [S((2, C), f32), S((2, neck), f32), S((2, neck), f32)],
+        in_specs=[VM] * 22 + [ANY],
+        out_specs=[ANY] + [VM] * 7,
+        scratch_shapes=scratch,
+        compiler_params=pltpu.CompilerParams(collective_id=12, has_side_effects=True, vmem_limit_bytes=VLIM),
+        name="bottleneck_back",
+    )(*args)
+
+
 def norm_coeffs(totals, squares, count):
     average = totals / count
     return average, lax.rsqrt(squares / count - average * average + eps)
@@ -406,73 +1146,34 @@
         a = a.reshape((Q, rows, 4) + a.shape[1:])
         return jnp.swapaxes(a, 0, 1).reshape((rows, cols) + a.shape[3:])
 
-    kt = jnp.concatenate([jnp.swapaxes(w.reshape(9, C, -1), 1, 2) for w in (w_rate, w_rate_double, w_rate_triple)])
-    full_reduce = lax.all_gather(w_reduce, "fsdp", axis=1, tiled=True)
-    full_dilated = lax.all_gather(w_dilated, "fsdp", axis=3, tiled=True)
-    full_expand = lax.all_gather(w_expand, "fsdp", axis=1, tiled=True)
-    kernel = lax.all_to_all(kt, "fsdp", split_axis=2, concat_axis=1, tiled=True)
-    full_point = lax.all_gather(w_point, "fsdp", axis=1, tiled=True)
-    full_merge = lax.all_gather(w_merge, "fsdp", axis=1, tiled=True)
-    full_pool = lax.all_gather(w_pool, "fsdp", axis=1, tiled=True)
-    full_classes = lax.all_gather(w_classes, "fsdp", axis=0, tiled=True)
-
-    x0 = perm(features)
     local_crop = perm(crop_ids) - lax.axis_index("dp") * CROPS_TILE
     in_crop = perm(crop_ids) >= 0
     inside = in_crop.astype(jnp.float32)[:, None]
-    key_loc = jnp.where(in_crop, local_crop + 1, 0).astype(jnp.bfloat16)
-    key_all = lax.all_gather(key_loc.reshape(Q, h), "fsdp", axis=1, tiled=True)
-    key_pad = jnp.pad(key_all, ((0, 0), (PAD, PAD)))
-    key = jnp.broadcast_to(key_pad[:, :, None], key_pad.shape + (128,))
-
-    a_one = flat_dot(x0, full_reduce)
-    neck = a_one.shape[1]
-    st = total_sum(
-        [jnp.sum(a_one * inside, axis=0), jnp.sum(a_one * a_one * inside, axis=0), jnp.full((neck,), jnp.sum(inside))], 1
-    )
-    count = st[2, 0]
-    m_one, s_one = norm_coeffs(st[0], st[1], count)
-    n_one = (a_one - m_one) * s_one
-    p_one = n_one * gain_reduce + bias_reduce
-    h_one = jax.nn.silu(p_one).astype(jnp.bfloat16)
-
-    def halo(a):
-        a = a.reshape(Q, h, -1)
-        e = 4 * DILATION_SPAN
-        up = passed_along(a[:, h - e :], "fsdp", 1)
-        down = passed_along(a[:, :e], "fsdp", -1)
-        return jnp.concatenate([up, a, down], axis=1)
-
-    e = 4 * DILATION_SPAN
-    key_near = lax.dynamic_slice_in_dim(key_pad, PAD - e + h * place, h + 2 * e, axis=1)
-    key_here = key_near[:, e : e + h]
-
-    def taps(a):
-        a = jnp.pad(a, ((1, 1), (0, 0), (0, 0)))
-        kn = jnp.pad(key_near, ((1, 1), (0, 0)))
-        pieces = []
-        for i in range(3):
-            for j in range(3):
-                ok = (kn[j : j + Q, e * i : e * i + h] == key_here) & (key_here > 0)
-                pieces.append(jnp.where(ok[:, :, None], a[j : j + Q, e * i : e * i + h], 0).reshape(N, -1))
-        return pieces
-
-    x_taps = taps(halo(h_one))
-    a_two = sum(flat_dot(x_taps[t], full_dilated[t // 3, t % 3]) for t in range(9))
-    st = total_sum([jnp.sum(a_two * inside, axis=0), jnp.sum(a_two * a_two * inside, axis=0)], 2)
-    m_two, s_two = norm_coeffs(st[0], st[1], count)
-    n_two = (a_two - m_two) * s_two
-    p_two = n_two * gain_dilated + bias_dilated
-    h_two = jax.nn.silu(p_two).astype(jnp.bfloat16)
-    a_three = flat_dot(h_two, full_expand)
-    st = total_sum([jnp.sum(a_three * inside, axis=0), jnp.sum(a_three * a_three * inside, axis=0)], 3)
-    m_three, s_three = norm_coeffs(st[0], st[1], count)
-    n_three = (a_three - m_three) * s_three
-    p_three = n_three * gain_expand + bias_expand + x0
-    y = jax.nn.silu(p_three).astype(jnp.bfloat16)
-
-    y_own = spread_channels(y.reshape(Q, h, C), 4)
-    part = conv_forward(y_own, key, kernel, steps)
+    key_loc = jnp.where(in_crop, local_crop + 1, 0)
+    kb = jnp.broadcast_to(key_loc.astype(jnp.bfloat16)[:, None], (N, 128)).reshape(Q, h, 128)
+    ins = jnp.broadcast_to(inside, (N, 128))
+    rates = [jnp.swapaxes(w.reshape(9, C, -1), 1, 2) for w in (w_rate, w_rate_double, w_rate_triple)]
+    vecs = [v[None, :] for v in (gain_reduce, bias_reduce, gain_dilated, bias_dilated, gain_expand, bias_expand)]
+    (
+        y_own, y, n_three, l_three, n_one, l_one, n_two, l_two, ext, h_two, key, kernel,
+        wr, wd, full_expand, wp, wm, wc, count,
+    ) = bottleneck(
+        features.reshape(N, C), kb, ins, vecs,
+        [
+            w_reduce.T, jnp.swapaxes(w_dilated.reshape(9, w_dilated.shape[2], -1), 1, 2), w_expand, w_point.T, w_merge.T,
+            jnp.pad(w_classes, ((0, 0), (0, 128 - CLASSES))),
+        ],
+        rates + [w_pool.T[None]],
+    )
+    neck = gain_reduce.shape[0]
+    stats = count
+    count = count[0, 0]
+    y = y.reshape(N, C)
+    full_reduce, full_point, full_merge, full_classes = wr.T, wp.T, wm.T, wc[:, :CLASSES]
+    neck = gain_reduce.shape[0]
+    full_pool = lax.all_gather(w_pool, "fsdp", axis=1, tiled=True)
+
+    part = conv_forward(y_own, key, kernel[:27], steps)
     a_rates = scatter_sum(part.reshape(nf, N, 3 * W), 5)
     a_point = flat_dot(y, full_point)
     a_br = jnp.concatenate([a_point, a_rates], axis=1)
@@ -522,51 +1223,46 @@
     )
     crop_grad = lax.psum(crop_grad, "fsdp")
     d_pool = (crop_grad * slope(pool_act)).astype(jnp.bfloat16)
-    owned = (jnp.arange(CROPS_TILE) % nf == place).astype(jnp.float32)[:, None]
-    grad_pool = inner_dot(pooled, (d_pool * owned).astype(jnp.bfloat16))
-    grad_pooled = outer_dot(d_pool, full_pool) / crop_sizes[:, None]
-    g_all = gather_rows(d_br[:, W:].reshape(Q, h, 3 * W), 10)
-    d_y_own = conv_data(g_all, key, kernel, steps)
-    d_y = collect_channels(d_y_own, 11).reshape(N, C).astype(jnp.float32)
-    grad_k = conv_weight(y_own, key, g_all, steps, W)
-    grad_k = lax.all_to_all(grad_k, "fsdp", split_axis=1, concat_axis=2, tiled=True)
+
+    def eight(a):
+        return jnp.pad(a, ((0, 8 - a.shape[0]), (0, 0)))
+
+    pooled_own = lax.dynamic_slice_in_dim(pooled, place * (C // nf), C // nf, axis=1)
+    sizes = jnp.broadcast_to(jnp.pad(crop_sizes, (0, 8 - CROPS_TILE), constant_values=1.0)[:, None], (8, 128))
+    d_y, grad_k = branches_back(
+        d_br[:, W:].reshape(Q, h, 3 * W), y_own, key, kernel, eight(pooled_own), eight(d_pool), sizes, steps
+    )
     grad_k = lax.psum(grad_k, "dp").astype(jnp.float32)
-    grad_point = inner_dot(y, d_br[:, :W])
-    d_y = d_y + outer_dot(d_br[:, :W], full_point)
-    d_y = d_y + lax.dot_general(
-        member.astype(jnp.float32), grad_pooled, (((1,), (0,)), ((), ())),
-        precision=lax.Precision.HIGHEST, preferred_element_type=jnp.float32,
-    )
-    d_p3 = d_y * slope(p_three)
-    d_three, gg_expand, gb_expand = back(d_p3, n_three, s_three, gain_expand, 12)
-    grad_expand = inner_dot(h_two, d_three)
-    d_h2 = outer_dot(d_three, full_expand)
-    d_two, gg_dilated, gb_dilated = back(d_h2 * slope(p_two), n_two, s_two, gain_dilated, 13)
-    grad_dilated = jnp.stack([inner_dot(x_taps[t], d_two) for t in range(9)])
-    d_taps = taps(halo(d_two))
-    d_h1 = sum(outer_dot(d_taps[8 - t], full_dilated[t // 3, t % 3]) for t in range(9))
-    d_one, gg_reduce, gb_reduce = back(d_h1 * slope(p_one), n_one, s_one, gain_reduce, 14)
-    grad_reduce = inner_dot(x0, d_one)
-    grad_features = unperm(d_p3 + outer_dot(d_one, full_reduce))
-
-    def shard(g, dim):
-        g = lax.psum_scatter(g, "fsdp", scatter_dimension=dim, tiled=True)
-        return lax.psum(g.astype(jnp.bfloat16), "dp").astype(jnp.float32)
-
-    grad_k = jnp.swapaxes(grad_k.reshape(3, 3, 3, -1, C), 3, 4)
+    rest = jnp.concatenate(
+        [grad_merge.T, jnp.pad(grad_classes, ((0, 0), (0, 128 - CLASSES)))], axis=1
+    ).astype(jnp.bfloat16)
+    rest = jnp.pad(rest, ((0, 0), (0, -(C + rest.shape[1]) % 512)))
+    grad_features, pm, ex, di, re_, st3, st2, st1 = bottleneck_back(
+        features.reshape(N, C), ins, stats, vecs[0], vecs[2], vecs[4], d_y.reshape(N, C), d_br[:, :W], y, rest, wp,
+        n_three, l_three, full_expand, n_two, l_two, h_two, wd, ext, n_one, l_one, wr, key,
+    )
+    pm = pm.astype(jnp.float32)
+    grad_point, grad_merge, grad_classes = pm[:, :C].T, pm[:, C : C + 5 * W].T, pm[:, C + 5 * W : C + 5 * W + CLASSES]
+    grad_features = grad_features.reshape(rows, cols, C)
+    grad_reduce = re_.astype(jnp.float32).T
+    grad_dilated = jnp.swapaxes(di.astype(jnp.float32), 1, 2).reshape(3, 3, neck, -1)
+    grad_expand = ex.astype(jnp.float32)
+    gg_expand, gb_expand, gg_dilated, gb_dilated, gg_reduce, gb_reduce = st3[1], st3[0], st2[1], st2[0], st1[1], st1[0]
+    grad_pool = grad_k[27].T
+    grad_k = jnp.swapaxes(grad_k[:27].reshape(3, 3, 3, -1, C), 3, 4)
     return (
         class_logits,
         grad_features,
-        shard(grad_reduce, 1), gg_reduce, gb_reduce,
-        shard(grad_dilated, 2).reshape(3, 3, neck, -1), gg_dilated, gb_dilated,
-        shard(grad_expand, 1), gg_expand, gb_expand,
-        shard(grad_point, 1), gg_br[:W], gb_br[:W],
+        grad_reduce, gg_reduce, gb_reduce,
+        grad_dilated, gg_dilated, gb_dilated,
+        grad_expand, gg_expand, gb_expand,
+        grad_point, gg_br[:W], gb_br[:W],
         grad_k[0], gg_br[W : 2 * W], gb_br[W : 2 * W],
         grad_k[1], gg_br[2 * W : 3 * W], gb_br[2 * W : 3 * W],
         grad_k[2], gg_br[3 * W :], gb_br[3 * W :],
-        shard(grad_pool, 1),
-        shard(grad_merge, 1), gg_merge, gb_merge,
-        shard(grad_classes, 0),
+        grad_pool,
+        grad_merge, gg_merge, gb_merge,
+        grad_classes,
     )
 
 

time: 1160 us -> 716 us (0.62)
  waiting for transfers between devices: 297 us -> 13.5 us
  Pallas kernels: 354 us -> 570 us
  local copies, waits for them, and re-layouts: 175 us -> 32.8 us
  blocking collectives: 122 us -> 35.8 us
  matrix products: 89.4 us -> 14.3 us
  other arithmetic: 82.9 us -> 24.9 us
  starting transfers between devices: 16.6 us -> 0.08 us
    pallas_call x5 -> x3, Pallas kernels: 169 us -> 455 us  [the longest x1 170 us: bottleneck(): pl.pallas_call(bottleneck_kernel, out_shape=outs, in_specs=[VM] * 9 + [AN...]
    psum x1, waiting for transfers between devices: 153 us -> 12.8 us  [fast_body(): grad_k = lax.psum(grad_k, 'dp').astype(jnp.float32)]
    all_to_all x2 -> x0, waiting for transfers between devices: 82.6 us -> none  [the longest x1 82.6 us: fast_body(): lax.all_to_all(grad_k, 'fsdp', split_axis=1, concat_axis=2, tiled=True)]
    all_gather x3 -> x0, blocking collectives: 73.6 us -> none  [the longest x1 48.5 us: fast_body(): key_all = lax.all_gather(key_loc.reshape(Q, h), 'fsdp', axis=1, tiled=True)]
    pallas_call x10 -> x4, Pallas kernels: 111 us -> 39.9 us  [total_sum(): pl.pallas_call(sum_kernel, out_shape=jax.ShapeDtypeStruct((R, C), jnp.flo...]
    unnamed x218 -> x103, local copies, waits for them, and re-layouts: 44.5 us -> 6.24 us
    unnamed x14 -> x2, waiting for transfers between devices: 34.7 us -> 0.7 us
    dot_general x15 -> x3, matrix products: 30.8 us -> 3.3 us  [inner_dot(): lax.dot_general(first_op, second_op, (((0,), (0,)), ((), ())), preferred_...]
  transfers between devices with their start and end apart: 19 -> 2, of which waited for: 5 -> 1; matrix products, arithmetic and copies ran while one was open for 26% -> 5% of each run, Pallas kernels for 28% -> 58%
where the time goes in v2:
time: 716 us; the launch traced here: 707 us
  Pallas kernels  570 us (80%)
  blocking collectives  35.8 us (5%)
  local copies, waits for them, and re-layouts  32.8 us (5%)
  other arithmetic  24.9 us (3%)
  between operations  15 us (2%)
  matrix products  14.3 us (2%)
  waiting for transfers between devices  13.5 us (2%)
    pallas_call x1, Pallas kernels, bottleneck(): pl.pallas_call(bottleneck_kernel, out_shape=outs, in_specs=[VM] * 9 + [AN...  170 us
    pallas_call x1, Pallas kernels, bottleneck_back(): pl.pallas_call(bottleneck_back_kernel, out_shape=[S((N, C), f32)] + [S(b,...  158 us
    pallas_call x1, Pallas kernels, branches_back(): pl.pallas_call(functools.partial(branches_back_kernel, steps), out_shape=...  127 us
    pallas_call x1, Pallas kernels, scatter_sum(): pl.pallas_call(scatter_kernel, out_shape=jax.ShapeDtypeStruct((R, C), jnp...  47.7 us
    pallas_call x4, Pallas kernels, total_sum(): pl.pallas_call(sum_kernel, out_shape=jax.ShapeDtypeStruct((R, C), jnp.flo...  39.9 us
    pallas_call x1, Pallas kernels, conv_forward(): pl.pallas_call(functools.partial(conv_forward_kernel, steps), out_shape=j...  27.2 us
    psum x1, blocking collectives, fast_body(): crop_sums, crop_sizes = lax.psum((crop_sums, crop_sizes), 'fsdp')  23.1 us
  transfers between devices with their start and end apart: 2, of which 1 were waited for; matrix products, arithmetic and copies ran while one was open for 5% of the time, Pallas kernels for 58%

profile of v2, /device:TPU:0, one launch (start us, length us, event | category | flops | bytes accessed | tf_op | source)
XLA Modules:
  0.0 706.5 jit_solution(14699094464286186082)
XLA Ops:
  13.5 170.0 %bottleneck.1 = (bf16[16,544,256]{2,1,0:T(8,128)(2,1)}, bf16[16,32,2048]{2,1,0:T(8,128)(2,1)}, bf16[512,2048]{1,0:T(8,128)(2,1)}, bf16[512,2048]{1,0:T(8,128)(2,...) custom-call(bf16[512,2048]{1,0:T(8,128)(2,1)} %bitcast.114, ...), custom_call_target="tpu_custom_call" | custom-call | tf_op jit(solution)/shard_map/bottleneck/pallas_call | solution.py:680
  183.5 4.2 slice.147.k_ref
  187.7 27.2 %conv_forward.1 = bf16[8,16,32,768]{3,2,1,0:T(8,128)(2,1)} custom-call(bf16[16,544,256]{2,1,0:T(8,128)(2,1)} %get-tuple-element.59.y_ref, bf16[16,544,128]{2,1,0:T(8,128)(2,1)} %get-tuple-element.60.key_ref.key_any, bf16[27,256,256]{2,1,0:T(8,128)(2,1)} %slice.147.k_ref), custom_call_target="tpu_custom_call" | custom-call | tf_op jit(solution)/shard_map/conv_forward/pallas_call | solution.py:273
  214.9 47.7 %scatter_5.1 = f32[512,768]{1,0:T(8,128)} custom-call(bf16[8,512,768]{2,1,0:T(8,128)(2,1)} %bitcast.113), custom_call_target="tpu_custom_call" | custom-call | tf_op jit(solution)/shard_map/scatter_5/pallas_call | solution.py:205
  262.6 2.4 fusion.24
  266.2 10.1 %total_sum_6.1 = f32[2,1024]{1,0:T(2,128)} custom-call(f32[2,1024]{1,0:T(2,128)} %pad_maximum_fusion.4.x_ref), custom_call_target="tpu_custom_call" | custom-call | tf_op jit(solution)/shard_map/total_sum_6/pallas_call | solution.py:67
  276.4 1.2 slice.149
  278.6 2.0 fusion.16
  280.6 23.1 %all-reduce.6 = (f32[4,2048]{1,0:T(4,128)S(1)}, f32[4]{0:T(128)S(1)}) all-reduce(f32[4,2048]{1,0:T(4,128)S(1)} %fusion.16, f32[4]{0:T(128)S(1)} %convert_reduce_fusion), channel_id=1, replica_groups=mesh['dp'=4,'fsdp'=8] {'fsdp'}, use_global_device_ids=true, to_apply=%region_2.3 | all-reduce | flops 8196 | bytes 65568 | tf_op jit(solution)/shard_map/psum | solution.py:1184
  305.7 1.6 multiply_convert_fusion.1
  307.3 1.6 fusion.25
  309.6 1.9 multiply_reduce_fusion.7
  312.1 9.4 %total_sum_7.1 = f32[2,256]{1,0:T(2,128)} custom-call(f32[2,256]{1,0:T(2,128)} %pad_maximum_fusion.8.x_ref), custom_call_target="tpu_custom_call" | custom-call | tf_op jit(solution)/shard_map/total_sum_7/pallas_call | solution.py:67
  321.5 1.4 add_rsqrt_fusion.1
  323.4 2.6 multiply_reduce_fusion.5
  326.6 10.6 %total_sum_8.1 = f32[2,256]{1,0:T(2,128)} custom-call(f32[2,256]{1,0:T(2,128)} %pad_maximum_fusion.9.x_ref), custom_call_target="tpu_custom_call" | custom-call | tf_op jit(solution)/shard_map/total_sum_8/pallas_call | solution.py:67
  337.1 1.9 fusion.22
  339.1 1.9 multiply_convert_fusion.2
  341.0 1.7 fusion.26
  342.7 2.5 multiply_reduce_fusion.1
  346.1 9.8 %total_sum_9.1 = f32[2,1024]{1,0:T(2,128)} custom-call(f32[2,1024]{1,0:T(2,128)} %pad_maximum_fusion.5.x_ref), custom_call_target="tpu_custom_call" | custom-call | tf_op jit(solution)/shard_map/total_sum_9/pallas_call | solution.py:67
  356.0 1.4 slice_divide_fusion
  357.4 2.9 multiply_convert_fusion
  361.3 12.7 %psum.30 = f32[4,256]{1,0:T(4,128)S(1)} all-reduce(f32[4,256]{1,0:T(4,128)S(1)} %fusion.3), channel_id=1, replica_groups=mesh['dp'=4,'fsdp'=8] {'fsdp'}, use_global_device_ids=true, to_apply=%region_13.14 | all-reduce | flops 1024 | bytes 8192 | tf_op jit(solution)/shard_map/psum | solution.py:1224
  375.3 127.4 %branches_back.1 = (bf16[16,32,2048]{2,1,0:T(8,128)(2,1)}, bf16[28,32,2048]{2,1,0:T(8,128)(2,1)}) custom-call(bf16[16,32,768]{2,1,0:T(8,128)(2,1)} %bitcast.120, bf16[16,544,256]{2,1,0:T(8,128)(2,1)} %get-tuple-element.59.y_ref, bf16[16,544,128]{2,1,0:T(8,128)(2,1)} %get-tuple-element.60.key_ref.key_any, bf16[28,256,256]{2,1,0:T(8,128)(2,1)} %get-tuple-element.61.k_ref, ...), custom_call_target="tpu_custom_call" | custom-call | tf_op jit(solution)/shard_map/branches_back/pallas_call | solution.py:806
  506.0 158.0 %bottleneck_back.1 = (f32[512,2048]{1,0:T(8,128)}, bf16[32,3584]{1,0:T(8,128)(2,1)}, bf16[512,256]{1,0:T(8,128)(2,1)}, bf16[9,64,512]{2,1,0:T(8,128)(2,1)}, bf16...) custom-call(bf16[512,2048]{1,0:T(8,128)(2,1)} %bitcast.115, ...), custom_call_target="tpu_custom_call" | custom-call | tf_op jit(solution)/shard_map/bottleneck_back/pallas_call | solution.py:1110
  664.1 1.0 convert_element_type.92
  666.8 2.2 reshape.195
  675.1 12.8 %all-reduce.9.cloned.1.call-done = bf16[28,32,2048]{2,1,0:T(8,128)(2,1)} async-done(((bf16[28,32,2048]{2,1,0:T(8,128)(2,1)}), bf16[28,32,2048]{2,1,0:T(8,128)(2,1)}) %all-reduce.9.cloned.1.call-update) | async-done | bytes 3670032 | tf_op jit(solution)/shard_map/psum | solution.py:1235
  688.0 2.9 slice.197
  690.9 3.6 slice_bitcast_fusion
  697.5 2.0 copy.119
  (165 shorter events, 29.7 us)
Async XLA Ops:
  7.2 300.1 %all-gather.2.cloned.1.call-start = ((), (), s32[]{:S(2)}) async-start(), calls=%async_computation | async-start | bytes 1179648 | tf_op jit(solution)/shard_map/all_gather | solution.py:1174
  7.9 680.0 %all-reduce.9.cloned.1.call-start = ((), (), s32[]{:S(2)}) async-start(), calls=%async_computation.1 | async-start | bytes 7340032 | tf_op jit(solution)/shard_map/psum | solution.py:1235
  9.1 299.8 %copy-start.25 = (pred[512]{0:T(512)(128)(4,1)}, pred[512]{0:T(512)(128)(4,1)S(1)}, u32[]{:S(2)}) copy-start(pred[512]{0:T(512)(128)(4,1)S(1)} %ge.35) | copy-start | bytes 1540
  11.3 297.7 %copy-start.18 = (s32[512]{0:T(512)}, s32[512]{0:T(512)S(1)}, u32[]{:S(2)}) copy-start(s32[512]{0:T(512)S(1)} %sub.107) | copy-start | bytes 6148
  214.9 47.7 %copy-start.3 = (bf16[256,2048]{1,0:T(8,128)(2,1)S(1)}, bf16[256,2048]{1,0:T(8,128)(2,1)}, u32[]{:S(2)}) copy-start(bf16[256,2048]{1,0:T(8,128)(2,1)} %get-tuple-element.58.wp) | copy-start | bytes 3145732
  265.1 12.5 %copy-start.30 = (s32[8,64]{1,0:T(8,128)S(1)}, s32[8,64]{1,0:T(8,128)}, u32[]{:S(2)}) copy-start(s32[8,64]{1,0:T(8,128)} %param.31) | copy-start | bytes 6148
  265.1 39.8 %copy-start.40 = (f32[256]{0:T(256)S(1)}, f32[256]{0:T(256)}, u32[]{:S(2)}) copy-start(f32[256]{0:T(256)} %param.51) | copy-start | bytes 3076
  265.1 39.8 %copy-start.41 = (f32[256]{0:T(256)S(1)}, f32[256]{0:T(256)}, u32[]{:S(2)}) copy-start(f32[256]{0:T(256)} %param.48) | copy-start | bytes 3076
  265.1 39.8 %copy-start.42 = (f32[256]{0:T(256)S(1)}, f32[256]{0:T(256)}, u32[]{:S(2)}) copy-start(f32[256]{0:T(256)} %param.45) | copy-start | bytes 3076
  265.1 39.8 %copy-start.43 = (f32[256]{0:T(256)S(1)}, f32[256]{0:T(256)}, u32[]{:S(2)}) copy-start(f32[256]{0:T(256)} %param.42) | copy-start | bytes 3076
  265.2 39.7 %copy-start.44 = (f32[256]{0:T(256)S(1)}, f32[256]{0:T(256)}, u32[]{:S(2)}) copy-start(f32[256]{0:T(256)} %param.52) | copy-start | bytes 3076
  265.2 39.7 %copy-start.45 = (f32[256]{0:T(256)S(1)}, f32[256]{0:T(256)}, u32[]{:S(2)}) copy-start(f32[256]{0:T(256)} %param.49) | copy-start | bytes 3076
  265.2 39.7 %copy-start.46 = (f32[256]{0:T(256)S(1)}, f32[256]{0:T(256)}, u32[]{:S(2)}) copy-start(f32[256]{0:T(256)} %param.46) | copy-start | bytes 3076
  265.2 39.7 %copy-start.47 = (f32[256]{0:T(256)S(1)}, f32[256]{0:T(256)}, u32[]{:S(2)}) copy-start(f32[256]{0:T(256)} %param.43) | copy-start | bytes 3076
  276.4 28.6 %copy-start.24 = (f32[2,1024]{1,0:T(2,128)S(1)}, f32[2,1024]{1,0:T(2,128)}, u32[]{:S(2)}) copy-start(f32[2,1024]{1,0:T(2,128)} %total_sum_6.1) | copy-start | bytes 24580
  305.7 3.3 copy-start.14
  305.7 3.9 copy-start.7
  309.6 13.3 %copy-start.33 = (f32[256]{0:T(256)S(1)}, f32[256]{0:T(256)}, u32[]{:S(2)}) copy-start(f32[256]{0:T(256)} %param.55) | copy-start | bytes 3076
  309.6 13.3 %copy-start.39 = (f32[256]{0:T(256)S(1)}, f32[256]{0:T(256)}, u32[]{:S(2)}) copy-start(f32[256]{0:T(256)} %param.56) | copy-start | bytes 3076
  309.6 13.5 %copy-start.13 = (bf16[256,128]{1,0:T(8,128)(2,1)S(1)}, bf16[256,128]{1,0:T(8,128)(2,1)}, u32[]{:S(2)}) copy-start(bf16[256,128]{1,0:T(8,128)(2,1)} %get-tuple-element.64) | copy-start | bytes 196612
  323.4 15.7 %copy-start.34 = (f32[256]{0:T(256)S(1)}, f32[256]{0:T(256)}, u32[]{:S(2)}) copy-start(f32[256]{0:T(256)} %param.55) | copy-start | bytes 3076
  339.0 3.6 copy-start.35
  340.9 4.3 copy-start.5
  357.4 16.6 %copy-start.21 = (f32[4,256]{1,0:T(4,128)S(1)}, f32[4,256]{1,0:T(4,128)}, u32[]{:S(2)}) copy-start(f32[4,256]{1,0:T(4,128)} %copy-done.20) | copy-start | bytes 12292
  357.4 17.2 %copy-start.48 = (f32[8]{0:T(128)S(1)}, f32[8]{0:T(128)}, u32[]{:S(2)}) copy-start(f32[8]{0:T(128)} %pad.27) | copy-start | bytes 100
  664.0 5.0 copy-start.9
  664.0 6.5 copy-start.32
  664.0 7.1 %copy-start.31 = (f32[2,512]{1,0:T(2,128)S(1)}, f32[2,512]{1,0:T(2,128)}, u32[]{:S(2)}) copy-start(f32[2,512]{1,0:T(2,128)} %get-tuple-element.81) | copy-start | bytes 12292
  664.0 7.7 %copy-start.12 = (f32[2,1024]{1,0:T(2,128)S(1)}, f32[2,1024]{1,0:T(2,128)}, u32[]{:S(2)}) copy-start(f32[2,1024]{1,0:T(2,128)} %total_sum_9.1) | copy-start | bytes 24580
  664.1 8.2 %copy-start.27 = (f32[2,2048]{1,0:T(2,128)S(1)}, f32[2,2048]{1,0:T(2,128)}, u32[]{:S(2)}) copy-start(f32[2,2048]{1,0:T(2,128)} %get-tuple-element.83) | copy-start | bytes 49156
  665.1 9.2 %copy-start.8 = (bf16[64,2048]{1,0:T(8,128)(2,1)S(1)}, bf16[64,2048]{1,0:T(8,128)(2,1)}, u32[]{:S(2)}) copy-start(bf16[64,2048]{1,0:T(8,128)(2,1)} %get-tuple-element.78) | copy-start | bytes 786436
  690.9 4.3 copy-start.1
  (19 other events, 36.2 us)
Sparse Core Ops, SparseCore 0:
  9.9 33.1 all-gather.1
  502.9 185.0 all-reduce.8

commit v3 on v2

--- a/solution.py
+++ b/solution.py
@@ -408,6 +408,54 @@
             c.wait_send()
 
 
+class HalfGather:
+    def __init__(self, src, slot, half, sems, d, f):
+        self.src, self.slot, self.half, self.sems, self.d, self.f = src, slot, half, sems, d, f
+
+    def start(self):
+        far_s, far_r, near_s, near_r, side_s, side_r, local = self.sems
+        d, f = self.d, self.f
+        mine = self.slot(f)
+        a = self.half(d % 2)
+        self.far = {
+            k: remote(self.src.at[a], mine.at[a], far_s.at[k], far_r.at[k], d, f ^ (2 * k)) for k in (3, 1, 2)
+        }
+        self.near = [remote(self.src, mine, near_s.at[0], near_r.at[0], d, f ^ 1)]
+        self.own = pltpu.make_async_copy(self.src, mine, local)
+        self.own.start()
+
+    def forward(self):
+        far_s, far_r, near_s, near_r, side_s, side_r, local = self.sems
+        d, f = self.d, self.f
+        a = self.half(d % 2)
+        self.side = {}
+        for k in (1, 2, 3):
+            self.far[k].wait_recv()
+            got = self.slot(f ^ (2 * k)).at[a]
+            self.side[k] = remote(got, got, side_s.at[k], side_r.at[k], d ^ 1, f)
+            self.near.append(remote(got, got, near_s.at[k], near_r.at[k], d, f ^ 1))
+
+    def arrive(self):
+        far_s, far_r, near_s, near_r, side_s, side_r, local = self.sems
+        d, f = self.d, self.f
+        b = self.half(1 - d % 2)
+        for k in (1, 2, 3):
+            self.side[k].wait_recv()
+            got = self.slot(f ^ (2 * k)).at[b]
+            self.near.append(remote(got, got, near_s.at[k + 3], near_r.at[k + 3], d, f ^ 1))
+        self.own.wait()
+        for c in self.near:
+            c.wait_recv()
+
+    def finish(self):
+        for c in list(self.far.values()) + self.near + list(self.side.values()):
+            c.wait_send()
+
+
+def half_sems():
+    return [DMA((4,)), DMA((4,)), DMA((7,)), DMA((7,)), DMA((4,)), DMA((4,)), DMA(())]
+
+
 def gather_sems():
     return [DMA((4,)), DMA((4,)), DMA((4,)), DMA((4,)), DMA(())]
 
@@ -488,19 +536,33 @@
         return lambda g: ref.at[pl.ds(pl.multiple_of(n * g, n), n)]
 
     nr, nd_, ne, np_ = wr_s.shape[0], wd_s.shape[1], we_s.shape[1], wp_s.shape[0]
-    g_key = Gather(kb_ref, lambda g: key.at[:, pl.ds(pl.multiple_of(PAD + h * g, 16), h), :], take(5), d, f)
+    def half(n, lead=()):
+        return lambda a: lead + (pl.ds(pl.multiple_of(n * a, n), n),)
+
     g_wr = Gather(wr_s, rows_of(wr, nr), take(5), d, f)
-    g_wd = Gather(wd_s, lambda g: wd.at[:, pl.ds(pl.multiple_of(nd_ * g, 16), nd_), :], take(5), d, f)
-    g_we = Gather(we_s, lambda g: we.at[:, pl.ds(pl.multiple_of(ne * g, 128), ne)], take(5), d, f)
+    g_wd = [
+        HalfGather(
+            wd_s.at[pl.ds(3 * i, 3)],
+            lambda g, i=i: wd.at[pl.ds(3 * i, 3), pl.ds(pl.multiple_of(nd_ * g, 16), nd_), :],
+            half(nd_ // 2, (slice(None),)), take(7), d, f,
+        )
+        for i in range(3)
+    ]
+    g_we = HalfGather(
+        we_s, lambda g: we.at[:, pl.ds(pl.multiple_of(ne * g, 128), ne)], half(we_s.shape[0] // 2), take(7), d, f
+    )
     g_wp = Gather(wp_s, rows_of(wp_o, np_), take(5), d, f)
     g_wm = Gather(wm_s, rows_of(wm_o, np_), take(5), d, f)
     g_wc = Gather(wc_s, rows_of(wc_o, np_), take(5), d, f)
-    ks, kr, kl, hs, hr, ys, yr, yl, os_ = take(9)
-    sum1, sum2, sum3 = take(6), take(6), take(6)
-
-    g_key.start()
+    ks, kr, kl, zs, zk, hs, hr, ys, yr, yl, os_, qs, qr, kc = take(14)
+    sum1, sum2, sum3 = (Sum(take(6), d, f) for _ in range(3))
+
+    key_sent = [
+        remote(kb_ref, kc.at[f], qs.at[k], qr.at[k], d, f ^ k) for k in (6, 7, 2, 3, 4, 5, 1)
+    ]
+    kc[f] = kb_ref[...]
     g_wr.start()
-    g_wd.start()
+    g_wd[0].start()
     order = lax.broadcasted_iota(jnp.int32, (N, N), 0)
     m, r, q = order % 4, (order // 4) % rows, order // h
     pick = (r * (N // rows) + q * 4 + m) == lax.broadcasted_iota(jnp.int32, (N, N), 1)
@@ -509,10 +571,11 @@
         xp[:, c : c + 256] = nn_dot(pick, x_ref[:, c : c + 256]).astype(jnp.bfloat16)
     key[:, :PAD, :] = jnp.zeros((Q, PAD, 128), jnp.bfloat16)
     key[:, PAD + T :, :] = jnp.zeros((Q, PAD, 128), jnp.bfloat16)
-    g_key.forward()
     g_wr.forward()
-    g_we.start()
+    g_wd[1].start()
+    g_wd[2].start()
     g_wr.arrive()
+    g_wd[0].forward()
     sums, squares = [], []
     for c in range(0, neck, 256):
         a = nt_dot(xp[...], wr[c : c + 256, :])
@@ -521,7 +584,45 @@
         sums.append(s)
         squares.append(t)
     inside = jnp.sum(ins_ref[...], axis=0, keepdims=True)
-    st = sum_all([cat_rows(sums), cat_rows(squares), cat_rows([inside] * (neck // 128))], sum1, d, f)
+    sum1.start([cat_rows(sums), cat_rows(squares), cat_rows([inside] * (neck // 128))])
+    g_we.start()
+    g_wd[1].forward()
+    g_wd[2].forward()
+    kparts = (k_s0, k_s1, k_s2, kp_s)
+
+    def kslot(b, g, lo, n):
+        o = kparts[b].shape[1]
+        return k_o.at[pl.ds(9 * b, kparts[b].shape[0]), pl.ds(pl.multiple_of(o * g + lo, 16), n), :]
+
+    kcp, kfar = [], {}
+
+    def kernels_out(b):
+        src = kparts[b]
+        o = src.shape[1] // 2
+        lo = pl.multiple_of(o * (d % 2), 16)
+        for k in (6, 7, 2, 3, 4, 5):
+            to = pl.ds(pl.multiple_of((f ^ k) * 256, 128), 256)
+            kfar[b, k] = remote(
+                src.at[:, pl.ds(lo, o), to], kslot(b, f, lo, o), ks.at[b, k], kr.at[b, k], d, f ^ k
+            )
+        to = pl.ds(pl.multiple_of((f ^ 1) * 256, 128), 256)
+        kcp.append(remote(src.at[:, :, to], kslot(b, f, 0, 2 * o), ks.at[b, 1], kr.at[b, 1], d, f ^ 1))
+        own = pl.ds(pl.multiple_of(f * 256, 128), 256)
+        c = pltpu.make_async_copy(src.at[:, :, own], kslot(b, f, 0, 2 * o), kl.at[b])
+        c.start()
+        kcp.append(c)
+
+    def kernels_aside(b):
+        o = kparts[b].shape[1] // 2
+        lo = pl.multiple_of(o * (d % 2), 16)
+        for k in (2, 3, 4, 5, 6, 7):
+            kfar[b, k].wait_recv()
+            got = kslot(b, f ^ k, lo, o)
+            kcp.append(remote(got, got, zs.at[b, k], zk.at[b, k], d ^ 1, f))
+
+    sum1.turn()
+    st = sum1.result()
+    g_we.forward()
     count = st[2:3, :]
     cnt_o[...] = jnp.zeros_like(cnt_o)
     cnt_o[0:1, :neck] = count
@@ -537,41 +638,23 @@
         l1[:, w] = lean.astype(jnp.bfloat16)
     up = remote(ext.at[:, pl.ds(e, e)], ext.at[:, pl.ds(e + h, e)], hs.at[0], hr.at[0], d, lax.rem(f + 7, 8))
     down = remote(ext.at[:, pl.ds(h, e)], ext.at[:, pl.ds(0, e)], hs.at[1], hr.at[1], d, lax.rem(f + 1, 8))
-    g_wd.forward()
-    kcp = []
-    for k in (6, 7, 2, 3, 4, 5, 1):
-        for b, src in enumerate((k_s0, k_s1, k_s2, kp_s)):
-            n = src.shape[0]
-            o = src.shape[1]
-            kcp.append(
-                remote(
-                    src.at[:, :, pl.ds(pl.multiple_of((f ^ k) * 256, 128), 256)],
-                    k_o.at[pl.ds(9 * b, n), pl.ds(pl.multiple_of(o * f, 16), o), :],
-                    ks.at[b, k], kr.at[b, k], d, f ^ k,
-                )
-            )
-    for b, src in enumerate((k_s0, k_s1, k_s2, kp_s)):
-        n = src.shape[0]
-        o = src.shape[1]
-        c = pltpu.make_async_copy(
-            src.at[:, :, pl.ds(pl.multiple_of(f * 256, 128), 256)],
-            k_o.at[pl.ds(9 * b, n), pl.ds(pl.multiple_of(o * f, 16), o), :],
-            kl.at[b],
-        )
-        c.start()
-        kcp.append(c)
-    for g in (g_wp, g_wm, g_wc):
-        g.start()
-    g_key.arrive()
+    for c in key_sent:
+        c.wait()
+    for g in range(8):
+        turned = kc[g].T
+        for q in range(Q):
+            key[q, PAD + h * g : PAD + h * g + h, :] = jnp.broadcast_to(turned[:h, q : q + 1], (h, 128)).astype(jnp.bfloat16)
+    for b in range(4):
+        kernels_out(b)
     outs = [(n1, n1_o), (l1, l1_o), (key, key_o), (wr, wr_o)]
     base = pl.multiple_of(PAD + h * f, 16)
     up.wait()
     down.wait()
     outs.append((ext, ext_o))
-    g_wd.arrive()
     outs.append((wd, wd_o))
     a2[...] = jnp.zeros_like(a2)
     for i in range(3):
+        g_wd[i].arrive()
         for j in (1, 0, 2):
             lo, hi = span(j - 1, Q)
             ok = same_crop(
@@ -587,7 +670,10 @@
         s, t = column_sums(a2[:, c : c + 256], ins_ref[...])
         sums.append(s)
         squares.append(t)
-    st = sum_all([cat_rows(sums), cat_rows(squares)], sum2, d, f)
+    sum2.start([cat_rows(sums), cat_rows(squares)])
+    kernels_aside(0)
+    sum2.turn()
+    st = sum2.result()
     mean = st[0:1] / count
     inv = lax.rsqrt(st[1:2] / count - mean * mean + eps)
     cnt_o[2:3, :neck] = inv
@@ -599,7 +685,6 @@
         n2[:, w] = n.astype(jnp.bfloat16)
         l2[:, w] = lean.astype(jnp.bfloat16)
     outs += [(n2, n2_o), (l2, l2_o), (h2, h2_o)]
-    g_we.forward()
     g_we.arrive()
     outs.append((we, we_o))
     sums, squares = [], []
@@ -609,11 +694,16 @@
         s, t = column_sums(a, ins_ref[...])
         sums.append(s)
         squares.append(t)
-    st = sum_all([cat_rows(sums), cat_rows(squares)], sum3, d, f)
+    sum3.start([cat_rows(sums), cat_rows(squares)])
+    kernels_aside(1)
+    sum3.turn()
+    for g in (g_wp, g_wm, g_wc):
+        g.start()
+    st = sum3.result()
     total = count[:, :1]
     mean3 = st[0:1] / total
     inv3 = lax.rsqrt(st[1:2] / total - mean3 * mean3 + eps)
-    coef = sum3[0]
+    coef = sum3.b1
     coef[0, 0:1, :] = mean3
     coef[0, 1:2, :] = inv3
     cnt_o[3:4, :] = inv3
@@ -636,6 +726,8 @@
             sent.append(own)
     outs += [(y, y_o), (n3, n3_o), (l3, l3_o)]
     saved = []
+    kernels_aside(2)
+    kernels_aside(3)
     for n, (src, to) in enumerate(outs):
         c = pltpu.make_async_copy(src, to, os_.at[n])
         c.start()
@@ -644,15 +736,18 @@
         g.forward()
     for g in (g_wp, g_wm, g_wc):
         g.arrive()
-    for g in (g_key, g_wr, g_wd, g_we, g_wp, g_wm, g_wc):
+    for g in [g_wr, g_we, g_wp, g_wm, g_wc] + g_wd:
         g.finish()
+    for c in kfar.values():
+        c.wait_send()
     for c in kcp + sent + saved:
         c.wait()
 
 
 def bottleneck(x, kb, ins, vecs, shards, kparts):
     N, C = x.shape
-    Q, h, _ = kb.shape
+    Q = kb.shape[0]
+    h = N // Q
     wr, wd, we, wp, wm, wc = shards
     neck = we.shape[0]
     W = 8 * wp.shape[0]
@@ -673,9 +768,9 @@
         V((N, neck), b16), V((N, neck), b16), V((N, neck), b16), V((N, neck), b16), V((Q, TT, 128), b16),
         V((neck, C), b16), V((9, neck, neck), b16), V((neck, C), b16),
     ]
-    for _ in range(7):
-        scratch += gather_sems()
-    scratch += [DMA((4, 8)), DMA((4, 8)), DMA((4,)), DMA((2,)), DMA((2,)), DMA((8,)), DMA((8,)), DMA(()), DMA((16,))]
+    scratch += gather_sems() + half_sems() * 4 + gather_sems() * 3
+    scratch += [DMA((4, 8)), DMA((4, 8)), DMA((4,)), DMA((4, 8)), DMA((4, 8)), DMA((2,)), DMA((2,)), DMA((8,)), DMA((8,)), DMA(()), DMA((16,))]
+    scratch += [DMA((8,)), DMA((8,)), V((8, Q, 128), f32)]
     scratch += sum_sems(3, neck) + sum_sems(2, neck) + sum_sems(2, C)
     return pl.pallas_call(
         bottleneck_kernel,
@@ -690,30 +785,80 @@
 
 def branches_back_kernel(
     steps, d_ref, y_ref, key_ref, k_ref, pooled_ref, dr_ref, size_ref, dy_o, gk_o,
-    g, gt, x, gk, dyo, acc, gp, *sems,
+    g, gt, x, gk, fin, in1, in2, dyo, acc, gp, *sems,
 ):
     sems = list(sems)
-    f, d = greet(range(1, 8), ())
+    f, d = greet(range(1, 8), range(1, 4))
     Q, h, w = y_ref.shape[0], d_ref.shape[1], y_ref.shape[2]
     W = k_ref.shape[1]
     T = 8 * h
     o = W // 8
-    g_d = Gather(d_ref, lambda n: g.at[:, pl.ds(pl.multiple_of(PAD + h * n, 16), h), :], sems[:5], d, f)
-    ws, wr, wl, ds_, dr_, dl = sems[5:]
-    g_d.start()
+    taps = gk.shape[0]
+    gathers = [
+        Gather(
+            d_ref.at[:, :, pl.ds(b * W, W)],
+            lambda n, b=b: g.at[:, pl.ds(pl.multiple_of(PAD + h * n, 16), h), pl.ds(b * W, W)],
+            sems[5 * b : 5 * b + 5], d, f,
+        )
+        for b in range(3)
+    ]
+    ws, wr, wl, ds_, dr_, dl, s1, r1, s2, r2, s3, r3 = sems[15:]
+    for c in gathers:
+        c.start()
+    outer = d % 3 == 0
+
+    def to_inner(t):
+        return pltpu.make_async_remote_copy(
+            src_ref=gk.at[t], dst_ref=in1.at[t], send_sem=s1.at[t], recv_sem=r1.at[t],
+            device_id=(d ^ 1, f), device_id_type=MESH,
+        )
+
+    def across(t):
+        return pltpu.make_async_remote_copy(
+            src_ref=gk.at[t], dst_ref=in2.at[t], send_sem=s2.at[t], recv_sem=r2.at[t],
+            device_id=(d ^ 3, f), device_id_type=MESH,
+        )
+
+    def to_outer(t):
+        return pltpu.make_async_remote_copy(
+            src_ref=fin.at[t], dst_ref=fin.at[t], send_sem=s3.at[t], recv_sem=r3.at[t],
+            device_id=(d ^ 1, f), device_id_type=MESH,
+        )
+
+    def hand(t):
+        @pl.when(outer)
+        def _():
+            to_inner(t).start()
+
+    def first(t):
+        @pl.when(jnp.logical_not(outer))
+        def _():
+            to_inner(t).wait_recv()
+            gk[t] = (gk[t].astype(jnp.float32) + in1[t].astype(jnp.float32)).astype(gk.dtype)
+            across(t).start()
+
+    def second(t):
+        @pl.when(jnp.logical_not(outer))
+        def _():
+            across(t).wait_recv()
+            fin[t] = (gk[t].astype(jnp.float32) + in2[t].astype(jnp.float32)).astype(fin.dtype)
+            to_outer(t).start()
+
+        @pl.when(outer)
+        def _():
+            to_outer(t).wait_recv()
+
     gk[27] = tn_dot(dr_ref[...], pooled_ref[...]).astype(gk.dtype)
     gp[...] = nn_dot(dr_ref[...], k_ref[27]) / size_ref[:, :1]
-    g_d.forward()
-    g_d.arrive()
-
-    def turn(q, _):
-        for b in range(3):
+    for b, s in enumerate(steps):
+        gathers[b].forward()
+        gathers[b].arrive()
+
+        def turn(q, _):
             gt[b * W : (b + 1) * W, pl.ds(pl.multiple_of(q * T, 256), T)] = g[q, PAD : PAD + T, b * W : (b + 1) * W].T
-        return 0
-
-    lax.fori_loop(0, Q, turn, 0)
-    cps = []
-    for b, s in enumerate(steps):
+            return 0
+
+        lax.fori_loop(0, Q, turn, 0)
         for i in (-1, 0, 1):
             for j in (-1, 0, 1):
                 lo, hi = span(s * j, Q)
@@ -725,19 +870,20 @@
                     return 0
 
                 lax.fori_loop(lo, hi, one, 0)
-                gk[9 * b + 3 * (i + 1) + j + 1] = nn_dot(
+                t = 9 * b + 3 * (i + 1) + j + 1
+                gk[t] = nn_dot(
                     gt[b * W : (b + 1) * W, lo * T : hi * T], x[: (hi - lo) * T, :]
                 ).astype(gk.dtype)
-        n = 9 if b < 2 else 10
-        for k in (6, 7, 2, 3, 4, 5, 1, 0):
-            src = gk.at[pl.ds(9 * b, n), pl.ds(pl.multiple_of(o * (f ^ k), 16), o), :]
-            dst = gk_o.at[pl.ds(9 * b, n), :, pl.ds(pl.multiple_of(w * f, 128), w)]
-            if k:
-                cps.append(remote(src, dst, ws.at[b, k], wr.at[b, k], d, f ^ k))
-            else:
-                c = pltpu.make_async_copy(src, dst, wl.at[b])
-                c.start()
-                cps.append(c)
+                hand(t)
+    hand(27)
+    cps = []
+    ready = 4
+
+    def lead(t, _):
+        first(t)
+        return 0
+
+    lax.fori_loop(0, ready, lead, 0)
 
     dst = dy_o.at[:, :, pl.ds(pl.multiple_of(w * f, 128), w)]
 
@@ -747,6 +893,7 @@
     def dest_step(m, _):
         k = 7 - m
         dest = f ^ k
+        first(ready + m)
         base = pl.multiple_of(PAD + h * dest, 16)
         here = key_ref[:, pl.ds(base, h), :].astype(jnp.float32).reshape(Q * h, 128)
         here = jnp.concatenate([here] * (w // 128), axis=1)
@@ -754,21 +901,8 @@
         for c in range(CROPS_TILE):
             total = jnp.where(here == c + 1.0, gp[c : c + 1, :], total)
         acc[...] = total
-        for b, s in enumerate(steps):
-            for i in (-1, 0, 1):
-                first = h * dest - 16 * s * i
-
-                @pl.when((first + h > 0) & (first < T))
-                def _():
-                    at = pl.multiple_of(base - 16 * s * i, 16)
-                    for j in (-1, 0, 1):
-                        lo, hi = span(-s * j, Q)
-                        ok = same_crop(
-                            key_ref[lo:hi, pl.ds(base, h), :], key_ref[lo - s * j : hi - s * j, pl.ds(at, h), :], W
-                        )
-                        v = jnp.where(ok, g[lo - s * j : hi - s * j, pl.ds(at, h), b * W : (b + 1) * W], 0)
-                        acc[lo * h : hi * h] += nn_dot(v.reshape((hi - lo) * h, W), k_ref[9 * b + 3 * (i + 1) + j + 1])
-
+        for b in range(3):
+            spaced_taps(g, key_ref, k_ref, acc, base, h, steps, -1, b * W, nn_dot, b)
         rows = rows_of(k)
         dyo[:, rows, :] = acc[...].reshape(Q, h, w).astype(dyo.dtype)
         src = dyo.at[:, rows, :]
@@ -784,6 +918,28 @@
         return 0
 
     lax.fori_loop(0, 8, dest_step, 0)
+    done = ready + 8
+
+    def first_when(t):
+        @pl.when(t < taps)
+        def _():
+            first(t)
+
+    groups = (9, 9, 5, 5)
+    at = 0
+    for n, size in enumerate(groups):
+        stop = at + size
+        lax.fori_loop(at, stop, lambda t, _: (first_when(t + done), second(t), 0)[-1], 0)
+        for k in (6, 7, 2, 3, 4, 5, 1, 0):
+            src = fin.at[pl.ds(at, size), pl.ds(pl.multiple_of(o * (f ^ k), 16), o), :]
+            to = gk_o.at[pl.ds(at, size), :, pl.ds(pl.multiple_of(w * f, 128), w)]
+            if k:
+                cps.append(remote(src, to, ws.at[n, k], wr.at[n, k], d, f ^ k))
+            else:
+                c = pltpu.make_async_copy(src, to, wl.at[n])
+                c.start()
+                cps.append(c)
+        at = stop
     for k in range(1, 8):
         c = pltpu.make_async_remote_copy(
             src_ref=dyo.at[:, rows_of(k), :], dst_ref=dst, send_sem=ds_.at[k], recv_sem=dr_.at[k],
@@ -791,9 +947,24 @@
         )
         c.wait()
     pltpu.make_async_copy(dyo.at[:, rows_of(0), :], dst, dl).wait()
-    g_d.finish()
+    for c in gathers:
+        c.finish()
     for c in cps:
         c.wait()
+
+    def sent(t, _):
+        @pl.when(outer)
+        def _():
+            to_inner(t).wait_send()
+
+        @pl.when(jnp.logical_not(outer))
+        def _():
+            across(t).wait_send()
+            to_outer(t).wait_send()
+
+        return 0
+
+    lax.fori_loop(0, taps, sent, 0)
 
 
 def branches_back(d, y, key, k, pooled, dr, sizes, steps):
@@ -809,11 +980,13 @@
         in_specs=[VM] * 7,
         out_specs=[ANY] * 2,
         scratch_shapes=[
-            V((Q, TT, W3), b16), V((W3, Q * T), b16), V((Q * T, w), b16), V((28, W, w), b16), V((Q, T, w), b16),
+            V((Q, TT, W3), b16), V((W3, Q * T), b16), V((Q * T, w), b16), V((28, W, w), b16), V((28, W, w), b16),
+            V((28, W, w), b16), V((28, W, w), b16), V((Q, T, w), b16),
             V((Q * h, w), f32), V((8, w), f32),
         ]
-        + gather_sems()
-        + [DMA((3, 8)), DMA((3, 8)), DMA((3,)), DMA((8,)), DMA((8,)), DMA(())],
+        + gather_sems() * 3
+        + [DMA((4, 8)), DMA((4, 8)), DMA((4,)), DMA((8,)), DMA((8,)), DMA(())]
+        + [DMA((28,))] * 6,
         compiler_params=pltpu.CompilerParams(collective_id=10, has_side_effects=True, vmem_limit_bytes=VLIM),
         name="branches_back",
     )(d, y, key, k, pooled, dr, sizes)
@@ -1118,6 +1291,229 @@
     )(*args)
 
 
+def spaced_taps(src, key, kernels, acc, base, h, steps, sign, first_lane, dot, b):
+    Q = key.shape[0]
+    s = sign * steps[b]
+    W = kernels.shape[1] if sign < 0 else src.shape[2]
+    lanes = slice(first_lane, first_lane + W)
+    for n, j in enumerate((0, -1, 1)):
+        lo, hi = span(s * j, Q)
+        here = key[lo:hi, pl.ds(base, h), :]
+        got = None
+        for i in (-1, 0, 1):
+            at = pl.multiple_of(base + 16 * s * i, 16)
+            ok = same_crop(here, key[lo + s * j : hi + s * j, pl.ds(at, h), :], W)
+            v = jnp.where(ok, src[lo + s * j : hi + s * j, pl.ds(at, h), lanes], 0).reshape((hi - lo) * h, W)
+            r = dot(v, kernels[9 * b + 3 * (i + 1) + j + 1])
+            got = r if got is None else got + r
+        if n == 0 and sign > 0:
+            acc[...] = got
+        else:
+            acc[lo * h : hi * h] += got
+
+
+def head_kernel(
+    steps, yo, key, kern, y, wp, wm, wc, ins_ref, kb, lab, st_ref, gb, bb, gm, bm,
+    lo_o, dp_o, dr_o, pm_o, pooled_o, dpool_o, size_o, sb_o, sm_o,
+    acc, near, mine, far, ab, nb, lb, joined, nm, lm, merged, pn, ps, pr, ss, rs,
+    *sems,
+):
+    sems = list(sems)
+    f, d = greet(range(1, 8), range(1, 4))
+    sum_b, sum_m, back_m, back_b = (Sum(sems[6 * n : 6 * n + 6], d, f) for n in range(4))
+    Q, h = pn.shape[1], pn.shape[2]
+    N = Q * h
+    w = yo.shape[2]
+    W = wp.shape[0]
+    T = 8 * h
+    c0 = f % 2
+    me = f // 2
+    f32, b16 = jnp.float32, jnp.bfloat16
+
+    def step(n, _):
+        k = 3 - n
+        g = me ^ k
+        for turn in range(2):
+            dest = 2 * g + (1 - c0 if turn == 0 else c0)
+            base = pl.multiple_of(PAD + h * dest, 16)
+            if turn == 1:
+                pltpu.make_async_remote_copy(
+                    src_ref=pn.at[k], dst_ref=near.at[k], send_sem=ps.at[k], recv_sem=pr.at[k],
+                    device_id=(d, f ^ 1), device_id_type=MESH,
+                ).wait_recv()
+            for b in range(3):
+                lanes = slice(b * W, (b + 1) * W)
+                spaced_taps(yo, key, kern, acc, base, h, steps, 1, 0, nt_dot, b)
+                if turn == 0:
+                    pn[k, :, :, lanes] = acc[...].astype(b16).reshape(Q, h, W)
+                else:
+                    val = acc[...] + near[k, :, :, lanes].astype(f32).reshape(N, W)
+                    mine[k, :, :, lanes] = val.astype(b16).reshape(Q, h, W)
+            if turn == 0:
+                remote(pn.at[k], near.at[k], ps.at[k], pr.at[k], d, f ^ 1)
+            else:
+
+                @pl.when(k > 0)
+                def _():
+                    remote(mine.at[k], far.at[k], ss.at[k], rs.at[k], d, f ^ (2 * k))
+
+        return 0
+
+    lax.fori_loop(0, 4, step, 0)
+    ab[:, :W] = nt_dot(y[...], wp[...])
+    crop = (lax.broadcasted_iota(jnp.int32, (T, 128), 1) + 1).astype(f32)
+
+    def crops(q, carry):
+        total, size = carry
+        one = (key[q, PAD : PAD + T, :].astype(f32) == crop).astype(f32).astype(b16)
+        return total + tn_dot(one, yo[q, PAD : PAD + T, :]), size + tn_dot(one, jnp.ones((T, 128), b16))
+
+    total, size = lax.fori_loop(0, Q, crops, (jnp.zeros((128, w), f32), jnp.zeros((128, 128), f32)))
+    size = jnp.where(size > 0, size, 1.0)[:8]
+    size_o[...] = size
+    pooled = (total[:8] / size[:, :1]).astype(b16)
+    pooled_o[...] = pooled
+    part = nt_dot(pooled, kern[27])
+    part = cat_rows([part[c : c + 1] for c in range(CROPS_TILE)])
+    ins = wide(ins_ref[...], 2)
+    for k in (3, 1, 2):
+        pltpu.make_async_remote_copy(
+            src_ref=mine.at[k], dst_ref=far.at[k], send_sem=ss.at[k], recv_sem=rs.at[k],
+            device_id=(d, f ^ (2 * k)), device_id_type=MESH,
+        ).wait()
+    ones, squares = [], []
+    for b in range(4):
+        lanes = slice(b * W, (b + 1) * W)
+        if b:
+            src = slice((b - 1) * W, b * W)
+            v = mine[0, :, :, src].astype(f32)
+            for k in (1, 2, 3):
+                v = v + far[k, :, :, src].astype(f32)
+            ab[:, lanes] = v.reshape(N, W)
+        s, t = column_sums(ab[:, lanes], ins_ref[...])
+        ones.append(s)
+        squares.append(t)
+    sum_b.start([cat_rows(ones), cat_rows(squares), part])
+    for k in range(4):
+        pltpu.make_async_remote_copy(
+            src_ref=pn.at[k], dst_ref=near.at[k], send_sem=ps.at[k], recv_sem=pr.at[k],
+            device_id=(d, f ^ 1), device_id_type=MESH,
+        ).wait_send()
+    sum_b.turn()
+    pool_act = sum_b.b2[d, 2:3, :]
+    pool, pool_lean = bend(pool_act)
+    pool = pool.astype(b16).astype(f32)
+    here = wide(kb[...].astype(f32), W // 128)
+    v = jnp.zeros((N, W), f32)
+    for c in range(CROPS_TILE):
+        v = jnp.where(here == c + 1.0, pool[:, c * W : (c + 1) * W], v)
+    joined[:, 4 * W :] = v.astype(b16)
+    tot = sum_b.result()
+    count = st_ref[0:1, 0:1]
+    mean = tot[0:1] / count
+    inv_b = lax.rsqrt(tot[1:2] / count - mean * mean + eps)
+    for b in range(4):
+        lanes = slice(b * W, (b + 1) * W)
+        n = (ab[:, lanes] - mean[:, lanes]) * inv_b[:, lanes]
+        act, lean = bend(n * gb[:, lanes] + bb[:, lanes])
+        joined[:, lanes] = act.astype(b16)
+        nb[:, lanes] = n.astype(b16)
+        lb[:, lanes] = lean.astype(b16)
+    am = nt_dot(joined[...], wm[...])
+    s, t = column_sums(am, ins_ref[...])
+    sum_m.start([s, t])
+    sum_m.turn()
+    tot = sum_m.result()
+    mean = tot[0:1] / count
+    inv_m = lax.rsqrt(tot[1:2] / count - mean * mean + eps)
+    n = (am - mean) * inv_m
+    act, lean = bend(n * gm[...] + bm[...])
+    merged[...] = act.astype(b16)
+    nm[...] = n
+    lm[...] = lean
+    logits = nn_dot(merged[...], wc[...])
+    lane = lax.broadcasted_iota(jnp.int32, (N, 128), 1)
+    valid = lane < CLASSES
+    top = jnp.max(jnp.where(valid, logits, -jnp.inf), axis=1, keepdims=True)
+    ex = jnp.where(valid, jnp.exp(logits - top), 0.0)
+    prob = ex / jnp.sum(ex, axis=1, keepdims=True)
+    target = (lab[...] == lane.astype(f32)).astype(f32)
+    dl = (ins_ref[...] * (prob - target) / count).astype(b16)
+    e = nt_dot(dl, wc[...]) * lm[...]
+    m = e * ins
+    back_m.start([jnp.sum(m, axis=0, keepdims=True), jnp.sum(m * nm[...], axis=0, keepdims=True)])
+    order = lax.broadcasted_iota(jnp.int32, (N, N), 1)
+    rows = h // 4
+    mm, r, q = order % 4, (order // 4) % rows, order // h
+    hit = (r * (N // rows) + q * 4 + mm) == lax.broadcasted_iota(jnp.int32, (N, N), 0)
+    lo_o[...] = nn_dot(hit.astype(f32).astype(b16), logits.astype(b16)).astype(b16)
+    back_m.turn()
+    J = joined.shape[1]
+    pm_o[:, J : J + 128] = tn_dot(merged[...], dl).astype(b16)
+    pm_o[:, J + 128 :] = jnp.zeros((W, pm_o.shape[1] - J - 128), b16)
+    tot = back_m.result()
+    sm_o[...] = tot
+    dm = (ins * gm[...] * inv_m * (e - tot[0:1] / count - nm[...] * (tot[1:2] / count))).astype(b16)
+    ones, crossed = [], []
+    for b in range(4):
+        lanes = slice(b * W, (b + 1) * W)
+        v = nn_dot(dm, wm[:, lanes]) * lb[:, lanes].astype(f32)
+        ab[:, lanes] = v
+        v = v * ins
+        ones.append(jnp.sum(v, axis=0, keepdims=True))
+        crossed.append(jnp.sum(v * nb[:, lanes].astype(f32), axis=0, keepdims=True))
+    v = nn_dot(dm, wm[:, 4 * W :])
+    part = cat_rows(
+        [jnp.sum(jnp.where(here == c + 1.0, v, 0.0), axis=0, keepdims=True) for c in range(CROPS_TILE)]
+    )
+    back_b.start([cat_rows(ones), cat_rows(crossed), part])
+    pm_o[:, :J] = tn_dot(dm, joined[...]).astype(b16)
+    back_b.turn()
+    v = (back_b.b2[d, 2:3, :] * pool_lean).astype(b16)
+    dpool_o[...] = jnp.zeros_like(dpool_o)
+    for c in range(CROPS_TILE):
+        dpool_o[c : c + 1, :] = v[:, c * W : (c + 1) * W]
+    tot = back_b.result()
+    sb_o[...] = tot[:2]
+    for b in range(4):
+        lanes = slice(b * W, (b + 1) * W)
+        v = ab[:, lanes] - tot[0:1, lanes] / count - nb[:, lanes].astype(f32) * (tot[1:2, lanes] / count)
+        v = (ins * v * (gb[:, lanes] * inv_b[:, lanes])).astype(b16)
+        if b:
+            dr_o[:, :, (b - 1) * W : b * W] = v.reshape(Q, h, W)
+        else:
+            dp_o[...] = v
+
+
+def head(steps, width, *args):
+    yo, key, kern, y, wp, wm = args[:6]
+    N, C = y.shape
+    Q = yo.shape[0]
+    h = N // Q
+    W = wp.shape[0]
+    J = wm.shape[1]
+    b16, f32 = jnp.bfloat16, jnp.float32
+    S, V = jax.ShapeDtypeStruct, pltpu.VMEM
+    return pl.pallas_call(
+        functools.partial(head_kernel, steps),
+        out_shape=[
+            S((N, 128), b16), S((N, W), b16), S((Q, h, 3 * W), b16), S((W, width), b16), S((8, C // 8), b16),
+            S((8, W), b16), S((8, 128), f32), S((2, 4 * W), f32), S((2, W), f32),
+        ],
+        in_specs=[VM] * 15,
+        out_specs=[VM] * 9,
+        scratch_shapes=[V((N, W), f32)]
+        + [V((4, Q, h, 3 * W), b16)] * 3
+        + [
+            V((N, 4 * W), f32), V((N, 4 * W), b16), V((N, 4 * W), b16), V((N, J), b16), V((N, W), f32), V((N, W), f32),
+            V((N, W), b16), V((4, Q, h, 3 * W), b16), DMA((4,)), DMA((4,)), DMA((4,)), DMA((4,)),
+        ]
+        + sum_sems(3, 4 * W) + sum_sems(2, W) + sum_sems(2, W) + sum_sems(3, 4 * W),
+        compiler_params=pltpu.CompilerParams(collective_id=5, has_side_effects=True, vmem_limit_bytes=VLIM),
+        name="head",
+    )(*args)
+
+
 def norm_coeffs(totals, squares, count):
     average = totals / count
     return average, lax.rsqrt(squares / count - average * average + eps)
@@ -1150,7 +1546,8 @@
     in_crop = perm(crop_ids) >= 0
     inside = in_crop.astype(jnp.float32)[:, None]
     key_loc = jnp.where(in_crop, local_crop + 1, 0)
-    kb = jnp.broadcast_to(key_loc.astype(jnp.bfloat16)[:, None], (N, 128)).reshape(Q, h, 128)
+    kb = jnp.broadcast_to(key_loc.astype(jnp.bfloat16)[:, None], (N, 128))
+    key_row = jnp.pad(key_loc.astype(jnp.float32).reshape(Q, h), ((0, 0), (0, 128 - h)))
     ins = jnp.broadcast_to(inside, (N, 128))
     rates = [jnp.swapaxes(w.reshape(9, C, -1), 1, 2) for w in (w_rate, w_rate_double, w_rate_triple)]
     vecs = [v[None, :] for v in (gain_reduce, bias_reduce, gain_dilated, bias_dilated, gain_expand, bias_expand)]
@@ -1158,7 +1555,7 @@
         y_own, y, n_three, l_three, n_one, l_one, n_two, l_two, ext, h_two, key, kernel,
         wr, wd, full_expand, wp, wm, wc, count,
     ) = bottleneck(
-        features.reshape(N, C), kb, ins, vecs,
+        features.reshape(N, C), key_row, ins, vecs,
         [
             w_reduce.T, jnp.swapaxes(w_dilated.reshape(9, w_dilated.shape[2], -1), 1, 2), w_expand, w_point.T, w_merge.T,
             jnp.pad(w_classes, ((0, 0), (0, 128 - CLASSES))),
@@ -1169,76 +1566,22 @@
     stats = count
     count = count[0, 0]
     y = y.reshape(N, C)
-    full_reduce, full_point, full_merge, full_classes = wr.T, wp.T, wm.T, wc[:, :CLASSES]
-    neck = gain_reduce.shape[0]
-    full_pool = lax.all_gather(w_pool, "fsdp", axis=1, tiled=True)
-
-    part = conv_forward(y_own, key, kernel[:27], steps)
-    a_rates = scatter_sum(part.reshape(nf, N, 3 * W), 5)
-    a_point = flat_dot(y, full_point)
-    a_br = jnp.concatenate([a_point, a_rates], axis=1)
-    member = local_crop[:, None] == jnp.arange(CROPS_TILE)[None, :]
-    member = (member & in_crop[:, None]).astype(jnp.bfloat16)
-    crop_sums = inner_dot(member, y)
-    crop_sizes = jnp.sum(member.astype(jnp.float32), axis=0)
-    crop_sums, crop_sizes = lax.psum((crop_sums, crop_sizes), "fsdp")
-    st = total_sum([jnp.sum(a_br * inside, axis=0), jnp.sum(a_br * a_br * inside, axis=0)], 6)
-    m_br, s_br = norm_coeffs(st[0], st[1], count)
-    g_br = jnp.concatenate([gain_point, gain_rate, gain_rate_double, gain_rate_triple])
-    b_br = jnp.concatenate([bias_point, bias_rate, bias_rate_double, bias_rate_triple])
-    n_br = (a_br - m_br) * s_br
-    p_br = n_br * g_br + b_br
-    u_br = jax.nn.silu(p_br).astype(jnp.bfloat16)
-    pooled = (crop_sums / crop_sizes[:, None]).astype(jnp.bfloat16)
-    pool_act = flat_dot(pooled, full_pool)
-    pool_low = jax.nn.silu(pool_act).astype(jnp.bfloat16)
-    u_pool = flat_dot(member, pool_low).astype(jnp.bfloat16)
-    joined = jnp.concatenate([u_br, u_pool], axis=1)
-    a_merge = flat_dot(joined, full_merge)
-    st = total_sum([jnp.sum(a_merge * inside, axis=0), jnp.sum(a_merge * a_merge * inside, axis=0)], 7)
-    m_merge, s_merge = norm_coeffs(st[0], st[1], count)
-    n_merge = (a_merge - m_merge) * s_merge
-    p_merge = n_merge * gain_merge + bias_merge
-    merged = jax.nn.silu(p_merge).astype(jnp.bfloat16)
-    logits = flat_dot(merged, full_classes)
-    class_logits = unperm(logits.astype(jnp.bfloat16))
-
-    probability = jax.nn.softmax(logits, axis=1)
-    targets = (perm(labels)[:, None] == jnp.arange(CLASSES)[None, :]).astype(jnp.float32)
-    d_logits = (inside * (probability - targets) / count).astype(jnp.bfloat16)
-    grad_classes = inner_dot(merged, d_logits)
-
-    def back(up, n, s, gain, cid):
-        st = total_sum([jnp.sum(up * inside, axis=0), jnp.sum(up * n * inside, axis=0)], cid)
-        d = inside * gain * s * (up - st[0] / count - n * st[1] / count)
-        return d.astype(jnp.bfloat16), st[1], st[0]
-
-    d_merge, gg_merge, gb_merge = back(outer_dot(d_logits, full_classes) * slope(p_merge), n_merge, s_merge, gain_merge, 8)
-    grad_merge = inner_dot(joined, d_merge)
-    d_joined = outer_dot(d_merge, full_merge)
-    d_br, gg_br, gb_br = back(d_joined[:, : 4 * W] * slope(p_br), n_br, s_br, g_br, 9)
-    crop_grad = lax.dot_general(
-        member.astype(jnp.float32), d_joined[:, 4 * W :], (((0,), (0,)), ((), ())),
-        precision=lax.Precision.HIGHEST, preferred_element_type=jnp.float32,
-    )
-    crop_grad = lax.psum(crop_grad, "fsdp")
-    d_pool = (crop_grad * slope(pool_act)).astype(jnp.bfloat16)
-
-    def eight(a):
-        return jnp.pad(a, ((0, 8 - a.shape[0]), (0, 0)))
-
-    pooled_own = lax.dynamic_slice_in_dim(pooled, place * (C // nf), C // nf, axis=1)
-    sizes = jnp.broadcast_to(jnp.pad(crop_sizes, (0, 8 - CROPS_TILE), constant_values=1.0)[:, None], (8, 128))
-    d_y, grad_k = branches_back(
-        d_br[:, W:].reshape(Q, h, 3 * W), y_own, key, kernel, eight(pooled_own), eight(d_pool), sizes, steps
-    )
-    grad_k = lax.psum(grad_k, "dp").astype(jnp.float32)
-    rest = jnp.concatenate(
-        [grad_merge.T, jnp.pad(grad_classes, ((0, 0), (0, 128 - CLASSES)))], axis=1
-    ).astype(jnp.bfloat16)
-    rest = jnp.pad(rest, ((0, 0), (0, -(C + rest.shape[1]) % 512)))
+    g_br = jnp.concatenate([gain_point, gain_rate, gain_rate_double, gain_rate_triple])[None]
+    b_br = jnp.concatenate([bias_point, bias_rate, bias_rate_double, bias_rate_triple])[None]
+    lab = jnp.broadcast_to(perm(labels).astype(jnp.float32)[:, None], (N, 128))
+    J = wm.shape[1]
+    width = J + 128 + -(C + J + 128) % 512
+    logits, d_point, d_rates, rest, pooled, d_pool, sizes, st_br, st_m = head(
+        steps, width, y_own, key, kernel, y, wp, wm, wc, ins, kb, lab, stats, g_br, b_br,
+        gain_merge[None], bias_merge[None],
+    )
+    class_logits = logits[:, :CLASSES].reshape(rows, cols, CLASSES)
+    gb_br, gg_br = st_br[0], st_br[1]
+    gb_merge, gg_merge = st_m[0], st_m[1]
+    d_y, grad_k = branches_back(d_rates, y_own, key, kernel, pooled, d_pool, sizes, steps)
+    grad_k = grad_k.astype(jnp.float32)
     grad_features, pm, ex, di, re_, st3, st2, st1 = bottleneck_back(
-        features.reshape(N, C), ins, stats, vecs[0], vecs[2], vecs[4], d_y.reshape(N, C), d_br[:, :W], y, rest, wp,
+        features.reshape(N, C), ins, stats, vecs[0], vecs[2], vecs[4], d_y.reshape(N, C), d_point, y, rest, wp,
         n_three, l_three, full_expand, n_two, l_two, h_two, wd, ext, n_one, l_one, wr, key,
     )
     pm = pm.astype(jnp.float32)

time: 716 us -> 555 us (0.78)
  Pallas kernels: 570 us -> 511 us
  blocking collectives: 35.8 us -> 0 us
  other arithmetic: 24.9 us -> 10.4 us
  matrix products: 14.3 us -> 0 us
  between operations: 15 us -> 1.26 us
  waiting for transfers between devices: 13.5 us -> 0 us
  local copies, waits for them, and re-layouts: 32.8 us -> 23.2 us
    pallas_call x1, Pallas kernels: 127 us -> 186 us  [branches_back(): pl.pallas_call(functools.partial(branches_back_kernel, steps), out_shape=...]
    pallas_call x1, Pallas kernels: 170 us -> 125 us  [bottleneck(): pl.pallas_call(bottleneck_kernel, out_shape=outs, in_specs=[VM] * 9 + [AN...]
    pallas_call x1, Pallas kernels: 158 us -> 117 us  [bottleneck_back(): pl.pallas_call(bottleneck_back_kernel, out_shape=[S((N, C), f32)] + [S(b,...]
    psum x2 -> x0, blocking collectives: 35.8 us -> none  [the longest x1 23.1 us: fast_body(): crop_sums, crop_sizes = lax.psum((crop_sums, crop_sizes), 'fsdp')]
    pallas_call x6 -> x1, Pallas kernels: 115 us -> 83.2 us  [head(): pl.pallas_call(functools.partial(head_kernel, steps), out_shape=[S((N, 12...]
    dot_general x11 -> x0, matrix products: 14.3 us -> none  [the longest x5 6.46 us: flat_dot(): return jnp.dot(first_op, second_op, preferred_element_type=jnp.float32)]
    psum x1 -> x0, waiting for transfers between devices: 12.8 us -> none  [fast_body(): grad_k = lax.psum(grad_k, 'dp').astype(jnp.float32)]
    slice x5 -> x0, local copies, waits for them, and re-layouts: 7.63 us -> none  [the longest x1 4.17 us: fast_body(): part = conv_forward(y_own, key, kernel[:27], steps)]
  transfers between devices with their start and end apart: 2 -> 0, of which waited for: 1 -> 0; matrix products, arithmetic and copies ran while one was open for 5% -> 0% of each run, Pallas kernels for 58% -> 0%
where the time goes in v3:
time: 555 us; the launch traced here: 546 us
  Pallas kernels  511 us (92%)
  local copies, waits for them, and re-layouts  23.2 us (4%)
  other arithmetic  10.4 us (2%)
    pallas_call x1, Pallas kernels, branches_back(): pl.pallas_call(functools.partial(branches_back_kernel, steps), out_shape=...  186 us
    pallas_call x1, Pallas kernels, bottleneck(): pl.pallas_call(bottleneck_kernel, out_shape=outs, in_specs=[VM] * 9 + [AN...  125 us
    pallas_call x1, Pallas kernels, bottleneck_back(): pl.pallas_call(bottleneck_back_kernel, out_shape=[S((N, C), f32)] + [S(b,...  117 us
    pallas_call x1, Pallas kernels, head(): pl.pallas_call(functools.partial(head_kernel, steps), out_shape=[S((N, 12...  83.2 us

profile of v3, /device:TPU:0, one launch (start us, length us, event | category | flops | bytes accessed | tf_op | source)
XLA Modules:
  0.0 545.7 jit_solution(6724461848222672745)
XLA Ops:
  0.7 0.7 fusion
  1.6 0.6 pad.8.kb_ref
  2.2 0.7 compare_convert_fusion
  3.3 0.8 broadcast_in_dim.53.ins_ref
  4.1 0.8 copy.66
  4.9 0.6 pad.9.wc_s
  5.6 125.1 %bottleneck.1 = (bf16[16,544,256]{2,1,0:T(8,128)(2,1)}, bf16[16,32,2048]{2,1,0:T(8,128)(2,1)}, bf16[512,2048]{1,0:T(8,128)(2,1)}, bf16[512,2048]{1,0:T(8,128)(2,...) custom-call(bf16[512,2048]{1,0:T(8,128)(2,1)} %bitcast.86, ...), custom_call_target="tpu_custom_call" | custom-call | tf_op jit(solution)/shard_map/bottleneck/pallas_call | solution.py:775
  130.8 0.2 copy.68
  131.1 0.8 broadcast_in_dim.61.kb
  132.3 0.8 broadcast_in_dim.62.lab
  133.2 0.6 pad_maximum_fusion
  133.8 0.6 pad_maximum_fusion.1
  134.4 83.2 %head.1 = (bf16[512,128]{1,0:T(8,128)(2,1)}, bf16[512,256]{1,0:T(8,128)(2,1)}, bf16[16,32,768]{2,1,0:T(8,128)(2,1)}, bf16[256,1536]{1,0:T(8,128)(2,1)}, bf16[8,2...) custom-call(bf16[16,544,256]{2,1,0:T(8,128)(2,1)} %get-tuple-element.66, ...), custom_call_target="tpu_custom_call" | custom-call | tf_op jit(solution)/shard_map/head/pallas_call | solution.py:1497
  217.6 1.7 copy.71
  219.2 186.0 %branches_back.1 = (bf16[16,32,2048]{2,1,0:T(8,128)(2,1)}, bf16[28,32,2048]{2,1,0:T(8,128)(2,1)}) custom-call(bf16[16,32,768]{2,1,0:T(8,128)(2,1)} %get-tuple-element.75.d_ref, bf16[16,544,256]{2,1,0:T(8,128)(2,1)} %get-tuple-element.66.yo.y_ref, bf16[16,544,128]{2,1,0:T(8,128)(2,1)} %get-tuple-element.67.key.key_ref.key_any, ...), custom_call_target="tpu_custom_call" | custom-call | tf_op jit(solution)/shard_map/branches_back/pallas_call | solution.py:977
  405.2 116.6 %bottleneck_back.1 = (f32[512,2048]{1,0:T(8,128)}, bf16[32,3584]{1,0:T(8,128)(2,1)}, bf16[512,256]{1,0:T(8,128)(2,1)}, bf16[9,64,512]{2,1,0:T(8,128)(2,1)}, bf16...) custom-call(bf16[512,2048]{1,0:T(8,128)(2,1)} %bitcast.87, ...), custom_call_target="tpu_custom_call" | custom-call | tf_op jit(solution)/shard_map/bottleneck_back/pallas_call | solution.py:1283
  521.8 1.9 convert_bitcast_fusion
  523.8 1.4 fusion.4
  525.1 2.2 reshape.179
  527.3 1.8 convert_element_type.69
  529.1 1.4 fusion.2
  530.5 1.0 convert_element_type.70
  531.5 0.7 slice_bitcast_fusion.4
  532.2 0.6 fusion.3
  532.8 0.9 slice.143
  533.8 3.1 slice_bitcast_fusion
  536.9 0.9 convert_element_type.71
  537.8 0.7 slice_bitcast_fusion.3
  538.5 0.7 slice_bitcast_fusion.5
  539.2 0.7 slice.149
  539.9 0.7 copy.72
  540.6 4.7 copy.74
  (36 shorter events, 1.2 us)
Async XLA Ops:
  5.5 126.4 %copy-start.2 = (s32[8,64]{1,0:T(8,128)S(1)}, s32[8,64]{1,0:T(8,128)}, u32[]{:S(2)}) copy-start(s32[8,64]{1,0:T(8,128)} %param.31) | copy-start | bytes 6148
  5.5 127.6 %copy-start.4 = (f32[256]{0:T(256)S(1)}, f32[256]{0:T(256)}, u32[]{:S(2)}) copy-start(f32[256]{0:T(256)} %param.51) | copy-start | bytes 3076
  5.5 127.6 %copy-start.5 = (f32[256]{0:T(256)S(1)}, f32[256]{0:T(256)}, u32[]{:S(2)}) copy-start(f32[256]{0:T(256)} %param.48) | copy-start | bytes 3076
  5.5 127.7 %copy-start.6 = (f32[256]{0:T(256)S(1)}, f32[256]{0:T(256)}, u32[]{:S(2)}) copy-start(f32[256]{0:T(256)} %param.45) | copy-start | bytes 3076
  5.5 127.6 %copy-start.7 = (f32[256]{0:T(256)S(1)}, f32[256]{0:T(256)}, u32[]{:S(2)}) copy-start(f32[256]{0:T(256)} %param.42) | copy-start | bytes 3076
  5.5 128.2 %copy-start.8 = (f32[256]{0:T(256)S(1)}, f32[256]{0:T(256)}, u32[]{:S(2)}) copy-start(f32[256]{0:T(256)} %param.52) | copy-start | bytes 3076
  5.5 128.2 %copy-start.9 = (f32[256]{0:T(256)S(1)}, f32[256]{0:T(256)}, u32[]{:S(2)}) copy-start(f32[256]{0:T(256)} %param.49) | copy-start | bytes 3076
  5.6 128.2 %copy-start.10 = (f32[256]{0:T(256)S(1)}, f32[256]{0:T(256)}, u32[]{:S(2)}) copy-start(f32[256]{0:T(256)} %param.46) | copy-start | bytes 3076
  5.6 128.2 %copy-start.11 = (f32[256]{0:T(256)S(1)}, f32[256]{0:T(256)}, u32[]{:S(2)}) copy-start(f32[256]{0:T(256)} %param.43) | copy-start | bytes 3076
  521.8 10.4 %copy-start.1 = (f32[2,1024]{1,0:T(2,128)S(1)}, f32[2,1024]{1,0:T(2,128)}, u32[]{:S(2)}) copy-start(f32[2,1024]{1,0:T(2,128)} %get-tuple-element.101) | copy-start | bytes 24580
  521.8 10.4 %copy-start.3 = (f32[2,256]{1,0:T(2,128)S(1)}, f32[2,256]{1,0:T(2,128)}, u32[]{:S(2)}) copy-start(f32[2,256]{1,0:T(2,128)} %get-tuple-element.103) | copy-start | bytes 6148
  521.8 11.0 %copy-start = (bf16[28,32,2048]{2,1,0:T(8,128)(2,1)S(1)}, bf16[28,32,2048]{2,1,0:T(8,128)(2,1)}, u32[]{:S(2)}) copy-start(bf16[28,32,2048]{2,1,0:T(8,128)(2,1)} %get-tuple-element.102) | copy-start | bytes 11010052

commit v4 on v3

--- a/solution.py
+++ b/solution.py
@@ -595,33 +595,39 @@
         return k_o.at[pl.ds(9 * b, kparts[b].shape[0]), pl.ds(pl.multiple_of(o * g + lo, 16), n), :]
 
     kcp, kfar = [], {}
-
-    def kernels_out(b):
-        src = kparts[b]
-        o = src.shape[1] // 2
-        lo = pl.multiple_of(o * (d % 2), 16)
-        for k in (6, 7, 2, 3, 4, 5):
+    pieces = [(b, k) for b in range(3) for k in (6, 7, 2, 3, 4, 5)]
+
+    def out(*ns):
+        for b, k in [pieces[n] for n in ns]:
+            src = kparts[b]
+            o = src.shape[1] // 2
+            lo = pl.multiple_of(o * (d % 2), 16)
             to = pl.ds(pl.multiple_of((f ^ k) * 256, 128), 256)
             kfar[b, k] = remote(
                 src.at[:, pl.ds(lo, o), to], kslot(b, f, lo, o), ks.at[b, k], kr.at[b, k], d, f ^ k
             )
-        to = pl.ds(pl.multiple_of((f ^ 1) * 256, 128), 256)
-        kcp.append(remote(src.at[:, :, to], kslot(b, f, 0, 2 * o), ks.at[b, 1], kr.at[b, 1], d, f ^ 1))
-        own = pl.ds(pl.multiple_of(f * 256, 128), 256)
-        c = pltpu.make_async_copy(src.at[:, :, own], kslot(b, f, 0, 2 * o), kl.at[b])
-        c.start()
-        kcp.append(c)
-
-    def kernels_aside(b):
-        o = kparts[b].shape[1] // 2
-        lo = pl.multiple_of(o * (d % 2), 16)
-        for k in (2, 3, 4, 5, 6, 7):
+
+    def aside(*ns):
+        for b, k in [pieces[n] for n in ns]:
+            o = kparts[b].shape[1] // 2
+            lo = pl.multiple_of(o * (d % 2), 16)
             kfar[b, k].wait_recv()
             got = kslot(b, f ^ k, lo, o)
             kcp.append(remote(got, got, zs.at[b, k], zk.at[b, k], d ^ 1, f))
 
+    for b, src in enumerate(kparts):
+        o = src.shape[1]
+        for k in (6, 7, 2, 3, 4, 5, 1) if b == 3 else (1,):
+            to = pl.ds(pl.multiple_of((f ^ k) * 256, 128), 256)
+            kcp.append(remote(src.at[:, :, to], kslot(b, f, 0, o), ks.at[b, k], kr.at[b, k], d, f ^ k))
+        own = pl.ds(pl.multiple_of(f * 256, 128), 256)
+        c = pltpu.make_async_copy(src.at[:, :, own], kslot(b, f, 0, o), kl.at[b])
+        c.start()
+        kcp.append(c)
     sum1.turn()
+    out(0, 1)
     st = sum1.result()
+    out(2, 3)
     g_we.forward()
     count = st[2:3, :]
     cnt_o[...] = jnp.zeros_like(cnt_o)
@@ -644,8 +650,6 @@
         turned = kc[g].T
         for q in range(Q):
             key[q, PAD + h * g : PAD + h * g + h, :] = jnp.broadcast_to(turned[:h, q : q + 1], (h, 128)).astype(jnp.bfloat16)
-    for b in range(4):
-        kernels_out(b)
     outs = [(n1, n1_o), (l1, l1_o), (key, key_o), (wr, wr_o)]
     base = pl.multiple_of(PAD + h * f, 16)
     up.wait()
@@ -665,15 +669,19 @@
             v = jnp.where(ok, ext[lo + j - 1 : hi + j - 1, e * i : e * i + h, :], 0).reshape((hi - lo) * h, neck)
             for c in range(0, neck, 256):
                 a2[lo * h : hi * h, c : c + 256] += nt_dot(v, wd[3 * i + j, c : c + 256, :])
+            if (3 * i + j) % 2 == 0 and i < 2 + (j == 0):
+                out(4 + (3 * i + j) // 2)
     sums, squares = [], []
     for c in range(0, neck, 256):
         s, t = column_sums(a2[:, c : c + 256], ins_ref[...])
         sums.append(s)
         squares.append(t)
     sum2.start([cat_rows(sums), cat_rows(squares)])
-    kernels_aside(0)
+    aside(0, 1, 2, 3)
     sum2.turn()
+    out(8, 9)
     st = sum2.result()
+    out(10)
     mean = st[0:1] / count
     inv = lax.rsqrt(st[1:2] / count - mean * mean + eps)
     cnt_o[2:3, :neck] = inv
@@ -689,14 +697,20 @@
     outs.append((we, we_o))
     sums, squares = [], []
     for c in range(0, C, 256):
+        n = c // 256
+        if n % 2 == 0:
+            out(11 + n // 2)
+        else:
+            aside(4 + n // 2)
         a = nn_dot(h2[...], we[:, c : c + 256])
         a3[:, c : c + 256] = a
         s, t = column_sums(a, ins_ref[...])
         sums.append(s)
         squares.append(t)
     sum3.start([cat_rows(sums), cat_rows(squares)])
-    kernels_aside(1)
+    aside(8, 9)
     sum3.turn()
+    out(15, 16, 17)
     for g in (g_wp, g_wm, g_wc):
         g.start()
     st = sum3.result()
@@ -709,7 +723,8 @@
     cnt_o[3:4, :] = inv3
     sent = []
     dst = yo_o.at[:, pl.ds(base, h), :]
-    for k in (6, 7, 2, 3, 4, 5, 1, 0):
+    for m, k in enumerate((6, 7, 2, 3, 4, 5, 1, 0)):
+        aside(10 + m)
         g = f ^ k
         w = pl.ds(pl.multiple_of(g * 256, 256), 256)
         n = (a3[:, w] - coef[0, 0:1, w]) * coef[0, 1:2, w]
@@ -726,8 +741,6 @@
             sent.append(own)
     outs += [(y, y_o), (n3, n3_o), (l3, l3_o)]
     saved = []
-    kernels_aside(2)
-    kernels_aside(3)
     for n, (src, to) in enumerate(outs):
         c = pltpu.make_async_copy(src, to, os_.at[n])
         c.start()
@@ -785,7 +798,7 @@
 
 def branches_back_kernel(
     steps, d_ref, y_ref, key_ref, k_ref, pooled_ref, dr_ref, size_ref, dy_o, gk_o,
-    g, gt, x, gk, fin, in1, in2, dyo, acc, gp, *sems,
+    g, gt, gk, fin, in1, in2, dyo, acc, gp, *sems,
 ):
     sems = list(sems)
     f, d = greet(range(1, 8), range(1, 4))
@@ -793,7 +806,7 @@
     W = k_ref.shape[1]
     T = 8 * h
     o = W // 8
-    taps = gk.shape[0]
+    taps = gk.shape[0] // 2
     gathers = [
         Gather(
             d_ref.at[:, :, pl.ds(b * W, W)],
@@ -807,21 +820,24 @@
         c.start()
     outer = d % 3 == 0
 
+    def two(ref, t):
+        return ref.at[pl.ds(2 * t, 2)]
+
     def to_inner(t):
         return pltpu.make_async_remote_copy(
-            src_ref=gk.at[t], dst_ref=in1.at[t], send_sem=s1.at[t], recv_sem=r1.at[t],
+            src_ref=two(gk, t), dst_ref=two(in1, t), send_sem=s1.at[t], recv_sem=r1.at[t],
             device_id=(d ^ 1, f), device_id_type=MESH,
         )
 
     def across(t):
         return pltpu.make_async_remote_copy(
-            src_ref=gk.at[t], dst_ref=in2.at[t], send_sem=s2.at[t], recv_sem=r2.at[t],
+            src_ref=two(gk, t), dst_ref=two(in2, t), send_sem=s2.at[t], recv_sem=r2.at[t],
             device_id=(d ^ 3, f), device_id_type=MESH,
         )
 
     def to_outer(t):
         return pltpu.make_async_remote_copy(
-            src_ref=fin.at[t], dst_ref=fin.at[t], send_sem=s3.at[t], recv_sem=r3.at[t],
+            src_ref=two(fin, t), dst_ref=two(fin, t), send_sem=s3.at[t], recv_sem=r3.at[t],
             device_id=(d ^ 1, f), device_id_type=MESH,
         )
 
@@ -834,14 +850,16 @@
         @pl.when(jnp.logical_not(outer))
         def _():
             to_inner(t).wait_recv()
-            gk[t] = (gk[t].astype(jnp.float32) + in1[t].astype(jnp.float32)).astype(gk.dtype)
+            for n in (2 * t, 2 * t + 1):
+                gk[n] = (gk[n].astype(jnp.float32) + in1[n].astype(jnp.float32)).astype(gk.dtype)
             across(t).start()
 
     def second(t):
         @pl.when(jnp.logical_not(outer))
         def _():
             across(t).wait_recv()
-            fin[t] = (gk[t].astype(jnp.float32) + in2[t].astype(jnp.float32)).astype(fin.dtype)
+            for n in (2 * t, 2 * t + 1):
+                fin[n] = (gk[n].astype(jnp.float32) + in2[n].astype(jnp.float32)).astype(fin.dtype)
             to_outer(t).start()
 
         @pl.when(outer)
@@ -864,26 +882,21 @@
                 lo, hi = span(s * j, Q)
                 a = PAD + 16 * s * i
 
-                def one(q, _):
+                got = None
+                for q in range(lo, hi):
                     ok = same_crop(key_ref[q, PAD : PAD + T, :], key_ref[q + s * j, a : a + T, :], w)
-                    x[pl.ds(pl.multiple_of((q - lo) * T, 256), T), :] = jnp.where(ok, y_ref[q + s * j, a : a + T, :], 0)
-                    return 0
-
-                lax.fori_loop(lo, hi, one, 0)
+                    v = jnp.where(ok, y_ref[q + s * j, a : a + T, :], 0)
+                    r = nn_dot(gt[b * W : (b + 1) * W, q * T : (q + 1) * T], v)
+                    got = r if got is None else got + r
                 t = 9 * b + 3 * (i + 1) + j + 1
-                gk[t] = nn_dot(
-                    gt[b * W : (b + 1) * W, lo * T : hi * T], x[: (hi - lo) * T, :]
-                ).astype(gk.dtype)
-                hand(t)
-    hand(27)
+                gk[t] = got.astype(gk.dtype)
+                if t % 2:
+                    hand(t // 2)
+                if b == 2 and t % 2:
+                    first((t - 18) // 2)
+    hand(13)
     cps = []
     ready = 4
-
-    def lead(t, _):
-        first(t)
-        return 0
-
-    lax.fori_loop(0, ready, lead, 0)
 
     dst = dy_o.at[:, :, pl.ds(pl.multiple_of(w * f, 128), w)]
 
@@ -893,10 +906,14 @@
     def dest_step(m, _):
         k = 7 - m
         dest = f ^ k
-        first(ready + m)
         base = pl.multiple_of(PAD + h * dest, 16)
         here = key_ref[:, pl.ds(base, h), :].astype(jnp.float32).reshape(Q * h, 128)
         here = jnp.concatenate([here] * (w // 128), axis=1)
+        @pl.when(m % 2 == 1)
+        def _():
+            first(ready + m // 2)
+            second(m // 2)
+
         total = jnp.zeros((Q * h, w), jnp.float32)
         for c in range(CROPS_TILE):
             total = jnp.where(here == c + 1.0, gp[c : c + 1, :], total)
@@ -918,21 +935,20 @@
         return 0
 
     lax.fori_loop(0, 8, dest_step, 0)
-    done = ready + 8
 
     def first_when(t):
         @pl.when(t < taps)
         def _():
             first(t)
 
-    groups = (9, 9, 5, 5)
+    groups = (4, 5, 3, 2)
     at = 0
     for n, size in enumerate(groups):
         stop = at + size
-        lax.fori_loop(at, stop, lambda t, _: (first_when(t + done), second(t), 0)[-1], 0)
+        lax.fori_loop(max(at, 4), stop, lambda t, _: (first_when(t + ready), second(t), 0)[-1], 0)
         for k in (6, 7, 2, 3, 4, 5, 1, 0):
-            src = fin.at[pl.ds(at, size), pl.ds(pl.multiple_of(o * (f ^ k), 16), o), :]
-            to = gk_o.at[pl.ds(at, size), :, pl.ds(pl.multiple_of(w * f, 128), w)]
+            src = fin.at[pl.ds(2 * at, 2 * size), pl.ds(pl.multiple_of(o * (f ^ k), 16), o), :]
+            to = gk_o.at[pl.ds(2 * at, 2 * size), :, pl.ds(pl.multiple_of(w * f, 128), w)]
             if k:
                 cps.append(remote(src, to, ws.at[n, k], wr.at[n, k], d, f ^ k))
             else:
@@ -980,13 +996,13 @@
         in_specs=[VM] * 7,
         out_specs=[ANY] * 2,
         scratch_shapes=[
-            V((Q, TT, W3), b16), V((W3, Q * T), b16), V((Q * T, w), b16), V((28, W, w), b16), V((28, W, w), b16),
+            V((Q, TT, W3), b16), V((W3, Q * T), b16), V((28, W, w), b16), V((28, W, w), b16),
             V((28, W, w), b16), V((28, W, w), b16), V((Q, T, w), b16),
             V((Q * h, w), f32), V((8, w), f32),
         ]
         + gather_sems() * 3
         + [DMA((4, 8)), DMA((4, 8)), DMA((4,)), DMA((8,)), DMA((8,)), DMA(())]
-        + [DMA((28,))] * 6,
+        + [DMA((14,))] * 6,
         compiler_params=pltpu.CompilerParams(collective_id=10, has_side_effects=True, vmem_limit_bytes=VLIM),
         name="branches_back",
     )(d, y, key, k, pooled, dr, sizes)
@@ -1023,13 +1039,12 @@
 
 
 class Reduce:
-    def __init__(self, full, part, near, far, tot, zr, out, quarter, sems, d, f):
-        self.full, self.part, self.near, self.fars, self.tot, self.zr, self.out = full, part, near, far, tot, zr, out
-        self.quarter, self.d, self.f = quarter, d, f
+    def __init__(self, full, part, near, far, tot, zin, zo, out, sems, d, f):
+        self.full, self.part, self.near, self.fars, self.tot, self.out = full, part, near, far, tot, out
+        self.zin, self.zo, self.d, self.f = zin, zo, d, f
         self.sems = sems
         self.c0 = f % 2
         self.me = f // 2
-        self.sent = []
 
     def pair(self):
         ps, pr = self.sems[:2]
@@ -1052,41 +1067,70 @@
                     remote(self.near.at[g], self.fars.at[k], ss.at[k], rs.at[k], self.d, self.f ^ (2 * k))
                 )
 
+    def to_inner(self):
+        ss, rs = self.sems[4:6]
+        return pltpu.make_async_remote_copy(
+            src_ref=self.tot, dst_ref=self.zin, send_sem=ss.at[0], recv_sem=rs.at[0],
+            device_id=(self.d ^ 1, self.f), device_id_type=MESH,
+        )
+
+    def across(self):
+        ss, rs = self.sems[4:6]
+        return pltpu.make_async_remote_copy(
+            src_ref=self.tot, dst_ref=self.zo, send_sem=ss.at[1], recv_sem=rs.at[1],
+            device_id=(self.d ^ 3, self.f), device_id_type=MESH,
+        )
+
+    def to_outer(self):
+        ss, rs = self.sems[4:6]
+        return pltpu.make_async_remote_copy(
+            src_ref=self.out, dst_ref=self.out, send_sem=ss.at[2], recv_sem=rs.at[2],
+            device_id=(self.d ^ 1, self.f), device_id_type=MESH,
+        )
+
     def tiles(self):
-        ss, rs = self.sems[4:6]
         for c in self.cps:
             c.wait()
         val = self.near[self.me].astype(jnp.float32)
         for k in (1, 2, 3):
             val = val + self.fars[k].astype(jnp.float32)
         self.tot[...] = val.astype(self.tot.dtype)
-        self.cps = [
-            remote(self.tot.at[self.quarter(self.d ^ k)], self.zr.at[self.d], ss.at[k], rs.at[k], self.d ^ k, self.f)
-            for k in (3, 2, 1)
-        ]
-        self.zr[self.d] = self.tot[self.quarter(self.d)]
-
-    def back(self):
-        ss, rs = self.sems[6:8]
-        for c in self.cps:
-            c.wait()
-        val = self.zr[0].astype(jnp.float32)
-        for k in (1, 2, 3):
-            val = val + self.zr[k].astype(jnp.float32)
-        mine = self.quarter(self.d)
-        self.out[mine] = val.astype(self.out.dtype)
-        self.cps = [
-            remote(self.out.at[mine], self.out.at[mine], ss.at[k], rs.at[k], self.d ^ k, self.f) for k in (3, 2, 1)
-        ]
+
+        @pl.when(self.d % 3 == 0)
+        def _():
+            self.to_inner().start()
+
+    def middle(self):
+        @pl.when(self.d % 3 > 0)
+        def _():
+            self.to_inner().wait_recv()
+            val = self.tot[...].astype(jnp.float32) + self.zin[...].astype(jnp.float32)
+            self.tot[...] = val.astype(self.tot.dtype)
+            self.across().start()
+
+    def last(self):
+        @pl.when(self.d % 3 > 0)
+        def _():
+            self.across().wait_recv()
+            val = self.tot[...].astype(jnp.float32) + self.zo[...].astype(jnp.float32)
+            self.out[...] = val.astype(self.out.dtype)
+            self.to_outer().start()
 
     def done(self):
-        for c in self.cps:
-            c.wait()
-
-
-def reduce_scratch(block, quarter):
+        @pl.when(self.d % 3 == 0)
+        def _():
+            self.to_inner().wait_send()
+            self.to_outer().wait_recv()
+
+        @pl.when(self.d % 3 > 0)
+        def _():
+            self.across().wait_send()
+            self.to_outer().wait_send()
+
+
+def reduce_scratch(block):
     V, b16 = pltpu.VMEM, jnp.bfloat16
-    return [V((4,) + block, b16), V((4,) + block, b16), V(block, b16), V((4,) + quarter, b16)] + [DMA((4,))] * 8
+    return [V((4,) + block, b16), V((4,) + block, b16), V(block, b16), V(block, b16), V(block, b16)] + [DMA((4,))] * 6
 
 
 def wide(row, n):
@@ -1114,22 +1158,21 @@
     neck = acc.shape[1]
     nb = neck // 8
     nw = pm.shape[0] // 8
-    PW = pm.shape[1] // 4
     W = dpt.shape[1]
 
     def ds(i, n):
         return pl.ds(pl.multiple_of(n * i, n), n)
 
-    def reducer(full, part, out, quarter):
-        near, far, tot, zr = take(4)
-        return Reduce(full, part, near, far, tot, zr, out, quarter, take(8), d, f)
-
-    r_pm = reducer(pm, lambda g: (ds(g, nw),), pm_o, lambda g: (slice(None), ds(g, PW)))
-    r_ex = reducer(ex, lambda g: (slice(None), ds(g, C // 8)), ex_o, lambda g: (ds(g, neck // 4),))
-    r_di = reducer(
-        di, lambda g: (slice(None), ds(g, nb)), di_o, lambda g: (slice(None), ds(g, nb // 4))
-    )
-    r_re = reducer(re_, lambda g: (ds(g, nb),), re_o, lambda g: (ds(g, nb // 4),))
+    def reducer(full, part, out):
+        near, far, tot, zin, zo = take(5)
+        return Reduce(full, part, near, far, tot, zin, zo, out, take(6), d, f)
+
+    r_pm = reducer(pm, lambda g: (ds(g, nw),), pm_o)
+    r_ex = reducer(ex, lambda g: (slice(None), ds(g, C // 8)), ex_o)
+    r_di = [
+        reducer(di.at[pl.ds(3 * i, 3)], lambda g: (slice(None), ds(g, nb)), di_o.at[pl.ds(3 * i, 3)]) for i in range(3)
+    ]
+    r_re = reducer(re_, lambda g: (ds(g, nb),), re_o)
     sum3, sum2, sum1 = (Sum(take(6), d, f) for _ in range(3))
 
     kcp = pltpu.make_async_copy(key_any.at[:, pl.ds(pl.multiple_of(PAD - e + h * f, 16), 2 * h), :], key, ksem)
@@ -1196,8 +1239,9 @@
             v = jnp.where(ok, ext[lo + j - 1 : hi + j - 1, e * i : e * i + h, :], 0).reshape((hi - lo) * h, neck)
             g = ext2[lo:hi, e : e + h, :].reshape((hi - lo) * h, neck)
             di[3 * i + j] = tn_dot(g, v).astype(jnp.bfloat16)
-    r_di.pair()
+        r_di[i].pair()
     up.wait()
+    r_pm.middle()
     down.wait()
     acc[...] = jnp.zeros_like(acc)
     for i in range(3):
@@ -1219,9 +1263,10 @@
         ones.append(jnp.sum(v, axis=0, keepdims=True))
         crossed.append(jnp.sum(v * n1[:, w].astype(jnp.float32), axis=0, keepdims=True))
     sum1.start([cat_rows(ones), cat_rows(crossed)])
-    r_di.far()
+    for r in r_di:
+        r.far()
     sum1.turn()
-    r_pm.back()
+    r_pm.last()
     r_ex.tiles()
     tot = sum1.result()
     s1_o[...] = tot
@@ -1233,6 +1278,9 @@
     for c in range(0, C, 256):
         re_[:, c : c + 256] = tn_dot(d1n[...], x_ref[:, c : c + 256]).astype(jnp.bfloat16)
     r_re.pair()
+    r_di[0].tiles()
+    r_re.far()
+    r_ex.middle()
     out = []
     for n, c in enumerate(range(0, C, 256)):
         w = slice(c, c + 256)
@@ -1243,17 +1291,24 @@
         cp.start()
         out.append(cp)
         if n == 1:
-            r_re.far()
+            r_di[0].middle()
+            r_ex.last()
         if n == 3:
-            r_ex.back()
+            r_di[1].tiles()
+            r_di[0].last()
         if n == 5:
-            r_di.tiles()
+            r_di[1].middle()
+        if n == 7:
+            r_di[2].tiles()
+            r_di[1].last()
+    r_di[2].middle()
     r_re.tiles()
-    r_di.back()
-    r_re.back()
+    r_di[2].last()
+    r_re.middle()
+    r_re.last()
     out[-2].wait()
     out[-1].wait()
-    for r in (r_pm, r_ex, r_di, r_re):
+    for r in [r_pm, r_ex, r_re] + r_di:
         r.done()
 
 
@@ -1266,23 +1321,18 @@
     PM = C + pm_in.shape[1]
     b16, f32 = jnp.bfloat16, jnp.float32
     S, V = jax.ShapeDtypeStruct, pltpu.VMEM
-    blocks = [
-        ((W // 8, PM), (W // 8, PM // 4)),
-        ((neck, C // 8), (neck // 4, C // 8)),
-        ((9, neck // 8, neck), (9, neck // 32, neck)),
-        ((neck // 8, C), (neck // 32, C)),
-    ]
+    blocks = [(W // 8, PM), (neck, C // 8), (9, neck // 8, neck), (neck // 8, C)]
     scratch = [
         V((W, PM), b16), V((neck, C), b16), V((9, neck, neck), b16), V((neck, C), b16), V((N, C), b16), V((N, C), b16),
         V((N, neck), f32), V((Q, 2 * h, neck), b16), V((N, neck), b16), V((Q, 2 * h, 128), b16), V((2, N, 256), f32),
         V((N, N), b16), DMA(()), DMA((2,)), DMA((2,)), DMA((2,)),
     ]
-    for block, quarter in blocks:
-        scratch += reduce_scratch(block, quarter)
+    for n in (0, 1, 2, 2, 2, 3):
+        scratch += reduce_scratch((3,) + blocks[2][1:] if n == 2 else blocks[n])
     scratch += sum_sems(2, C) + sum_sems(2, neck) + sum_sems(2, neck)
     return pl.pallas_call(
         bottleneck_back_kernel,
-        out_shape=[S((N, C), f32)] + [S(b, b16) for b, _ in blocks] + [S((2, C), f32), S((2, neck), f32), S((2, neck), f32)],
+        out_shape=[S((N, C), f32)] + [S(b, b16) for b in blocks] + [S((2, C), f32), S((2, neck), f32), S((2, neck), f32)],
         in_specs=[VM] * 22 + [ANY],
         out_specs=[ANY] + [VM] * 7,
         scratch_shapes=scratch,
@@ -1514,6 +1564,41 @@
     )(*args)
 
 
+def widen_kernel(gk, pm, ex, di, re_, k0, k1, k2, pool, point, merge, dilated, expand, reduce_):
+    for b, o in enumerate((k0, k1, k2)):
+
+        def tap(t, _):
+            o[t] = gk[9 * b + t].astype(jnp.float32)
+            return 0
+
+        lax.fori_loop(0, 9, tap, 0)
+    pool[...] = gk[27].astype(jnp.float32)
+    C = point.shape[1]
+    point[...] = pm[:, :C].astype(jnp.float32)
+    merge[...] = pm[:, C : C + merge.shape[1]].astype(jnp.float32)
+
+    def rows(t, _):
+        dilated[t] = di[t].astype(jnp.float32)
+        return 0
+
+    lax.fori_loop(0, 9, rows, 0)
+    expand[...] = ex[...].astype(jnp.float32)
+    reduce_[...] = re_[...].astype(jnp.float32)
+
+
+def widen(gk, pm, ex, di, re_, J):
+    _, o, C = gk.shape
+    shapes = [(9, o, C)] * 3 + [(o, C), (o, C), (o, J), di.shape, ex.shape, re_.shape]
+    return pl.pallas_call(
+        widen_kernel,
+        out_shape=[jax.ShapeDtypeStruct(v, jnp.float32) for v in shapes],
+        in_specs=[VM] * 5,
+        out_specs=[VM] * 9,
+        compiler_params=pltpu.CompilerParams(vmem_limit_bytes=VLIM),
+        name="widen",
+    )(gk, pm, ex, di, re_)
+
+
 def norm_coeffs(totals, squares, count):
     average = totals / count
     return average, lax.rsqrt(squares / count - average * average + eps)
@@ -1579,20 +1664,17 @@
     gb_br, gg_br = st_br[0], st_br[1]
     gb_merge, gg_merge = st_m[0], st_m[1]
     d_y, grad_k = branches_back(d_rates, y_own, key, kernel, pooled, d_pool, sizes, steps)
-    grad_k = grad_k.astype(jnp.float32)
     grad_features, pm, ex, di, re_, st3, st2, st1 = bottleneck_back(
         features.reshape(N, C), ins, stats, vecs[0], vecs[2], vecs[4], d_y.reshape(N, C), d_point, y, rest, wp,
         n_three, l_three, full_expand, n_two, l_two, h_two, wd, ext, n_one, l_one, wr, key,
     )
-    pm = pm.astype(jnp.float32)
-    grad_point, grad_merge, grad_classes = pm[:, :C].T, pm[:, C : C + 5 * W].T, pm[:, C + 5 * W : C + 5 * W + CLASSES]
+    grad_classes = pm[:, C + J : C + J + CLASSES].astype(jnp.float32)
+    *grad_k, grad_pool, grad_point, grad_merge, grad_dilated, grad_expand, grad_reduce = widen(grad_k, pm, ex, di, re_, J)
+    grad_k = [jnp.swapaxes(v.reshape(3, 3, -1, C), 2, 3) for v in grad_k]
+    grad_pool, grad_point, grad_merge, grad_reduce = grad_pool.T, grad_point.T, grad_merge.T, grad_reduce.T
+    grad_dilated = jnp.swapaxes(grad_dilated, 1, 2).reshape(3, 3, neck, -1)
     grad_features = grad_features.reshape(rows, cols, C)
-    grad_reduce = re_.astype(jnp.float32).T
-    grad_dilated = jnp.swapaxes(di.astype(jnp.float32), 1, 2).reshape(3, 3, neck, -1)
-    grad_expand = ex.astype(jnp.float32)
     gg_expand, gb_expand, gg_dilated, gb_dilated, gg_reduce, gb_reduce = st3[1], st3[0], st2[1], st2[0], st1[1], st1[0]
-    grad_pool = grad_k[27].T
-    grad_k = jnp.swapaxes(grad_k[:27].reshape(3, 3, 3, -1, C), 3, 4)
     return (
         class_logits,
         grad_features,

time: 555 us -> 509 us (0.917)
  Pallas kernels: 511 us -> 481 us
  local copies, waits for them, and re-layouts: 23.2 us -> 14.8 us
  other arithmetic: 10.4 us -> 3.29 us
    pallas_call x1, Pallas kernels: 186 us -> 154 us  [branches_back(): pl.pallas_call(functools.partial(branches_back_kernel, steps), out_shape=...]
    pallas_call x0 -> x1, Pallas kernels: none -> 6.91 us  [widen(): pl.pallas_call(widen_kernel, out_shape=[jax.ShapeDtypeStruct(v, jnp.float...]
    pallas_call x1, Pallas kernels: 117 us -> 111 us  [bottleneck_back(): pl.pallas_call(bottleneck_back_kernel, out_shape=[S((N, C), f32)] + [S(b,...]
where the time goes in v4:
time: 509 us; the launch traced here: 500 us
  Pallas kernels  481 us (94%)
  local copies, waits for them, and re-layouts  14.8 us (3%)
    pallas_call x1, Pallas kernels, branches_back(): pl.pallas_call(functools.partial(branches_back_kernel, steps), out_shape=...  154 us
    pallas_call x1, Pallas kernels, bottleneck(): pl.pallas_call(bottleneck_kernel, out_shape=outs, in_specs=[VM] * 9 + [AN...  124 us
    pallas_call x1, Pallas kernels, bottleneck_back(): pl.pallas_call(bottleneck_back_kernel, out_shape=[S((N, C), f32)] + [S(b,...  111 us
    pallas_call x1, Pallas kernels, head(): pl.pallas_call(functools.partial(head_kernel, steps), out_shape=[S((N, 12...  84.4 us

profile of v4, /device:TPU:0, one launch (start us, length us, event | category | flops | bytes accessed | tf_op | source)
XLA Modules:
  0.0 499.9 jit_solution(6466967744593027440)
XLA Ops:
  0.7 0.7 fusion
  1.4 0.1 copy.61
  1.6 0.6 pad.8.kb_ref
  2.2 0.7 compare_convert_fusion
  2.9 0.1 copy.64
  3.0 0.2 copy.65
  3.2 0.1 reshape.180
  3.3 0.8 broadcast_in_dim.53.ins_ref
  4.1 0.8 copy.66
  4.9 0.6 pad.9.wc_s
  5.6 124.4 %bottleneck.1 = (bf16[16,544,256]{2,1,0:T(8,128)(2,1)}, bf16[16,32,2048]{2,1,0:T(8,128)(2,1)}, bf16[512,2048]{1,0:T(8,128)(2,1)}, bf16[512,2048]{1,0:T(8,128)(2,...) custom-call(bf16[512,2048]{1,0:T(8,128)(2,1)} %bitcast.79, ...), custom_call_target="tpu_custom_call" | custom-call | tf_op jit(solution)/shard_map/bottleneck/pallas_call | solution.py:788
  130.0 0.1 copy.67
  130.1 0.2 copy.68
  130.3 0.1 convert_element_type.56
  130.4 0.8 broadcast_in_dim.61.kb
  131.2 0.1 copy.69
  131.3 0.2 copy.70
  131.5 0.1 convert_element_type.60
  131.6 0.8 broadcast_in_dim.62.lab
  132.5 0.6 pad_maximum_fusion
  133.1 0.6 pad_maximum_fusion.1
  133.7 84.4 %head.1 = (bf16[512,128]{1,0:T(8,128)(2,1)}, bf16[512,256]{1,0:T(8,128)(2,1)}, bf16[16,32,768]{2,1,0:T(8,128)(2,1)}, bf16[256,1536]{1,0:T(8,128)(2,1)}, bf16[8,2...) custom-call(bf16[16,544,256]{2,1,0:T(8,128)(2,1)} %get-tuple-element.75, ...), custom_call_target="tpu_custom_call" | custom-call | tf_op jit(solution)/shard_map/head/pallas_call | solution.py:1547
  218.1 1.7 copy.71
  219.8 154.1 %branches_back.1 = (bf16[16,32,2048]{2,1,0:T(8,128)(2,1)}, bf16[28,32,2048]{2,1,0:T(8,128)(2,1)}) custom-call(bf16[16,32,768]{2,1,0:T(8,128)(2,1)} %get-tuple-element.84.d_ref, bf16[16,544,256]{2,1,0:T(8,128)(2,1)} %get-tuple-element.75.yo.y_ref, bf16[16,544,128]{2,1,0:T(8,128)(2,1)} %get-tuple-element.76.key.key_ref.key_any, ...), custom_call_target="tpu_custom_call" | custom-call | tf_op jit(solution)/shard_map/branches_back/pallas_call | solution.py:993
  373.9 110.6 %bottleneck_back.1 = (f32[512,2048]{1,0:T(8,128)}, bf16[32,3584]{1,0:T(8,128)(2,1)}, bf16[512,256]{1,0:T(8,128)(2,1)}, bf16[9,64,512]{2,1,0:T(8,128)(2,1)}, bf16...) custom-call(bf16[512,2048]{1,0:T(8,128)(2,1)} %bitcast.80, ...), custom_call_target="tpu_custom_call" | custom-call | tf_op jit(solution)/shard_map/bottleneck_back/pallas_call | solution.py:1333
  484.6 6.9 %widen.1 = (f32[9,32,2048]{2,1,0:T(8,128)}, f32[9,32,2048]{2,1,0:T(8,128)}, f32[9,32,2048]{2,1,0:T(8,128)}, f32[32,2048]{1,0:T(8,128)}, f32[32,2048]{1,0:T(8,128...) custom-call(bf16[28,32,2048]{2,1,0:T(8,128)(2,1)} %get-tuple-element.103.gk, ...), custom_call_target="tpu_custom_call" | custom-call | tf_op jit(solution)/shard_map/widen/pallas_call | solution.py:1592
  491.5 0.6 fusion.4
  492.1 0.6 fusion.2
  492.7 0.6 fusion.3
  493.3 0.7 slice_convert_fusion
  494.0 0.7 copy.72
  494.7 4.7 copy.74
  (31 shorter events, 0.2 us)
Async XLA Ops:
  5.5 125.7 %copy-start.2 = (s32[8,64]{1,0:T(8,128)S(1)}, s32[8,64]{1,0:T(8,128)}, u32[]{:S(2)}) copy-start(s32[8,64]{1,0:T(8,128)} %param.31) | copy-start | bytes 6148
  5.5 126.9 %copy-start.6 = (f32[256]{0:T(256)S(1)}, f32[256]{0:T(256)}, u32[]{:S(2)}) copy-start(f32[256]{0:T(256)} %param.51) | copy-start | bytes 3076
  5.5 126.9 %copy-start.7 = (f32[256]{0:T(256)S(1)}, f32[256]{0:T(256)}, u32[]{:S(2)}) copy-start(f32[256]{0:T(256)} %param.48) | copy-start | bytes 3076
  5.5 126.9 %copy-start.8 = (f32[256]{0:T(256)S(1)}, f32[256]{0:T(256)}, u32[]{:S(2)}) copy-start(f32[256]{0:T(256)} %param.45) | copy-start | bytes 3076
  5.5 126.9 %copy-start.9 = (f32[256]{0:T(256)S(1)}, f32[256]{0:T(256)}, u32[]{:S(2)}) copy-start(f32[256]{0:T(256)} %param.42) | copy-start | bytes 3076
  5.5 127.5 %copy-start.10 = (f32[256]{0:T(256)S(1)}, f32[256]{0:T(256)}, u32[]{:S(2)}) copy-start(f32[256]{0:T(256)} %param.52) | copy-start | bytes 3076
  5.5 127.5 %copy-start.11 = (f32[256]{0:T(256)S(1)}, f32[256]{0:T(256)}, u32[]{:S(2)}) copy-start(f32[256]{0:T(256)} %param.49) | copy-start | bytes 3076
  5.6 127.5 %copy-start.12 = (f32[256]{0:T(256)S(1)}, f32[256]{0:T(256)}, u32[]{:S(2)}) copy-start(f32[256]{0:T(256)} %param.46) | copy-start | bytes 3076
  5.6 127.5 %copy-start.13 = (f32[256]{0:T(256)S(1)}, f32[256]{0:T(256)}, u32[]{:S(2)}) copy-start(f32[256]{0:T(256)} %param.43) | copy-start | bytes 3076
  484.6 7.0 %copy-start.3 = (f32[2,512]{1,0:T(2,128)S(1)}, f32[2,512]{1,0:T(2,128)}, u32[]{:S(2)}) copy-start(f32[2,512]{1,0:T(2,128)} %get-tuple-element.111) | copy-start | bytes 12292
  484.6 7.0 %copy-start.4 = (f32[2,512]{1,0:T(2,128)S(1)}, f32[2,512]{1,0:T(2,128)}, u32[]{:S(2)}) copy-start(f32[2,512]{1,0:T(2,128)} %get-tuple-element.109) | copy-start | bytes 12292
  484.6 7.5 %copy-start = (f32[2,2048]{1,0:T(2,128)S(1)}, f32[2,2048]{1,0:T(2,128)}, u32[]{:S(2)}) copy-start(f32[2,2048]{1,0:T(2,128)} %get-tuple-element.113) | copy-start | bytes 49156
  484.6 8.2 %copy-start.1 = (f32[2,1024]{1,0:T(2,128)S(1)}, f32[2,1024]{1,0:T(2,128)}, u32[]{:S(2)}) copy-start(f32[2,1024]{1,0:T(2,128)} %get-tuple-element.115) | copy-start | bytes 24580
  484.6 8.1 %copy-start.5 = (f32[2,256]{1,0:T(2,128)S(1)}, f32[2,256]{1,0:T(2,128)}, u32[]{:S(2)}) copy-start(f32[2,256]{1,0:T(2,128)} %get-tuple-element.121) | copy-start | bytes 6148

commit v5 on v4

--- a/solution.py
+++ b/solution.py
@@ -797,7 +797,7 @@
 
 
 def branches_back_kernel(
-    steps, d_ref, y_ref, key_ref, k_ref, pooled_ref, dr_ref, size_ref, dy_o, gk_o,
+    steps, d_ref, y_ref, key_ref, k_ref, pooled_ref, dr_ref, size_ref, dy_o, gk_o, tail_o,
     g, gt, gk, fin, in1, in2, dyo, acc, gp, *sems,
 ):
     sems = list(sems)
@@ -866,7 +866,7 @@
         def _():
             to_outer(t).wait_recv()
 
-    gk[27] = tn_dot(dr_ref[...], pooled_ref[...]).astype(gk.dtype)
+    tail_o[9] = tn_dot(dr_ref[...], pooled_ref[...]).astype(gk.dtype)
     gp[...] = nn_dot(dr_ref[...], k_ref[27]) / size_ref[:, :1]
     for b, s in enumerate(steps):
         gathers[b].forward()
@@ -889,12 +889,14 @@
                     r = nn_dot(gt[b * W : (b + 1) * W, q * T : (q + 1) * T], v)
                     got = r if got is None else got + r
                 t = 9 * b + 3 * (i + 1) + j + 1
-                gk[t] = got.astype(gk.dtype)
-                if t % 2:
-                    hand(t // 2)
-                if b == 2 and t % 2:
-                    first((t - 18) // 2)
-    hand(13)
+                if b < 2:
+                    gk[t] = got.astype(gk.dtype)
+                    if t % 2:
+                        hand(t // 2)
+                else:
+                    tail_o[t - 18] = got.astype(gk.dtype)
+                    if t % 2:
+                        first((t - 18) // 2)
     cps = []
     ready = 4
 
@@ -941,7 +943,7 @@
         def _():
             first(t)
 
-    groups = (4, 5, 3, 2)
+    groups = (4, 3, 2)
     at = 0
     for n, size in enumerate(groups):
         stop = at + size
@@ -992,17 +994,19 @@
     V = pltpu.VMEM
     return pl.pallas_call(
         functools.partial(branches_back_kernel, steps),
-        out_shape=[jax.ShapeDtypeStruct((Q, h, 8 * w), b16), jax.ShapeDtypeStruct((28, W // 8, 8 * w), b16)],
+        out_shape=[jax.ShapeDtypeStruct((Q, h, 8 * w), b16), jax.ShapeDtypeStruct((18, W // 8, 8 * w), b16),
+            jax.ShapeDtypeStruct((10, W, w), b16),
+        ],
         in_specs=[VM] * 7,
-        out_specs=[ANY] * 2,
+        out_specs=[ANY] * 2 + [VM],
         scratch_shapes=[
-            V((Q, TT, W3), b16), V((W3, Q * T), b16), V((28, W, w), b16), V((28, W, w), b16),
-            V((28, W, w), b16), V((28, W, w), b16), V((Q, T, w), b16),
+            V((Q, TT, W3), b16), V((W3, Q * T), b16), V((18, W, w), b16), V((18, W, w), b16),
+            V((18, W, w), b16), V((18, W, w), b16), V((Q, T, w), b16),
             V((Q * h, w), f32), V((8, w), f32),
         ]
         + gather_sems() * 3
         + [DMA((4, 8)), DMA((4, 8)), DMA((4,)), DMA((8,)), DMA((8,)), DMA(())]
-        + [DMA((14,))] * 6,
+        + [DMA((9,))] * 6,
         compiler_params=pltpu.CompilerParams(collective_id=10, has_side_effects=True, vmem_limit_bytes=VLIM),
         name="branches_back",
     )(d, y, key, k, pooled, dr, sizes)
@@ -1039,7 +1043,8 @@
 
 
 class Reduce:
-    def __init__(self, full, part, near, far, tot, zin, zo, out, sems, d, f):
+    def __init__(self, full, part, half, near, far, corner, tot, zin, zo, out, sems, d, f):
+        self.half, self.corner = half, corner
         self.full, self.part, self.near, self.fars, self.tot, self.out = full, part, near, far, tot, out
         self.zin, self.zo, self.d, self.f = zin, zo, d, f
         self.sems = sems
@@ -1062,10 +1067,30 @@
             g = self.me ^ k
             val = self.full[self.part(2 * g + self.c0)].astype(jnp.float32) + self.near[g].astype(jnp.float32)
             self.near[g] = val.astype(self.near.dtype)
-            if k:
-                self.cps.append(
-                    remote(self.near.at[g], self.fars.at[k], ss.at[k], rs.at[k], self.d, self.f ^ (2 * k))
+            if k == 3:
+                for a in (0, 1):
+                    self.cps.append(
+                        remote(
+                            self.near.at[(g,) + self.half(a)], self.corner.at[self.half(a)], ss.at[a], rs.at[a],
+                            self.d, self.f ^ (2 + 2 * a),
+                        )
+                    )
+
+    def beside(self):
+        ss, rs = self.sems[2:4]
+        for c in self.cps:
+            c.wait()
+        self.cps = []
+        for k in (1, 2):
+            g = self.me ^ k
+            a = self.half(2 - k)
+            val = self.near[(g,) + a].astype(jnp.float32) + self.corner[a].astype(jnp.float32)
+            self.near[(g,) + a] = val.astype(self.near.dtype)
+            self.cps.append(
+                remote(
+                    self.near.at[g], self.fars.at[k - 1], ss.at[k + 1], rs.at[k + 1], self.d, self.f ^ (2 * k)
                 )
+            )
 
     def to_inner(self):
         ss, rs = self.sems[4:6]
@@ -1092,8 +1117,8 @@
         for c in self.cps:
             c.wait()
         val = self.near[self.me].astype(jnp.float32)
-        for k in (1, 2, 3):
-            val = val + self.fars[k].astype(jnp.float32)
+        for k in (1, 2):
+            val = val + self.fars[k - 1].astype(jnp.float32)
         self.tot[...] = val.astype(self.tot.dtype)
 
         @pl.when(self.d % 3 == 0)
@@ -1130,7 +1155,7 @@
 
 def reduce_scratch(block):
     V, b16 = pltpu.VMEM, jnp.bfloat16
-    return [V((4,) + block, b16), V((4,) + block, b16), V(block, b16), V(block, b16), V(block, b16)] + [DMA((4,))] * 6
+    return [V((4,) + block, b16), V((2,) + block, b16), V(block, b16), V(block, b16), V(block, b16), V(block, b16)] + [DMA((4,))] * 6
 
 
 def wide(row, n):
@@ -1138,9 +1163,9 @@
 
 
 def bottleneck_back_kernel(
-    x_ref, ins_ref, st_ref, gr, gd, ge, dy, dpt, y_ref, pm_in, wp, n3, l3, we, n2, l2, h2, wd, ext, n1, l1, wr, key_any,
-    gf_o, pm_o, ex_o, di_o, re_o, s3_o, s2_o, s1_o,
-    pm, ex, di, re_, dp3, d3, acc, ext2, d1n, key, gf, pick, ksem, hs, hr, gs,
+    x_ref, ins_ref, st_ref, gr, gd, ge, dy, dpt, y_ref, pm_in, wp, n3, l3, we, n2, l2, h2, wd, ext, n1, l1, wr, key_any, tail,
+    gf_o, pm_o, ex_o, di_o, re_o, s3_o, s2_o, s1_o, tk_o,
+    pm, ex, di, dp3, d3, acc, ext2, d1n, key, gf, pick, in1, in2, ksem, hs, hr, gs, s1, r1, s2, r2, s3, r3, ws, wrs, wl,
     *sems,
 ):
     sems = list(sems)
@@ -1163,18 +1188,87 @@
     def ds(i, n):
         return pl.ds(pl.multiple_of(n * i, n), n)
 
-    def reducer(full, part, out):
-        near, far, tot, zin, zo = take(5)
-        return Reduce(full, part, near, far, tot, zin, zo, out, take(6), d, f)
-
-    r_pm = reducer(pm, lambda g: (ds(g, nw),), pm_o)
-    r_ex = reducer(ex, lambda g: (slice(None), ds(g, C // 8)), ex_o)
+    def reducer(full, part, half, out):
+        near, far, corner, tot, zin, zo = take(6)
+        return Reduce(full, part, half, near, far, corner, tot, zin, zo, out, take(6), d, f)
+
+    def half_rows(n):
+        return lambda a: (pl.ds(a * n, n),)
+
+    r_pm = reducer(pm, lambda g: (ds(g, nw),), half_rows(nw // 2), pm_o)
+    r_ex = reducer(ex, lambda g: (slice(None), ds(g, C // 8)), half_rows(neck // 2), ex_o)
     r_di = [
-        reducer(di.at[pl.ds(3 * i, 3)], lambda g: (slice(None), ds(g, nb)), di_o.at[pl.ds(3 * i, 3)]) for i in range(3)
+        reducer(
+            di.at[pl.ds(3 * i, 3)], lambda g: (slice(None), ds(g, nb)),
+            lambda a: (slice(None), pl.ds(a * (nb // 2), nb // 2)), di_o.at[pl.ds(3 * i, 3)],
+        )
+        for i in range(3)
     ]
-    r_re = reducer(re_, lambda g: (ds(g, nb),), re_o)
+    re_ = ex
+    r_re = reducer(re_, lambda g: (ds(g, nb),), half_rows(nb // 2), re_o)
     sum3, sum2, sum1 = (Sum(take(6), d, f) for _ in range(3))
 
+    outer = d % 3 == 0
+    o = in1.shape[1] // 8
+    lanes = in1.shape[2]
+    kout = []
+
+    def move(src, dst, ss, rs, t, other):
+        two = pl.ds(2 * t, 2)
+        return pltpu.make_async_remote_copy(
+            src_ref=src.at[two], dst_ref=dst.at[two], send_sem=ss.at[t], recv_sem=rs.at[t],
+            device_id=(d ^ other, f), device_id_type=MESH,
+        )
+
+    def to_inner(t):
+        return move(tail, in1, s1, r1, t, 1)
+
+    def across(t):
+        return move(in1, in2, s2, r2, t, 3)
+
+    def to_outer(t):
+        return move(in1, in1, s3, r3, t, 1)
+
+    def hand(t):
+        @pl.when(outer)
+        def _():
+            to_inner(t).start()
+
+    def first(t):
+        @pl.when(jnp.logical_not(outer))
+        def _():
+            to_inner(t).wait_recv()
+            for n in (2 * t, 2 * t + 1):
+                in1[n] = (in1[n].astype(jnp.float32) + tail[n].astype(jnp.float32)).astype(in1.dtype)
+            across(t).start()
+
+    def second(t):
+        @pl.when(jnp.logical_not(outer))
+        def _():
+            across(t).wait()
+            for n in (2 * t, 2 * t + 1):
+                in1[n] = (in1[n].astype(jnp.float32) + in2[n].astype(jnp.float32)).astype(in1.dtype)
+            to_outer(t).start()
+
+    def keep(n, at, size):
+        for t in range(at, at + size):
+
+            @pl.when(outer)
+            def _():
+                to_outer(t).wait_recv()
+
+        for k in (6, 7, 2, 3, 4, 5, 1, 0):
+            src = in1.at[pl.ds(2 * at, 2 * size), pl.ds(pl.multiple_of(o * (f ^ k), 16), o), :]
+            to = tk_o.at[pl.ds(2 * at, 2 * size), :, pl.ds(pl.multiple_of(lanes * f, 128), lanes)]
+            if k:
+                kout.append(remote(src, to, ws.at[n, k], wrs.at[n, k], d, f ^ k))
+            else:
+                c = pltpu.make_async_copy(src, to, wl.at[n])
+                c.start()
+                kout.append(c)
+
+    hand(0)
+    hand(1)
     kcp = pltpu.make_async_copy(key_any.at[:, pl.ds(pl.multiple_of(PAD - e + h * f, 16), 2 * h), :], key, ksem)
     kcp.start()
     count = st_ref[0:1, 0:1]
@@ -1186,6 +1280,8 @@
     ins = wide(ins_ref[...], 2)
     for c in range(0, C, 256):
         w = slice(c, c + 256)
+        if c == C // 2:
+            first(0)
         v = dy[:, w].astype(jnp.float32) + nn_dot(dpt[...], wp[:, w])
         v = v * l3[:, w].astype(jnp.float32)
         dp3[:, w] = v.astype(jnp.bfloat16)
@@ -1201,6 +1297,9 @@
     r_pm.far()
     tot = sum3.result()
     s3_o[...] = tot
+    second(0)
+    first(1)
+    hand(2)
     for c in range(0, C, 256):
         w = slice(c, c + 256)
         v = dp3[:, w].astype(jnp.float32) - tot[0:1, w] / count - n3[:, w].astype(jnp.float32) * (tot[1:2, w] / count)
@@ -1227,9 +1326,12 @@
         ext2[:, e : e + h, w] = v.astype(jnp.bfloat16).reshape(Q, h, 256)
     up = remote(ext2.at[:, pl.ds(e, e)], ext2.at[:, pl.ds(e + h, e)], hs.at[0], hr.at[0], d, lax.rem(f + 7, 8))
     down = remote(ext2.at[:, pl.ds(h, e)], ext2.at[:, pl.ds(0, e)], hs.at[1], hr.at[1], d, lax.rem(f + 1, 8))
+    second(1)
+    hand(3)
     kcp.wait()
-    r_pm.tiles()
+    r_pm.beside()
     r_ex.far()
+    first(2)
     for i in range(3):
         for j in range(3):
             lo, hi = span(j - 1, Q)
@@ -1240,11 +1342,20 @@
             g = ext2[lo:hi, e : e + h, :].reshape((hi - lo) * h, neck)
             di[3 * i + j] = tn_dot(g, v).astype(jnp.bfloat16)
         r_di[i].pair()
+        if i == 0:
+            hand(4)
+            first(3)
+            second(2)
+        if i == 1:
+            r_ex.beside()
     up.wait()
-    r_pm.middle()
     down.wait()
+    r_pm.tiles()
     acc[...] = jnp.zeros_like(acc)
     for i in range(3):
+        if i == 1:
+            first(4)
+            second(3)
         for j in (1, 0, 2):
             lo, hi = span(1 - j, Q)
             ok = same_crop(
@@ -1265,9 +1376,13 @@
     sum1.start([cat_rows(ones), cat_rows(crossed)])
     for r in r_di:
         r.far()
+    r_pm.middle()
     sum1.turn()
+    r_ex.tiles()
+    second(4)
     r_pm.last()
-    r_ex.tiles()
+    for r in r_di:
+        r.beside()
     tot = sum1.result()
     s1_o[...] = tot
     for c in range(0, neck, 256):
@@ -1290,6 +1405,8 @@
         cp = pltpu.make_async_copy(gf.at[n % 2], gf_o.at[:, pl.ds(c, 256)], gs.at[n % 2])
         cp.start()
         out.append(cp)
+        if n == 0:
+            r_re.beside()
         if n == 1:
             r_di[0].middle()
             r_ex.last()
@@ -1301,6 +1418,8 @@
         if n == 7:
             r_di[2].tiles()
             r_di[1].last()
+    keep(0, 0, 3)
+    keep(1, 3, 2)
     r_di[2].middle()
     r_re.tiles()
     r_di[2].last()
@@ -1308,6 +1427,18 @@
     r_re.last()
     out[-2].wait()
     out[-1].wait()
+    for t in range(5):
+
+        @pl.when(outer)
+        def _():
+            to_inner(t).wait_send()
+
+        @pl.when(jnp.logical_not(outer))
+        def _():
+            to_outer(t).wait_send()
+
+    for c in kout:
+        c.wait()
     for r in [r_pm, r_ex, r_re] + r_di:
         r.done()
 
@@ -1317,24 +1448,28 @@
     N, C = x.shape
     Q, h2_, neck = args[18].shape
     h = h2_ // 2
+    tail = args[23]
     W = dpt.shape[1]
     PM = C + pm_in.shape[1]
     b16, f32 = jnp.bfloat16, jnp.float32
     S, V = jax.ShapeDtypeStruct, pltpu.VMEM
     blocks = [(W // 8, PM), (neck, C // 8), (9, neck // 8, neck), (neck // 8, C)]
     scratch = [
-        V((W, PM), b16), V((neck, C), b16), V((9, neck, neck), b16), V((neck, C), b16), V((N, C), b16), V((N, C), b16),
+        V((W, PM), b16), V((neck, C), b16), V((9, neck, neck), b16), V((N, C), b16), V((N, C), b16),
         V((N, neck), f32), V((Q, 2 * h, neck), b16), V((N, neck), b16), V((Q, 2 * h, 128), b16), V((2, N, 256), f32),
-        V((N, N), b16), DMA(()), DMA((2,)), DMA((2,)), DMA((2,)),
+        V((N, N), b16), V(tail.shape, b16), V(tail.shape, b16),
+        DMA(()), DMA((2,)), DMA((2,)), DMA((2,)),
     ]
+    scratch += [DMA((5,))] * 6 + [DMA((2, 8)), DMA((2, 8)), DMA((2,))]
     for n in (0, 1, 2, 2, 2, 3):
         scratch += reduce_scratch((3,) + blocks[2][1:] if n == 2 else blocks[n])
     scratch += sum_sems(2, C) + sum_sems(2, neck) + sum_sems(2, neck)
     return pl.pallas_call(
         bottleneck_back_kernel,
-        out_shape=[S((N, C), f32)] + [S(b, b16) for b in blocks] + [S((2, C), f32), S((2, neck), f32), S((2, neck), f32)],
-        in_specs=[VM] * 22 + [ANY],
-        out_specs=[ANY] + [VM] * 7,
+        out_shape=[S((N, C), f32)] + [S(b, b16) for b in blocks] + [S((2, C), f32), S((2, neck), f32), S((2, neck), f32)]
+        + [S((10, W // 8, C), b16)],
+        in_specs=[VM] * 22 + [ANY, VM],
+        out_specs=[ANY] + [VM] * 7 + [ANY],
         scratch_shapes=scratch,
         compiler_params=pltpu.CompilerParams(collective_id=12, has_side_effects=True, vmem_limit_bytes=VLIM),
         name="bottleneck_back",
@@ -1365,7 +1500,7 @@
 def head_kernel(
     steps, yo, key, kern, y, wp, wm, wc, ins_ref, kb, lab, st_ref, gb, bb, gm, bm,
     lo_o, dp_o, dr_o, pm_o, pooled_o, dpool_o, size_o, sb_o, sm_o,
-    acc, near, mine, far, ab, nb, lb, joined, nm, lm, merged, pn, ps, pr, ss, rs,
+    acc, near, mine, far, corner, ab, nb, lb, joined, nm, lm, merged, pn, ps, pr, ss, rs,
     *sems,
 ):
     sems = list(sems)
@@ -1403,13 +1538,32 @@
                 remote(pn.at[k], near.at[k], ps.at[k], pr.at[k], d, f ^ 1)
             else:
 
-                @pl.when(k > 0)
+                @pl.when(k == 3)
                 def _():
-                    remote(mine.at[k], far.at[k], ss.at[k], rs.at[k], d, f ^ (2 * k))
+                    for a in (0, 1):
+                        by_way(a).start()
 
         return 0
 
-    lax.fori_loop(0, 4, step, 0)
+    def by_way(a):
+        two = pl.ds(a * (Q // 2), Q // 2)
+        return pltpu.make_async_remote_copy(
+            src_ref=mine.at[3, two], dst_ref=corner.at[two], send_sem=ss.at[a], recv_sem=rs.at[a],
+            device_id=(d, f ^ (2 + 2 * a)), device_id_type=MESH,
+        )
+
+    lax.fori_loop(0, 3, step, 0)
+    for a in (0, 1):
+        by_way(a).wait()
+    out = []
+    for k in (1, 2):
+        two = slice((2 - k) * (Q // 2), (3 - k) * (Q // 2))
+        for b in range(3):
+            lanes = slice(b * W, (b + 1) * W)
+            val = mine[k, two, :, lanes].astype(f32) + corner[two, :, lanes].astype(f32)
+            mine[k, two, :, lanes] = val.astype(b16)
+        out.append(remote(mine.at[k], far.at[k - 1], ss.at[k + 1], rs.at[k + 1], d, f ^ (2 * k)))
+    lax.fori_loop(3, 4, step, 0)
     ab[:, :W] = nt_dot(y[...], wp[...])
     crop = (lax.broadcasted_iota(jnp.int32, (T, 128), 1) + 1).astype(f32)
 
@@ -1426,19 +1580,16 @@
     part = nt_dot(pooled, kern[27])
     part = cat_rows([part[c : c + 1] for c in range(CROPS_TILE)])
     ins = wide(ins_ref[...], 2)
-    for k in (3, 1, 2):
-        pltpu.make_async_remote_copy(
-            src_ref=mine.at[k], dst_ref=far.at[k], send_sem=ss.at[k], recv_sem=rs.at[k],
-            device_id=(d, f ^ (2 * k)), device_id_type=MESH,
-        ).wait()
+    for c in out:
+        c.wait()
     ones, squares = [], []
     for b in range(4):
         lanes = slice(b * W, (b + 1) * W)
         if b:
             src = slice((b - 1) * W, b * W)
             v = mine[0, :, :, src].astype(f32)
-            for k in (1, 2, 3):
-                v = v + far[k, :, :, src].astype(f32)
+            for k in (1, 2):
+                v = v + far[k - 1, :, :, src].astype(f32)
             ab[:, lanes] = v.reshape(N, W)
         s, t = column_sums(ab[:, lanes], ins_ref[...])
         ones.append(s)
@@ -1553,7 +1704,7 @@
         in_specs=[VM] * 15,
         out_specs=[VM] * 9,
         scratch_shapes=[V((N, W), f32)]
-        + [V((4, Q, h, 3 * W), b16)] * 3
+        + [V((4, Q, h, 3 * W), b16)] * 2 + [V((2, Q, h, 3 * W), b16), V((Q, h, 3 * W), b16)]
         + [
             V((N, 4 * W), f32), V((N, 4 * W), b16), V((N, 4 * W), b16), V((N, J), b16), V((N, W), f32), V((N, W), f32),
             V((N, W), b16), V((4, Q, h, 3 * W), b16), DMA((4,)), DMA((4,)), DMA((4,)), DMA((4,)),
@@ -1564,15 +1715,15 @@
     )(*args)
 
 
-def widen_kernel(gk, pm, ex, di, re_, k0, k1, k2, pool, point, merge, dilated, expand, reduce_):
+def widen_kernel(gk, tk, pm, ex, di, re_, k0, k1, k2, pool, point, merge, dilated, expand, reduce_):
     for b, o in enumerate((k0, k1, k2)):
 
         def tap(t, _):
-            o[t] = gk[9 * b + t].astype(jnp.float32)
+            o[t] = (tk[t] if b == 2 else gk[9 * b + t]).astype(jnp.float32)
             return 0
 
         lax.fori_loop(0, 9, tap, 0)
-    pool[...] = gk[27].astype(jnp.float32)
+    pool[...] = tk[9].astype(jnp.float32)
     C = point.shape[1]
     point[...] = pm[:, :C].astype(jnp.float32)
     merge[...] = pm[:, C : C + merge.shape[1]].astype(jnp.float32)
@@ -1586,17 +1737,17 @@
     reduce_[...] = re_[...].astype(jnp.float32)
 
 
-def widen(gk, pm, ex, di, re_, J):
+def widen(gk, tk, pm, ex, di, re_, J):
     _, o, C = gk.shape
     shapes = [(9, o, C)] * 3 + [(o, C), (o, C), (o, J), di.shape, ex.shape, re_.shape]
     return pl.pallas_call(
         widen_kernel,
         out_shape=[jax.ShapeDtypeStruct(v, jnp.float32) for v in shapes],
-        in_specs=[VM] * 5,
+        in_specs=[VM] * 6,
         out_specs=[VM] * 9,
         compiler_params=pltpu.CompilerParams(vmem_limit_bytes=VLIM),
         name="widen",
-    )(gk, pm, ex, di, re_)
+    )(gk, tk, pm, ex, di, re_)
 
 
 def norm_coeffs(totals, squares, count):
@@ -1663,13 +1814,13 @@
     class_logits = logits[:, :CLASSES].reshape(rows, cols, CLASSES)
     gb_br, gg_br = st_br[0], st_br[1]
     gb_merge, gg_merge = st_m[0], st_m[1]
-    d_y, grad_k = branches_back(d_rates, y_own, key, kernel, pooled, d_pool, sizes, steps)
-    grad_features, pm, ex, di, re_, st3, st2, st1 = bottleneck_back(
+    d_y, grad_k, tail = branches_back(d_rates, y_own, key, kernel, pooled, d_pool, sizes, steps)
+    grad_features, pm, ex, di, re_, st3, st2, st1, tail = bottleneck_back(
         features.reshape(N, C), ins, stats, vecs[0], vecs[2], vecs[4], d_y.reshape(N, C), d_point, y, rest, wp,
-        n_three, l_three, full_expand, n_two, l_two, h_two, wd, ext, n_one, l_one, wr, key,
+        n_three, l_three, full_expand, n_two, l_two, h_two, wd, ext, n_one, l_one, wr, key, tail,
     )
     grad_classes = pm[:, C + J : C + J + CLASSES].astype(jnp.float32)
-    *grad_k, grad_pool, grad_point, grad_merge, grad_dilated, grad_expand, grad_reduce = widen(grad_k, pm, ex, di, re_, J)
+    *grad_k, grad_pool, grad_point, grad_merge, grad_dilated, grad_expand, grad_reduce = widen(grad_k, tail, pm, ex, di, re_, J)
     grad_k = [jnp.swapaxes(v.reshape(3, 3, -1, C), 2, 3) for v in grad_k]
     grad_pool, grad_point, grad_merge, grad_reduce = grad_pool.T, grad_point.T, grad_merge.T, grad_reduce.T
     grad_dilated = jnp.swapaxes(grad_dilated, 1, 2).reshape(3, 3, neck, -1)

time: 509 us -> 471 us (0.925)
  Pallas kernels: 481 us -> 443 us
    pallas_call x1, Pallas kernels: 154 us -> 117 us  [branches_back(): pl.pallas_call(functools.partial(branches_back_kernel, steps), out_shape=...]
where the time goes in v5:
time: 471 us; the launch traced here: 463 us
  Pallas kernels  443 us (94%)
  local copies, waits for them, and re-layouts  14.8 us (3%)
    pallas_call x1, Pallas kernels, bottleneck(): pl.pallas_call(bottleneck_kernel, out_shape=outs, in_specs=[VM] * 9 + [AN...  124 us
    pallas_call x1, Pallas kernels, branches_back(): pl.pallas_call(functools.partial(branches_back_kernel, steps), out_shape=...  117 us
    pallas_call x1, Pallas kernels, bottleneck_back(): pl.pallas_call(bottleneck_back_kernel, out_shape=[S((N, C), f32)] + [S(b,...  115 us
    pallas_call x1, Pallas kernels, head(): pl.pallas_call(functools.partial(head_kernel, steps), out_shape=[S((N, 12...  80.4 us

profile of v5, /device:TPU:0, one launch (start us, length us, event | category | flops | bytes accessed | tf_op | source)
XLA Modules:
  0.0 462.7 jit_solution(5208663963536827577)
XLA Ops:
  0.7 0.7 fusion
  1.4 0.1 copy.61
  1.6 0.6 pad.8.kb_ref
  2.2 0.7 compare_convert_fusion
  2.9 0.1 copy.64
  3.0 0.2 copy.65
  3.2 0.1 reshape.180
  3.3 0.8 broadcast_in_dim.53.ins_ref
  4.1 0.8 copy.66
  4.9 0.6 pad.9.wc_s
  5.6 124.4 %bottleneck.1 = (bf16[16,544,256]{2,1,0:T(8,128)(2,1)}, bf16[16,32,2048]{2,1,0:T(8,128)(2,1)}, bf16[512,2048]{1,0:T(8,128)(2,1)}, bf16[512,2048]{1,0:T(8,128)(2,...) custom-call(bf16[512,2048]{1,0:T(8,128)(2,1)} %bitcast.79, ...), custom_call_target="tpu_custom_call" | custom-call | tf_op jit(solution)/shard_map/bottleneck/pallas_call | solution.py:788
  130.0 0.1 copy.67
  130.1 0.2 copy.68
  130.3 0.1 convert_element_type.56
  130.4 0.8 broadcast_in_dim.61.kb
  131.2 0.1 copy.69
  131.3 0.2 copy.70
  131.5 0.1 convert_element_type.60
  131.6 0.8 broadcast_in_dim.62.lab
  132.4 0.6 pad_maximum_fusion
  133.1 0.6 pad_maximum_fusion.1
  133.7 80.4 %head.1 = (bf16[512,128]{1,0:T(8,128)(2,1)}, bf16[512,256]{1,0:T(8,128)(2,1)}, bf16[16,32,768]{2,1,0:T(8,128)(2,1)}, bf16[256,1536]{1,0:T(8,128)(2,1)}, bf16[8,2...) custom-call(bf16[16,544,256]{2,1,0:T(8,128)(2,1)} %get-tuple-element.77, ...), custom_call_target="tpu_custom_call" | custom-call | tf_op jit(solution)/shard_map/head/pallas_call | solution.py:1698
  214.0 1.7 copy.71
  215.7 116.8 %branches_back.1 = (bf16[16,32,2048]{2,1,0:T(8,128)(2,1)}, bf16[18,32,2048]{2,1,0:T(8,128)(2,1)}, bf16[10,256,256]{2,1,0:T(8,128)(2,1)}) custom-call(bf16[16,32,768]{2,1,0:T(8,128)(2,1)} %get-tuple-element.86.d_ref, bf16[16,544,256]{2,1,0:T(8,128)(2,1)} %get-tuple-element.77.yo.y_ref, bf16[16,544,128]{2,1,0:T(8,128)(2,1)} %get-tuple-element.78.key.key_ref.key_any, ...), custom_call_target="tpu_custom_call" | custom-call | tf_op jit(solution)/shard_map/branches_back/pallas_call | solution.py:995
  332.5 114.9 %bottleneck_back.1 = (f32[512,2048]{1,0:T(8,128)}, bf16[32,3584]{1,0:T(8,128)(2,1)}, bf16[512,256]{1,0:T(8,128)(2,1)}, bf16[9,64,512]{2,1,0:T(8,128)(2,1)}, bf16...) custom-call(bf16[512,2048]{1,0:T(8,128)(2,1)} %bitcast.80, ...), custom_call_target="tpu_custom_call" | custom-call | tf_op jit(solution)/shard_map/bottleneck_back/pallas_call | solution.py:1467
  447.5 6.9 %widen.1 = (f32[9,32,2048]{2,1,0:T(8,128)}, f32[9,32,2048]{2,1,0:T(8,128)}, f32[9,32,2048]{2,1,0:T(8,128)}, f32[32,2048]{1,0:T(8,128)}, f32[32,2048]{1,0:T(8,128...) custom-call(bf16[18,32,2048]{2,1,0:T(8,128)(2,1)} %get-tuple-element.106.gk, ...), custom_call_target="tpu_custom_call" | custom-call | tf_op jit(solution)/shard_map/widen/pallas_call | solution.py:1743
  454.3 0.6 fusion.4
  454.9 0.6 fusion.2
  455.5 0.6 fusion.3
  456.1 0.7 slice_convert_fusion
  456.9 0.7 copy.72
  457.5 4.7 %copy.74 = f32[8,64,2048]{2,1,0:T(8,128)} copy(f32[8,64,2048]{2,1,0:T(8,128)} %bitcast.83) | data formatting | bytes 8388608
  (31 shorter events, 0.2 us)
Async XLA Ops:
  5.5 125.7 %copy-start.2 = (s32[8,64]{1,0:T(8,128)S(1)}, s32[8,64]{1,0:T(8,128)}, u32[]{:S(2)}) copy-start(s32[8,64]{1,0:T(8,128)} %param.31) | copy-start | bytes 6148
  5.5 126.9 %copy-start.6 = (f32[256]{0:T(256)S(1)}, f32[256]{0:T(256)}, u32[]{:S(2)}) copy-start(f32[256]{0:T(256)} %param.51) | copy-start | bytes 3076
  5.5 126.9 %copy-start.7 = (f32[256]{0:T(256)S(1)}, f32[256]{0:T(256)}, u32[]{:S(2)}) copy-start(f32[256]{0:T(256)} %param.48) | copy-start | bytes 3076
  5.5 126.9 %copy-start.8 = (f32[256]{0:T(256)S(1)}, f32[256]{0:T(256)}, u32[]{:S(2)}) copy-start(f32[256]{0:T(256)} %param.45) | copy-start | bytes 3076
  5.5 126.9 %copy-start.9 = (f32[256]{0:T(256)S(1)}, f32[256]{0:T(256)}, u32[]{:S(2)}) copy-start(f32[256]{0:T(256)} %param.42) | copy-start | bytes 3076
  5.5 127.5 %copy-start.10 = (f32[256]{0:T(256)S(1)}, f32[256]{0:T(256)}, u32[]{:S(2)}) copy-start(f32[256]{0:T(256)} %param.52) | copy-start | bytes 3076
  5.5 127.5 %copy-start.11 = (f32[256]{0:T(256)S(1)}, f32[256]{0:T(256)}, u32[]{:S(2)}) copy-start(f32[256]{0:T(256)} %param.49) | copy-start | bytes 3076
  5.6 127.5 %copy-start.12 = (f32[256]{0:T(256)S(1)}, f32[256]{0:T(256)}, u32[]{:S(2)}) copy-start(f32[256]{0:T(256)} %param.46) | copy-start | bytes 3076
  5.6 127.5 %copy-start.13 = (f32[256]{0:T(256)S(1)}, f32[256]{0:T(256)}, u32[]{:S(2)}) copy-start(f32[256]{0:T(256)} %param.43) | copy-start | bytes 3076
  447.4 6.9 %copy-start.3 = (f32[2,512]{1,0:T(2,128)S(1)}, f32[2,512]{1,0:T(2,128)}, u32[]{:S(2)}) copy-start(f32[2,512]{1,0:T(2,128)} %get-tuple-element.115) | copy-start | bytes 12292
  447.4 6.9 %copy-start.4 = (f32[2,512]{1,0:T(2,128)S(1)}, f32[2,512]{1,0:T(2,128)}, u32[]{:S(2)}) copy-start(f32[2,512]{1,0:T(2,128)} %get-tuple-element.113) | copy-start | bytes 12292
  447.4 7.5 %copy-start = (f32[2,2048]{1,0:T(2,128)S(1)}, f32[2,2048]{1,0:T(2,128)}, u32[]{:S(2)}) copy-start(f32[2,2048]{1,0:T(2,128)} %get-tuple-element.117) | copy-start | bytes 49156
  447.4 8.1 %copy-start.1 = (f32[2,1024]{1,0:T(2,128)S(1)}, f32[2,1024]{1,0:T(2,128)}, u32[]{:S(2)}) copy-start(f32[2,1024]{1,0:T(2,128)} %get-tuple-element.119) | copy-start | bytes 24580
  447.4 8.1 %copy-start.5 = (f32[2,256]{1,0:T(2,128)S(1)}, f32[2,256]{1,0:T(2,128)}, u32[]{:S(2)}) copy-start(f32[2,256]{1,0:T(2,128)} %get-tuple-element.125) | copy-start | bytes 6148

commit v6 on v5

--- a/solution.py
+++ b/solution.py
@@ -376,6 +376,18 @@
         compiler_params=pltpu.CompilerParams(vmem_limit_bytes=VLIM),
         name="conv_weight",
     )(y, key, g)
+
+
+class Load:
+    def __init__(self, sems, **pairs):
+        self.cps = {}
+        for n, (name, (src, dst)) in enumerate(pairs.items()):
+            self.cps[name] = pltpu.make_async_copy(src, dst, sems.at[n])
+            self.cps[name].start()
+
+    def need(self, *names):
+        for name in names:
+            self.cps.pop(name).wait()
 
 
 class Gather:
@@ -797,10 +809,11 @@
 
 
 def branches_back_kernel(
-    steps, d_ref, y_ref, key_ref, k_ref, pooled_ref, dr_ref, size_ref, dy_o, gk_o, tail_o,
-    g, gt, gk, fin, in1, in2, dyo, acc, gp, *sems,
+    steps, d_ref, y_any, key_any, k_any, pooled_ref, dr_ref, size_ref, dy_o, gk_o, tail_o,
+    g, gt, gk, fin, in1, in2, dyo, acc, gp, y_ref, key_ref, k_ref, lsem, *sems,
 ):
     sems = list(sems)
+    load = Load(lsem, key=(key_any, key_ref), y=(y_any, y_ref), k=(k_any, k_ref))
     f, d = greet(range(1, 8), range(1, 4))
     Q, h, w = y_ref.shape[0], d_ref.shape[1], y_ref.shape[2]
     W = k_ref.shape[1]
@@ -866,6 +879,7 @@
         def _():
             to_outer(t).wait_recv()
 
+    load.need("key", "y", "k")
     tail_o[9] = tn_dot(dr_ref[...], pooled_ref[...]).astype(gk.dtype)
     gp[...] = nn_dot(dr_ref[...], k_ref[27]) / size_ref[:, :1]
     for b, s in enumerate(steps):
@@ -997,12 +1011,12 @@
         out_shape=[jax.ShapeDtypeStruct((Q, h, 8 * w), b16), jax.ShapeDtypeStruct((18, W // 8, 8 * w), b16),
             jax.ShapeDtypeStruct((10, W, w), b16),
         ],
-        in_specs=[VM] * 7,
+        in_specs=[VM] + [ANY] * 3 + [VM] * 3,
         out_specs=[ANY] * 2 + [VM],
         scratch_shapes=[
             V((Q, TT, W3), b16), V((W3, Q * T), b16), V((18, W, w), b16), V((18, W, w), b16),
             V((18, W, w), b16), V((18, W, w), b16), V((Q, T, w), b16),
-            V((Q * h, w), f32), V((8, w), f32),
+            V((Q * h, w), f32), V((8, w), f32), V(y.shape, b16), V(key.shape, b16), V(k.shape, b16), DMA((3,)),
         ]
         + gather_sems() * 3
         + [DMA((4, 8)), DMA((4, 8)), DMA((4,)), DMA((8,)), DMA((8,)), DMA(())]
@@ -1163,9 +1177,11 @@
 
 
 def bottleneck_back_kernel(
-    x_ref, ins_ref, st_ref, gr, gd, ge, dy, dpt, y_ref, pm_in, wp, n3, l3, we, n2, l2, h2, wd, ext, n1, l1, wr, key_any, tail,
+    x_any, ins_ref, st_ref, gr, gd, ge, dy_any, dpt, y_any, pm_in, wp_any, n3_any, l3_any, we_any, n2_any, l2_any, h2_any,
+    wd_any, ext_any, n1_any, l1_any, wr_any, key_any, tail_any,
     gf_o, pm_o, ex_o, di_o, re_o, s3_o, s2_o, s1_o, tk_o,
-    pm, ex, di, dp3, d3, acc, ext2, d1n, key, gf, pick, in1, in2, ksem, hs, hr, gs, s1, r1, s2, r2, s3, r3, ws, wrs, wl,
+    pm, ex, di, dp3, acc, ext2, d1n, key, gf, pick, in1, in2,
+    x_ref, dy, y_ref, wp, n3, l3, we, n2, l2, h2, wd, ext, n1, l1, wr, tail, lsem, ksem, hs, hr, gs, s1, r1, s2, r2, s3, r3, ws, wrs, wl,
     *sems,
 ):
     sems = list(sems)
@@ -1175,6 +1191,11 @@
         del sems[:n]
         return got
 
+    load = Load(
+        lsem, tail=(tail_any, tail), y=(y_any, y_ref), wp=(wp_any, wp), dy=(dy_any, dy), l3=(l3_any, l3), n3=(n3_any, n3),
+        we=(we_any, we), l2=(l2_any, l2), n2=(n2_any, n2), h2=(h2_any, h2), ext=(ext_any, ext), wd=(wd_any, wd),
+        l1=(l1_any, l1), n1=(n1_any, n1), x=(x_any, x_ref), wr=(wr_any, wr),
+    )
     f, d = greet(range(1, 8), range(1, 4))
     N, C = x_ref.shape
     Q, h = ext2.shape[0], ext2.shape[1] // 2
@@ -1205,6 +1226,7 @@
         for i in range(3)
     ]
     re_ = ex
+    d3 = dy
     r_re = reducer(re_, lambda g: (ds(g, nb),), half_rows(nb // 2), re_o)
     sum3, sum2, sum1 = (Sum(take(6), d, f) for _ in range(3))
 
@@ -1267,15 +1289,18 @@
                 c.start()
                 kout.append(c)
 
+    load.need("tail")
     hand(0)
     hand(1)
     kcp = pltpu.make_async_copy(key_any.at[:, pl.ds(pl.multiple_of(PAD - e + h * f, 16), 2 * h), :], key, ksem)
     kcp.start()
     count = st_ref[0:1, 0:1]
+    load.need("y")
     for c in range(0, C, 256):
         pm[:, c : c + 256] = tn_dot(dpt[...], y_ref[:, c : c + 256]).astype(jnp.bfloat16)
     pm[:, C:] = pm_in[...]
     r_pm.pair()
+    load.need("wp", "dy", "l3", "n3")
     ones, crossed = [], []
     ins = wide(ins_ref[...], 2)
     for c in range(0, C, 256):
@@ -1304,6 +1329,7 @@
         w = slice(c, c + 256)
         v = dp3[:, w].astype(jnp.float32) - tot[0:1, w] / count - n3[:, w].astype(jnp.float32) * (tot[1:2, w] / count)
         d3[:, w] = (ins * v * (ge[:, w] * st_ref[3:4, w])).astype(jnp.bfloat16)
+    load.need("we", "l2", "n2")
     ones, crossed = [], []
     for c in range(0, neck, 256):
         w = slice(c, c + 256)
@@ -1313,6 +1339,7 @@
         ones.append(jnp.sum(v, axis=0, keepdims=True))
         crossed.append(jnp.sum(v * n2[:, w].astype(jnp.float32), axis=0, keepdims=True))
     sum2.start([cat_rows(ones), cat_rows(crossed)])
+    load.need("h2")
     for c in range(0, C, 256):
         ex[:, c : c + 256] = tn_dot(h2[...], d3[:, c : c + 256]).astype(jnp.bfloat16)
     sum2.turn()
@@ -1329,6 +1356,7 @@
     second(1)
     hand(3)
     kcp.wait()
+    load.need("ext", "wd", "l1", "n1")
     r_pm.beside()
     r_ex.far()
     first(2)
@@ -1390,6 +1418,7 @@
         v = acc[:, w] - tot[0:1, w] / count - n1[:, w].astype(jnp.float32) * (tot[1:2, w] / count)
         v = (ins * v * (gr[:, w] * st_ref[1:2, w])).astype(jnp.bfloat16)
         d1n[:, w] = nn_dot(pick[...], v).astype(jnp.bfloat16)
+    load.need("x", "wr")
     for c in range(0, C, 256):
         re_[:, c : c + 256] = tn_dot(d1n[...], x_ref[:, c : c + 256]).astype(jnp.bfloat16)
     r_re.pair()
@@ -1455,9 +1484,13 @@
     S, V = jax.ShapeDtypeStruct, pltpu.VMEM
     blocks = [(W // 8, PM), (neck, C // 8), (9, neck // 8, neck), (neck // 8, C)]
     scratch = [
-        V((W, PM), b16), V((neck, C), b16), V((9, neck, neck), b16), V((N, C), b16), V((N, C), b16),
+        V((W, PM), b16), V((neck, C), b16), V((9, neck, neck), b16), V((N, C), b16),
         V((N, neck), f32), V((Q, 2 * h, neck), b16), V((N, neck), b16), V((Q, 2 * h, 128), b16), V((2, N, 256), f32),
         V((N, N), b16), V(tail.shape, b16), V(tail.shape, b16),
+    ]
+    scratch += [V(args[n].shape, args[n].dtype) for n in (0, 6, 8, 10, 11, 12, 13, 14, 15, 16, 17, 18, 19, 20, 21, 23)]
+    scratch += [
+        DMA((16,)),
         DMA(()), DMA((2,)), DMA((2,)), DMA((2,)),
     ]
     scratch += [DMA((5,))] * 6 + [DMA((2, 8)), DMA((2, 8)), DMA((2,))]
@@ -1468,7 +1501,7 @@
         bottleneck_back_kernel,
         out_shape=[S((N, C), f32)] + [S(b, b16) for b in blocks] + [S((2, C), f32), S((2, neck), f32), S((2, neck), f32)]
         + [S((10, W // 8, C), b16)],
-        in_specs=[VM] * 22 + [ANY, VM],
+        in_specs=[VM if n in (1, 2, 3, 4, 5, 7, 9) else ANY for n in range(24)],
         out_specs=[ANY] + [VM] * 7 + [ANY],
         scratch_shapes=scratch,
         compiler_params=pltpu.CompilerParams(collective_id=12, has_side_effects=True, vmem_limit_bytes=VLIM),
@@ -1498,12 +1531,13 @@
 
 
 def head_kernel(
-    steps, yo, key, kern, y, wp, wm, wc, ins_ref, kb, lab, st_ref, gb, bb, gm, bm,
+    steps, yo, key, kern, y_any, wp_any, wm_any, wc, ins_ref, kb, lab, st_ref, gb, bb, gm, bm,
     lo_o, dp_o, dr_o, pm_o, pooled_o, dpool_o, size_o, sb_o, sm_o,
-    acc, near, mine, far, corner, ab, nb, lb, joined, nm, lm, merged, pn, ps, pr, ss, rs,
+    acc, near, mine, far, corner, ab, nb, lb, joined, nm, lm, merged, pn, ps, pr, ss, rs, y, wp, wm, lsem,
     *sems,
 ):
     sems = list(sems)
+    load = Load(lsem, y=(y_any, y), wp=(wp_any, wp), wm=(wm_any, wm))
     f, d = greet(range(1, 8), range(1, 4))
     sum_b, sum_m, back_m, back_b = (Sum(sems[6 * n : 6 * n + 6], d, f) for n in range(4))
     Q, h = pn.shape[1], pn.shape[2]
@@ -1564,6 +1598,7 @@
             mine[k, two, :, lanes] = val.astype(b16)
         out.append(remote(mine.at[k], far.at[k - 1], ss.at[k + 1], rs.at[k + 1], d, f ^ (2 * k)))
     lax.fori_loop(3, 4, step, 0)
+    load.need("y", "wp", "wm")
     ab[:, :W] = nt_dot(y[...], wp[...])
     crop = (lax.broadcasted_iota(jnp.int32, (T, 128), 1) + 1).astype(f32)
 
@@ -1701,13 +1736,14 @@
             S((N, 128), b16), S((N, W), b16), S((Q, h, 3 * W), b16), S((W, width), b16), S((8, C // 8), b16),
             S((8, W), b16), S((8, 128), f32), S((2, 4 * W), f32), S((2, W), f32),
         ],
-        in_specs=[VM] * 15,
+        in_specs=[VM] * 3 + [ANY] * 3 + [VM] * 9,
         out_specs=[VM] * 9,
         scratch_shapes=[V((N, W), f32)]
         + [V((4, Q, h, 3 * W), b16)] * 2 + [V((2, Q, h, 3 * W), b16), V((Q, h, 3 * W), b16)]
         + [
             V((N, 4 * W), f32), V((N, 4 * W), b16), V((N, 4 * W), b16), V((N, J), b16), V((N, W), f32), V((N, W), f32),
             V((N, W), b16), V((4, Q, h, 3 * W), b16), DMA((4,)), DMA((4,)), DMA((4,)), DMA((4,)),
+            V(y.shape, b16), V(wp.shape, b16), V(wm.shape, b16), DMA((3,)),
         ]
         + sum_sems(3, 4 * W) + sum_sems(2, W) + sum_sems(2, W) + sum_sems(3, 4 * W),
         compiler_params=pltpu.CompilerParams(collective_id=5, has_side_effects=True, vmem_limit_bytes=VLIM),

time: 471 us -> 461 us (0.979)
  Pallas kernels: 443 us -> 433 us
    pallas_call x1, Pallas kernels: 115 us -> 109 us  [bottleneck_back(): pl.pallas_call(bottleneck_back_kernel, out_shape=[S((N, C), f32)] + [S(b,...]
where the time goes in v6:
time: 461 us; the launch traced here: 452 us
  Pallas kernels  433 us (94%)
  local copies, waits for them, and re-layouts  14.8 us (3%)
    pallas_call x1, Pallas kernels, bottleneck(): pl.pallas_call(bottleneck_kernel, out_shape=outs, in_specs=[VM] * 9 + [AN...  124 us
    pallas_call x1, Pallas kernels, branches_back(): pl.pallas_call(functools.partial(branches_back_kernel, steps), out_shape=...  114 us
    pallas_call x1, Pallas kernels, bottleneck_back(): pl.pallas_call(bottleneck_back_kernel, out_shape=[S((N, C), f32)] + [S(b,...  109 us
    pallas_call x1, Pallas kernels, head(): pl.pallas_call(functools.partial(head_kernel, steps), out_shape=[S((N, 12...  79.3 us

profile of v6, /device:TPU:0, one launch (start us, length us, event | category | flops | bytes accessed | tf_op | source)
XLA Modules:
  0.0 452.4 jit_solution(18315062588284931317)
XLA Ops:
  0.7 0.7 fusion
  1.4 0.1 copy.61
  1.6 0.6 pad.8.kb_ref
  2.2 0.7 compare_convert_fusion
  2.9 0.1 copy.64
  3.0 0.2 copy.65
  3.2 0.1 reshape.180
  3.3 0.8 broadcast_in_dim.53.ins_ref
  4.1 0.8 copy.66
  4.9 0.6 pad.9.wc_s
  5.6 124.4 %bottleneck.1 = (bf16[16,544,256]{2,1,0:T(8,128)(2,1)}, bf16[16,32,2048]{2,1,0:T(8,128)(2,1)}, bf16[512,2048]{1,0:T(8,128)(2,1)}, bf16[512,2048]{1,0:T(8,128)(2,...) custom-call(bf16[512,2048]{1,0:T(8,128)(2,1)} %bitcast.79, ...), custom_call_target="tpu_custom_call" | custom-call | tf_op jit(solution)/shard_map/bottleneck/pallas_call | solution.py:800
  130.0 0.1 copy.67
  130.1 0.2 copy.68
  130.3 0.1 convert_element_type.56
  130.4 0.8 broadcast_in_dim.61.kb
  131.2 0.1 copy.69
  131.3 0.2 copy.70
  131.5 0.1 convert_element_type.60
  131.6 0.8 broadcast_in_dim.62.lab
  132.4 0.6 pad_maximum_fusion
  133.1 0.6 pad_maximum_fusion.1
  133.7 79.3 %head.1 = (bf16[512,128]{1,0:T(8,128)(2,1)}, bf16[512,256]{1,0:T(8,128)(2,1)}, bf16[16,32,768]{2,1,0:T(8,128)(2,1)}, bf16[256,1536]{1,0:T(8,128)(2,1)}, bf16[8,2...) custom-call(bf16[16,544,256]{2,1,0:T(8,128)(2,1)} %get-tuple-element.77, ...), custom_call_target="tpu_custom_call" | custom-call | tf_op jit(solution)/shard_map/head/pallas_call | solution.py:1733
  213.0 1.7 copy.71
  214.6 113.6 %branches_back.1 = (bf16[16,32,2048]{2,1,0:T(8,128)(2,1)}, bf16[18,32,2048]{2,1,0:T(8,128)(2,1)}, bf16[10,256,256]{2,1,0:T(8,128)(2,1)}) custom-call(bf16[16,32,768]{2,1,0:T(8,128)(2,1)} %get-tuple-element.86.d_ref, bf16[16,544,256]{2,1,0:T(8,128)(2,1)} %get-tuple-element.77.yo.y_any, bf16[16,544,128]{2,1,0:T(8,128)(2,1)} %get-tuple-element.78.key.key_any, ...), custom_call_target="tpu_custom_call" | custom-call | tf_op jit(solution)/shard_map/branches_back/pallas_call | solution.py:1009
  328.3 108.9 %bottleneck_back.1 = (f32[512,2048]{1,0:T(8,128)}, bf16[32,3584]{1,0:T(8,128)(2,1)}, bf16[512,256]{1,0:T(8,128)(2,1)}, bf16[9,64,512]{2,1,0:T(8,128)(2,1)}, bf16...) custom-call(bf16[512,2048]{1,0:T(8,128)(2,1)} %bitcast.80, ...), custom_call_target="tpu_custom_call" | custom-call | tf_op jit(solution)/shard_map/bottleneck_back/pallas_call | solution.py:1500
  437.2 6.9 %widen.1 = (f32[9,32,2048]{2,1,0:T(8,128)}, f32[9,32,2048]{2,1,0:T(8,128)}, f32[9,32,2048]{2,1,0:T(8,128)}, f32[32,2048]{1,0:T(8,128)}, f32[32,2048]{1,0:T(8,128...) custom-call(bf16[18,32,2048]{2,1,0:T(8,128)(2,1)} %get-tuple-element.106.gk, ...), custom_call_target="tpu_custom_call" | custom-call | tf_op jit(solution)/shard_map/widen/pallas_call | solution.py:1779
  444.1 0.6 fusion.4
  444.7 0.6 fusion.2
  445.3 0.6 fusion.3
  445.9 0.7 slice_convert_fusion
  446.6 0.7 copy.72
  447.3 4.7 %copy.74 = f32[8,64,2048]{2,1,0:T(8,128)} copy(f32[8,64,2048]{2,1,0:T(8,128)} %bitcast.83) | data formatting | bytes 8388608
  (31 shorter events, 0.2 us)
Async XLA Ops:
  5.5 125.7 %copy-start.2 = (s32[8,64]{1,0:T(8,128)S(1)}, s32[8,64]{1,0:T(8,128)}, u32[]{:S(2)}) copy-start(s32[8,64]{1,0:T(8,128)} %param.31) | copy-start | bytes 6148
  5.5 126.9 %copy-start.6 = (f32[256]{0:T(256)S(1)}, f32[256]{0:T(256)}, u32[]{:S(2)}) copy-start(f32[256]{0:T(256)} %param.51) | copy-start | bytes 3076
  5.5 126.9 %copy-start.7 = (f32[256]{0:T(256)S(1)}, f32[256]{0:T(256)}, u32[]{:S(2)}) copy-start(f32[256]{0:T(256)} %param.48) | copy-start | bytes 3076
  5.5 126.9 %copy-start.8 = (f32[256]{0:T(256)S(1)}, f32[256]{0:T(256)}, u32[]{:S(2)}) copy-start(f32[256]{0:T(256)} %param.45) | copy-start | bytes 3076
  5.5 126.9 %copy-start.9 = (f32[256]{0:T(256)S(1)}, f32[256]{0:T(256)}, u32[]{:S(2)}) copy-start(f32[256]{0:T(256)} %param.42) | copy-start | bytes 3076
  5.5 127.5 %copy-start.10 = (f32[256]{0:T(256)S(1)}, f32[256]{0:T(256)}, u32[]{:S(2)}) copy-start(f32[256]{0:T(256)} %param.52) | copy-start | bytes 3076
  5.5 127.5 %copy-start.11 = (f32[256]{0:T(256)S(1)}, f32[256]{0:T(256)}, u32[]{:S(2)}) copy-start(f32[256]{0:T(256)} %param.49) | copy-start | bytes 3076
  5.6 127.5 %copy-start.12 = (f32[256]{0:T(256)S(1)}, f32[256]{0:T(256)}, u32[]{:S(2)}) copy-start(f32[256]{0:T(256)} %param.46) | copy-start | bytes 3076
  5.6 127.5 %copy-start.13 = (f32[256]{0:T(256)S(1)}, f32[256]{0:T(256)}, u32[]{:S(2)}) copy-start(f32[256]{0:T(256)} %param.43) | copy-start | bytes 3076
  437.2 6.9 %copy-start.3 = (f32[2,512]{1,0:T(2,128)S(1)}, f32[2,512]{1,0:T(2,128)}, u32[]{:S(2)}) copy-start(f32[2,512]{1,0:T(2,128)} %get-tuple-element.115) | copy-start | bytes 12292
  437.2 6.9 %copy-start.4 = (f32[2,512]{1,0:T(2,128)S(1)}, f32[2,512]{1,0:T(2,128)}, u32[]{:S(2)}) copy-start(f32[2,512]{1,0:T(2,128)} %get-tuple-element.113) | copy-start | bytes 12292
  437.2 7.5 %copy-start = (f32[2,2048]{1,0:T(2,128)S(1)}, f32[2,2048]{1,0:T(2,128)}, u32[]{:S(2)}) copy-start(f32[2,2048]{1,0:T(2,128)} %get-tuple-element.117) | copy-start | bytes 49156
  437.2 8.1 %copy-start.1 = (f32[2,1024]{1,0:T(2,128)S(1)}, f32[2,1024]{1,0:T(2,128)}, u32[]{:S(2)}) copy-start(f32[2,1024]{1,0:T(2,128)} %get-tuple-element.119) | copy-start | bytes 24580
  437.2 8.1 %copy-start.5 = (f32[2,256]{1,0:T(2,128)S(1)}, f32[2,256]{1,0:T(2,128)}, u32[]{:S(2)}) copy-start(f32[2,256]{1,0:T(2,128)} %get-tuple-element.125) | copy-start | bytes 6148

commit v7 on v6

--- a/solution.py
+++ b/solution.py
@@ -523,10 +523,10 @@
 
 
 def bottleneck_kernel(
-    x_ref, kb_ref, ins_ref, gr, br, gd, bd, ge, be,
+    x_any, kb_ref, ins_ref, gr, br, gd, bd, ge, be,
     wr_s, wd_s, we_s, wp_s, wm_s, wc_s, k_s0, k_s1, k_s2, kp_s,
     yo_o, y_o, n3_o, l3_o, n1_o, l1_o, n2_o, l2_o, ext_o, h2_o, key_o, k_o, wr_o, wd_o, we_o, wp_o, wm_o, wc_o, cnt_o,
-    xp, a1, a2, a3, ext, h2, y, n3, l3, n1, l1, n2, l2, key, wr, wd, we,
+    x_ref, lsem, xp, a1, a2, a3, ext, h2, y, n3, l3, n1, l1, n2, l2, key, wr, wd, we,
     *sems,
 ):
     sems = list(sems)
@@ -536,6 +536,7 @@
         del sems[:n]
         return got
 
+    load = Load(lsem, x=(x_any, x_ref))
     f, d = greet(range(1, 8), range(1, 4))
     N, C = x_ref.shape
     Q, h = ext.shape[0], ext.shape[1] // 2
@@ -579,6 +580,7 @@
     m, r, q = order % 4, (order // 4) % rows, order // h
     pick = (r * (N // rows) + q * 4 + m) == lax.broadcasted_iota(jnp.int32, (N, N), 1)
     pick = pick.astype(jnp.float32).astype(jnp.bfloat16)
+    load.need("x")
     for c in range(0, C, 256):
         xp[:, c : c + 256] = nn_dot(pick, x_ref[:, c : c + 256]).astype(jnp.bfloat16)
     key[:, :PAD, :] = jnp.zeros((Q, PAD, 128), jnp.bfloat16)
@@ -598,8 +600,6 @@
     inside = jnp.sum(ins_ref[...], axis=0, keepdims=True)
     sum1.start([cat_rows(sums), cat_rows(squares), cat_rows([inside] * (neck // 128))])
     g_we.start()
-    g_wd[1].forward()
-    g_wd[2].forward()
     kparts = (k_s0, k_s1, k_s2, kp_s)
 
     def kslot(b, g, lo, n):
@@ -637,6 +637,8 @@
         c.start()
         kcp.append(c)
     sum1.turn()
+    g_wd[1].forward()
+    g_wd[2].forward()
     out(0, 1)
     st = sum1.result()
     out(2, 3)
@@ -692,6 +694,8 @@
     aside(0, 1, 2, 3)
     sum2.turn()
     out(8, 9)
+    for g in (g_wp, g_wm, g_wc):
+        g.start()
     st = sum2.result()
     out(10)
     mean = st[0:1] / count
@@ -721,10 +725,8 @@
         squares.append(t)
     sum3.start([cat_rows(sums), cat_rows(squares)])
     aside(8, 9)
+    out(15, 16, 17)
     sum3.turn()
-    out(15, 16, 17)
-    for g in (g_wp, g_wm, g_wc):
-        g.start()
     st = sum3.result()
     total = count[:, :1]
     mean3 = st[0:1] / total
@@ -788,7 +790,7 @@
     ]
     V = pltpu.VMEM
     scratch = [
-        V((N, C), b16), V((N, neck), f32), V((N, neck), f32), V((N, C), f32), V((Q, 2 * h, neck), b16), V((N, neck), b16),
+        V((N, C), b16), DMA((1,)), V((N, C), b16), V((N, neck), f32), V((N, neck), f32), V((N, C), f32), V((Q, 2 * h, neck), b16), V((N, neck), b16),
         V((Q, h, C), b16), V((N, C), b16), V((N, C), b16),
         V((N, neck), b16), V((N, neck), b16), V((N, neck), b16), V((N, neck), b16), V((Q, TT, 128), b16),
         V((neck, C), b16), V((9, neck, neck), b16), V((neck, C), b16),
@@ -800,7 +802,7 @@
     return pl.pallas_call(
         bottleneck_kernel,
         out_shape=outs,
-        in_specs=[VM] * 9 + [ANY] * 10,
+        in_specs=[ANY] + [VM] * 8 + [ANY] * 10,
         out_specs=[ANY] * 18 + [VM],
         scratch_shapes=scratch,
         compiler_params=pltpu.CompilerParams(collective_id=1, has_side_effects=True, vmem_limit_bytes=VLIM),

time: 461 us -> 452 us (0.980)
  Pallas kernels: 433 us -> 424 us
    pallas_call x1, Pallas kernels: 124 us -> 118 us  [bottleneck(): pl.pallas_call(bottleneck_kernel, out_shape=outs, in_specs=[ANY] + [VM] *...]
where the time goes in v7:
time: 452 us; the launch traced here: 443 us
  Pallas kernels  424 us (94%)
  local copies, waits for them, and re-layouts  14.8 us (3%)
    pallas_call x1, Pallas kernels, bottleneck(): pl.pallas_call(bottleneck_kernel, out_shape=outs, in_specs=[ANY] + [VM] *...  118 us
    pallas_call x1, Pallas kernels, branches_back(): pl.pallas_call(functools.partial(branches_back_kernel, steps), out_shape=...  114 us
    pallas_call x1, Pallas kernels, bottleneck_back(): pl.pallas_call(bottleneck_back_kernel, out_shape=[S((N, C), f32)] + [S(b,...  107 us
    pallas_call x1, Pallas kernels, head(): pl.pallas_call(functools.partial(head_kernel, steps), out_shape=[S((N, 12...  77.8 us

profile of v7, /device:TPU:0, one launch (start us, length us, event | category | flops | bytes accessed | tf_op | source)
XLA Modules:
  0.0 443.1 jit_solution(16243309099327876325)
XLA Ops:
  0.7 0.7 fusion
  1.4 0.1 copy.61
  1.6 0.6 pad.8.kb_ref
  2.2 0.7 compare_convert_fusion
  2.9 0.1 copy.64
  3.0 0.2 copy.65
  3.2 0.1 reshape.180
  3.3 0.8 broadcast_in_dim.53.ins_ref
  4.1 0.8 copy.66
  4.9 0.6 pad.9.wc_s
  5.6 118.0 %bottleneck.1 = (bf16[16,544,256]{2,1,0:T(8,128)(2,1)}, bf16[16,32,2048]{2,1,0:T(8,128)(2,1)}, bf16[512,2048]{1,0:T(8,128)(2,1)}, bf16[512,2048]{1,0:T(8,128)(2,...) custom-call(bf16[512,2048]{1,0:T(8,128)(2,1)} %bitcast.79, ...), custom_call_target="tpu_custom_call" | custom-call | tf_op jit(solution)/shard_map/bottleneck/pallas_call | solution.py:802
  123.5 0.1 copy.67
  123.7 0.2 copy.68
  123.8 0.1 convert_element_type.56
  124.0 0.8 broadcast_in_dim.61.kb
  124.8 0.1 copy.69
  124.9 0.2 copy.70
  125.0 0.1 convert_element_type.60
  125.1 0.8 broadcast_in_dim.62.lab
  126.0 0.6 pad_maximum_fusion
  126.6 0.6 pad_maximum_fusion.1
  127.2 77.8 %head.1 = (bf16[512,128]{1,0:T(8,128)(2,1)}, bf16[512,256]{1,0:T(8,128)(2,1)}, bf16[16,32,768]{2,1,0:T(8,128)(2,1)}, bf16[256,1536]{1,0:T(8,128)(2,1)}, bf16[8,2...) custom-call(bf16[16,544,256]{2,1,0:T(8,128)(2,1)} %get-tuple-element.77, ...), custom_call_target="tpu_custom_call" | custom-call | tf_op jit(solution)/shard_map/head/pallas_call | solution.py:1735
  205.0 1.7 copy.71
  206.7 113.7 %branches_back.1 = (bf16[16,32,2048]{2,1,0:T(8,128)(2,1)}, bf16[18,32,2048]{2,1,0:T(8,128)(2,1)}, bf16[10,256,256]{2,1,0:T(8,128)(2,1)}) custom-call(bf16[16,32,768]{2,1,0:T(8,128)(2,1)} %get-tuple-element.86.d_ref, bf16[16,544,256]{2,1,0:T(8,128)(2,1)} %get-tuple-element.77.yo.y_any, bf16[16,544,128]{2,1,0:T(8,128)(2,1)} %get-tuple-element.78.key.key_any, ...), custom_call_target="tpu_custom_call" | custom-call | tf_op jit(solution)/shard_map/branches_back/pallas_call | solution.py:1011
  320.4 107.4 %bottleneck_back.1 = (f32[512,2048]{1,0:T(8,128)}, bf16[32,3584]{1,0:T(8,128)(2,1)}, bf16[512,256]{1,0:T(8,128)(2,1)}, bf16[9,64,512]{2,1,0:T(8,128)(2,1)}, bf16...) custom-call(bf16[512,2048]{1,0:T(8,128)(2,1)} %bitcast.80, ...), custom_call_target="tpu_custom_call" | custom-call | tf_op jit(solution)/shard_map/bottleneck_back/pallas_call | solution.py:1502
  427.9 6.9 %widen.1 = (f32[9,32,2048]{2,1,0:T(8,128)}, f32[9,32,2048]{2,1,0:T(8,128)}, f32[9,32,2048]{2,1,0:T(8,128)}, f32[32,2048]{1,0:T(8,128)}, f32[32,2048]{1,0:T(8,128...) custom-call(bf16[18,32,2048]{2,1,0:T(8,128)(2,1)} %get-tuple-element.106.gk, ...), custom_call_target="tpu_custom_call" | custom-call | tf_op jit(solution)/shard_map/widen/pallas_call | solution.py:1781
  434.7 0.6 fusion.4
  435.3 0.6 fusion.2
  436.0 0.6 fusion.3
  436.6 0.7 slice_convert_fusion
  437.3 0.7 copy.72
  438.0 4.7 %copy.74 = f32[8,64,2048]{2,1,0:T(8,128)} copy(f32[8,64,2048]{2,1,0:T(8,128)} %bitcast.83) | data formatting | bytes 8388608
  (31 shorter events, 0.2 us)
Async XLA Ops:
  5.5 119.2 %copy-start.2 = (s32[8,64]{1,0:T(8,128)S(1)}, s32[8,64]{1,0:T(8,128)}, u32[]{:S(2)}) copy-start(s32[8,64]{1,0:T(8,128)} %param.31) | copy-start | bytes 6148
  5.5 120.5 %copy-start.6 = (f32[256]{0:T(256)S(1)}, f32[256]{0:T(256)}, u32[]{:S(2)}) copy-start(f32[256]{0:T(256)} %param.51) | copy-start | bytes 3076
  5.5 120.5 %copy-start.7 = (f32[256]{0:T(256)S(1)}, f32[256]{0:T(256)}, u32[]{:S(2)}) copy-start(f32[256]{0:T(256)} %param.48) | copy-start | bytes 3076
  5.5 120.5 %copy-start.8 = (f32[256]{0:T(256)S(1)}, f32[256]{0:T(256)}, u32[]{:S(2)}) copy-start(f32[256]{0:T(256)} %param.45) | copy-start | bytes 3076
  5.5 120.5 %copy-start.9 = (f32[256]{0:T(256)S(1)}, f32[256]{0:T(256)}, u32[]{:S(2)}) copy-start(f32[256]{0:T(256)} %param.42) | copy-start | bytes 3076
  5.5 121.1 %copy-start.10 = (f32[256]{0:T(256)S(1)}, f32[256]{0:T(256)}, u32[]{:S(2)}) copy-start(f32[256]{0:T(256)} %param.52) | copy-start | bytes 3076
  5.5 121.0 %copy-start.11 = (f32[256]{0:T(256)S(1)}, f32[256]{0:T(256)}, u32[]{:S(2)}) copy-start(f32[256]{0:T(256)} %param.49) | copy-start | bytes 3076
  5.6 121.0 %copy-start.12 = (f32[256]{0:T(256)S(1)}, f32[256]{0:T(256)}, u32[]{:S(2)}) copy-start(f32[256]{0:T(256)} %param.46) | copy-start | bytes 3076
  5.6 121.0 %copy-start.13 = (f32[256]{0:T(256)S(1)}, f32[256]{0:T(256)}, u32[]{:S(2)}) copy-start(f32[256]{0:T(256)} %param.43) | copy-start | bytes 3076
  427.8 6.9 %copy-start.3 = (f32[2,512]{1,0:T(2,128)S(1)}, f32[2,512]{1,0:T(2,128)}, u32[]{:S(2)}) copy-start(f32[2,512]{1,0:T(2,128)} %get-tuple-element.115) | copy-start | bytes 12292
  427.8 6.9 %copy-start.4 = (f32[2,512]{1,0:T(2,128)S(1)}, f32[2,512]{1,0:T(2,128)}, u32[]{:S(2)}) copy-start(f32[2,512]{1,0:T(2,128)} %get-tuple-element.113) | copy-start | bytes 12292
  427.8 7.5 %copy-start = (f32[2,2048]{1,0:T(2,128)S(1)}, f32[2,2048]{1,0:T(2,128)}, u32[]{:S(2)}) copy-start(f32[2,2048]{1,0:T(2,128)} %get-tuple-element.117) | copy-start | bytes 49156
  427.9 8.1 %copy-start.1 = (f32[2,1024]{1,0:T(2,128)S(1)}, f32[2,1024]{1,0:T(2,128)}, u32[]{:S(2)}) copy-start(f32[2,1024]{1,0:T(2,128)} %get-tuple-element.119) | copy-start | bytes 24580
  427.9 8.1 %copy-start.5 = (f32[2,256]{1,0:T(2,128)S(1)}, f32[2,256]{1,0:T(2,128)}, u32[]{:S(2)}) copy-start(f32[2,256]{1,0:T(2,128)} %get-tuple-element.125) | copy-start | bytes 6148
